TPU v7x, 32 devices: a whole 2x2x4 slice. The times are simulated.
32 devices in a mesh: seq: 8 (over z, y), ch: 4 (over x, core).
Axes of the slice: x: 2, y: 2, z: 4, core: 2. Of those that a mesh axis runs over, the one named last changes fastest.
Arguments:
- inputs: float32 [8, 4096, 512], P('seq', None, 'ch'), may hold values from -6 to 6
- cotangent: float32 [8, 4096, 512], P('seq', 'ch'), may hold values from -6 to 6
- norm_gain: float32 [512], replicated, may hold values from 0.5 to 1.5
- delta: float32 [512, 16], replicated, may hold values from -4 to 4
- alpha: float32 [512, 16], replicated, may hold values from -4 to 4
- beta: float32 [512, 16], replicated, may hold values from -4 to 4
- eta: float32 [512, 16], replicated, may hold values from -4 to 4
- omega: float32 [512], replicated, may hold values from -1 to 1
- w_value: float32 [512, 1024], replicated, may hold values from -0.25 to 0.25
- w_base: float32 [512, 2176], replicated, may hold values from -0.25 to 0.25
- qk_scale: float32 [2, 128], replicated, may hold values from 1 to 3
- qk_shift: float32 [2, 128], replicated, may hold values from -0.5 to 0.5
- w_hidden: float32 [1024, 512], replicated, may hold values from -0.046875 to 0.046875
- ffn_gain: float32 [512], replicated, may hold values from 0.5 to 1.5
- w_up: float32 [512, 1024], replicated, may hold values from -0.25 to 0.25
- w_down: float32 [1024, 512], replicated, may hold values from -0.1875 to 0.1875
- lengths: int32 [8], P('seq'), may hold values from 2049 to 4095, as said below
- key_mask: int32 [8, 128], P('seq'), may hold values 0 or 1
Outputs:
- output: float32 [8, 4096, 512], P('seq', 'ch')
- input_grad: float32 [8, 4096, 512], P('seq', None, 'ch')
- norm_gain_grad: float32 [512], replicated
- delta_grad: float32 [512, 16], replicated
- alpha_grad: float32 [512, 16], replicated
- beta_grad: float32 [512, 16], replicated
- eta_grad: float32 [512, 16], replicated
- omega_grad: float32 [512], replicated
- w_value_grad: float32 [512, 1024], replicated
- w_base_grad: float32 [512, 2176], replicated
- qk_scale_grad: float32 [2, 128], replicated
- qk_shift_grad: float32 [2, 128], replicated
- w_hidden_grad: float32 [1024, 512], replicated
- ffn_gain_grad: float32 [512], replicated
- w_up_grad: float32 [512, 1024], replicated
- w_down_grad: float32 [1024, 512], replicated
Inputs may be any that keep to these rules, and one draw needn't show every extreme that they name: `lengths`: no length is a multiple of 128; of the one sequence in a row one is longer than 3072; the first sequence has length 4095.
All inputs are finite; a program needn't handle non-finite values. No bound on the sum of `key_mask` on one device may be relied on, other than what follows from the above.
Results may differ from a plain program's by a relative error of at most 0.0003.
Values sent between devices are 32-bit elements; how exact they have to be, the bound alone decides.
No kernel may reach another device: no remote copies, remote signals or barrier semaphores. Data moves between devices by JAX's collectives and lax.ppermute only.
A program may use at most 192 MiB of HBM per device.

v0:
```python
import math

import jax
import jax.numpy as jnp
from jax import lax
from jax.experimental import pallas as pl
from jax.experimental.pallas import tpu as pltpu
from jax.sharding import PartitionSpec as P

EPS = 1e-05
CENTER = math.sqrt(0.5)
SPREAD = math.sqrt(0.25 / math.pi)
F32 = jnp.float32
BF16 = jnp.bfloat16
NN = ((1,), (0,))
NT = ((1,), (1,))
TN = ((0,), (0,))
LANES = 128
SUBS = 8
TILE = 256
SMALL = 32
NORM_MIB = 24
FORWARD_MIB = 46
BACKWARD_MIB = 46
VMEM = pl.BlockSpec(memory_space=pltpu.VMEM)
SMEM = pl.BlockSpec(memory_space=pltpu.SMEM)
HBM = pl.BlockSpec(memory_space=pltpu.HBM)


def params(mib):
    return pltpu.CompilerParams(vmem_limit_bytes=mib << 20)


def ordered_call(kernel, tokens, *, in_specs, prefetch=0, grid=None, out_specs, scratch_shapes=(), **rest):
    count, extra = prefetch + len(in_specs), len(tokens)

    def body(*refs):
        kernel(*refs[:count], *refs[count + extra :])

    spec = pltpu.PrefetchScalarGridSpec(
        num_scalar_prefetch=prefetch,
        grid=grid or (1,),
        in_specs=list(in_specs) + [VMEM] * extra,
        out_specs=out_specs,
        scratch_shapes=scratch_shapes,
    )
    run = pl.pallas_call(body, grid_spec=spec, **rest)
    return lambda *args: run(*args, *tokens)


def shape_of(*shape, dtype=F32):
    return jax.ShapeDtypeStruct(shape, dtype)


def split(value):
    high = value.astype(BF16)
    return high, (value - high.astype(F32)).astype(BF16)


def dot(left, right, dims):
    return lax.dot_general(left, right, (dims, ((), ())), preferred_element_type=F32)


def mm3(left, right, dims):
    return (
        dot(left[0], right[0], dims)
        + dot(left[1], right[0], dims)
        + dot(left[0], right[1], dims)
    )


def mm3_short(left, right, dims):
    (left_axis,), (right_axis,) = dims
    return dot(
        jnp.concatenate([left[0], left[1], left[0]], left_axis),
        jnp.concatenate([right[0], right[0], right[1]], right_axis),
        dims,
    )


def sigmoid(value):
    return 0.5 * jnp.tanh(0.5 * value) + 0.5


def rows_sum(value):
    return jnp.sum(value, -1, keepdims=True)


def split_kernel(*refs):
    count = len(refs) // 3
    for index in range(count):
        high, low = split(refs[index][...])
        refs[count + 2 * index][...] = high
        refs[count + 2 * index + 1][...] = low


def split_weights(weights, steps=8):
    def spec(weight):
        return pl.BlockSpec((weight.shape[0] // steps, weight.shape[1]), lambda i: (i, 0))

    out = pl.pallas_call(
        split_kernel,
        grid=(steps,),
        in_specs=[spec(w) for w in weights],
        out_specs=[spec(w) for w in weights for _ in range(2)],
        out_shape=[jax.ShapeDtypeStruct(w.shape, BF16) for w in weights for _ in range(2)],
        compiler_params=params(SMALL),
        cost_estimate=pl.CostEstimate(
            flops=4 * sum(w.size for w in weights),
            bytes_accessed=8 * sum(w.size for w in weights),
            transcendentals=0,
        ),
        name="split_weights",
    )(*weights)
    return [(out[2 * i], out[2 * i + 1]) for i in range(len(weights))]


def turned(value):
    return jnp.transpose(value, (1, 0, 2))


def take_steps(ref, g, span, t):
    rows = jnp.stack([ref[g, pl.ds(c * span + t, SUBS), :] for c in range(SUBS)])
    rows = turned(rows)
    return [rows[i] for i in range(SUBS)]


def put_steps(ref, g, span, t, values):
    rows = turned(jnp.stack(values))
    for c in range(SUBS):
        ref[g, pl.ds(c * span + t, SUBS), :] = rows[c]


def rows_of(ref, g, these):
    return [jnp.broadcast_to(ref[g, n : n + 1, :], (SUBS, LANES)) for n in these]


def tree_sum(parts):
    while len(parts) > 1:
        parts = [sum(parts[i : i + 2]) for i in range(0, len(parts), 2)]
    return parts[0]


def scan_ends(source_ref, g, keep_ref, states, span, reverse):
    keeps = rows_of(keep_ref, g, range(states))

    def steps(i, state):
        t = pl.multiple_of((span // SUBS - 1 - i if reverse else i) * SUBS, SUBS)
        fresh = take_steps(source_ref, g, span, t)
        for value in reversed(fresh) if reverse else fresh:
            state = tuple(k * s + value for k, s in zip(keeps, state))
        return state

    zero = jnp.zeros((SUBS, LANES), F32)
    return lax.fori_loop(0, span // SUBS, steps, (zero,) * states, unroll=2)


def fold_ends(ends_ref, group, chunk_keep, states, order):
    total = jnp.zeros((states, LANES), F32)
    for chunk in order:
        total = chunk_keep * total + ends_ref[group, pl.ds(chunk, states, stride=SUBS), :]
    return total


def norm_kernel(x_ref, gain_ref, keep_ref, chunk_keep_ref, normed_ref, ends_ref, final_ref):
    groups, rows, _ = x_ref.shape
    states = keep_ref.shape[1]
    span = rows // SUBS
    width = groups * LANES

    def normalise(i, carry):
        here = pl.ds(pl.multiple_of(i * LANES, LANES), LANES)
        pieces = [x_ref[g, here, :] for g in range(groups)]
        mean = rows_sum(sum(pieces)) / width
        square = rows_sum(sum(p * p for p in pieces)) / width
        scale = lax.rsqrt(square - mean * mean + EPS)
        for g in range(groups):
            normed_ref[g, here, :] = (pieces[g] - mean) * scale * gain_ref[g]
        return carry

    lax.fori_loop(0, rows // LANES, normalise, 0)
    for g in range(groups):
        ends = scan_ends(normed_ref, g, keep_ref, states, span, False)
        for n in range(states):
            ends_ref[g, n * SUBS : (n + 1) * SUBS, :] = ends[n]
        final_ref[g] = fold_ends(ends_ref, g, chunk_keep_ref[g], states, range(SUBS))


def mix_kernel(
    place_ref,
    normed_ref,
    ends_ref,
    finals_ref,
    keep_ref,
    coef_ref,
    chunk_keep_ref,
    device_keep_ref,
    omega_ref,
    total_ref,
    start_ref,
):
    groups, rows, _ = normed_ref.shape
    states = keep_ref.shape[1]
    span = rows // SUBS
    ways = finals_ref.shape[0]
    place = place_ref[0]
    for g in range(groups):
        state = jnp.zeros((states, LANES), F32)
        for d in range(ways):
            state = jnp.where(d < place, device_keep_ref[g] * state + finals_ref[d, g], state)
        for chunk in range(SUBS):
            start_ref[g, pl.ds(chunk, states, stride=SUBS), :] = state
            state = chunk_keep_ref[g] * state + ends_ref[g, pl.ds(chunk, states, stride=SUBS), :]
        keeps = rows_of(keep_ref, g, range(states))
        coefs = rows_of(coef_ref, g, range(states))
        omega = jnp.broadcast_to(omega_ref[g], (SUBS, LANES))

        def steps(i, state):
            t = pl.multiple_of(i * SUBS, SUBS)
            totals = []
            for fresh in take_steps(normed_ref, g, span, t):
                state = tuple(k * s + fresh for k, s in zip(keeps, state))
                totals.append(tree_sum([c * s for c, s in zip(coefs, state)] + [omega * fresh]))
            put_steps(total_ref, g, span, t, totals)
            return state

        first = tuple(start_ref[g, n * SUBS : (n + 1) * SUBS, :] for n in range(states))
        lax.fori_loop(0, span // SUBS, steps, first, unroll=2)


def back_ends_kernel(grad_ref, keep_ref, chunk_keep_ref, ends_ref, final_ref):
    _, rows, _ = grad_ref.shape
    states = keep_ref.shape[1]
    span = rows // SUBS
    for g in range(1):
        ends = scan_ends(grad_ref, g, keep_ref, states, span, True)
        for n in range(states):
            ends_ref[g, n * SUBS : (n + 1) * SUBS, :] = ends[n]
        final_ref[g] = fold_ends(ends_ref, g, chunk_keep_ref[g], states, reversed(range(SUBS)))


def back_kernel(
    place_ref,
    grad_ref,
    ends_ref,
    finals_ref,
    start_ref,
    normed_ref,
    part_ref,
    keep_ref,
    coef_ref,
    chunk_keep_ref,
    device_keep_ref,
    sum_ref,
    coef_grad_ref,
    keep_grad_ref,
    init_ref,
):
    _, rows, _ = grad_ref.shape
    states = keep_ref.shape[1]
    span = rows // SUBS
    ways = finals_ref.shape[0]
    place = place_ref[0]
    half = states // 2
    zero = jnp.zeros((SUBS, LANES), F32)
    for g in range(1):
        whole_g = 0
        state = jnp.zeros((states, LANES), F32)
        for d in reversed(range(ways)):
            state = jnp.where(
                d > place, device_keep_ref[whole_g] * state + finals_ref[d, whole_g], state
            )
        for chunk in reversed(range(SUBS)):
            init_ref[pl.ds(chunk, states, stride=SUBS), :] = state
            state = (
                chunk_keep_ref[whole_g] * state
                + ends_ref[whole_g, pl.ds(chunk, states, stride=SUBS), :]
            )
        for part in range(2):
            these = range(part * half, (part + 1) * half)
            keeps = rows_of(keep_ref, whole_g, these)
            coefs = rows_of(coef_ref, whole_g, these)

            def steps(i, carry):
                lam, second, coef_acc, keep_acc = carry
                t = pl.multiple_of((span // SUBS - 1 - i) * SUBS, SUBS)
                fresh = take_steps(grad_ref, g, span, t)
                source = take_steps(normed_ref, g, span, t)
                outs = [None] * SUBS
                for j in reversed(range(SUBS)):
                    keep_acc = tuple(a + v * source[j] for a, v in zip(keep_acc, second))
                    lam = tuple(k * l + fresh[j] for k, l in zip(keeps, lam))
                    coef_acc = tuple(a + l * source[j] for a, l in zip(coef_acc, lam))
                    second = tuple(l + k * v for l, k, v in zip(lam, keeps, second))
                    outs[j] = tree_sum([c * l for c, l in zip(coefs, lam)])
                rows = turned(jnp.stack(outs))
                before = part_ref if part == 0 else sum_ref
                for c in range(SUBS):
                    here = pl.ds(c * span + t, SUBS)
                    sum_ref[g, here, :] = before[g, here, :] + rows[c]
                return lam, second, coef_acc, keep_acc

            first = tuple(init_ref[n * SUBS : (n + 1) * SUBS, :] for n in these)
            nothing = (zero,) * half
            lam, second, coef_acc, keep_acc = lax.fori_loop(
                0, span // SUBS, steps, (first, nothing, nothing, nothing)
            )
            for j, n in enumerate(these):
                start = start_ref[whole_g, n * SUBS : (n + 1) * SUBS, :]
                keep_acc_n = keep_acc[j] + start * second[j]
                coef_grad_ref[g, n : n + 1, :] = jnp.sum(coef_acc[j], 0, keepdims=True)
                keep_grad_ref[g, n : n + 1, :] = jnp.sum(keep_acc_n, 0, keepdims=True)


def unnorm_kernel(
    x_ref,
    sum_a,
    sum_b,
    direct_ref,
    gain_ref,
    coef_a,
    coef_b,
    keep_a,
    keep_b,
    omega_ref,
    ffn_ref,
    qk_ref,
    out_ref,
    small_ref,
    gain_grad,
):
    groups, rows, _ = x_ref.shape
    width = groups * LANES
    share = sum_a.shape[0]
    tile = pl.program_id(0)

    @pl.when(tile == 0)
    def _():
        gain_grad[...] = jnp.zeros_like(gain_grad)

    pieces = [x_ref[g] for g in range(groups)]
    mean = rows_sum(sum(pieces)) / width
    square = rows_sum(sum(p * p for p in pieces)) / width
    scale = lax.rsqrt(square - mean * mean + EPS)
    centered = [(p - mean) * scale for p in pieces]
    grads = [(sum_a, sum_b)[g // share][g % share] for g in range(groups)]
    for g in range(groups):
        gain_grad[g : g + 1, :] += jnp.sum(grads[g] * centered[g], 0, keepdims=True)
    scaled = [grads[g] * gain_ref[g] for g in range(groups)]
    plain = rows_sum(sum(scaled)) / width
    cross = rows_sum(sum(s * c for s, c in zip(scaled, centered))) / width
    for g in range(groups):
        out_ref[g] = direct_ref[g] + scale * (scaled[g] - plain - centered[g] * cross)

    @pl.when(tile == pl.num_programs(0) - 1)
    def _():
        states = coef_a.shape[1]
        for i, refs in enumerate(((coef_a, coef_b), (keep_a, keep_b))):
            for g in range(groups):
                at = slice(g * states, (g + 1) * states)
                small_ref[at, i * LANES : (i + 1) * LANES] = refs[g // share][g % share]
        at = groups * states
        small_ref[at:, :] = jnp.zeros((small_ref.shape[0] - at, 2 * LANES), F32)
        small_ref[at : at + groups, :LANES] = gain_grad[:groups]
        for g in range(groups):
            here = slice(at + groups + g, at + groups + g + 1)
            small_ref[here, :LANES] = omega_ref[g]
            small_ref[here, LANES:] = ffn_ref[:, g * LANES : (g + 1) * LANES]
        small_ref[at : at + 4, LANES:] = qk_ref[0:4, :]


def group_spec(array, lowest=0):
    axis = array.ndim - 3
    block = array.shape[:axis] + (1,) + array.shape[axis + 1 :]
    return pl.BlockSpec(block, lambda g: (0,) * axis + (lowest + g, 0, 0))


def scan_call(kernel, name, scalars, arrays, outs, tokens=(), lowest=0, count=None, scratch=(), work=4):
    count = count or arrays[0].shape[-3]
    states, rows = outs[-1].shape[-2], arrays[0].shape[-2]
    return ordered_call(
        kernel,
        tokens,
        grid=(count,),
        in_specs=[SMEM] * len(scalars) + [group_spec(v, lowest) for v in arrays],
        out_specs=[group_spec(v) for v in outs],
        scratch_shapes=scratch,
        out_shape=outs,
        compiler_params=params(SMALL),
        cost_estimate=pl.CostEstimate(
            flops=work * rows * count * LANES * 16,
            bytes_accessed=12 * rows * count * LANES,
            transcendentals=0,
        ),
        name=name,
    )(*scalars, *arrays)


def back_call(lowest, count, place_info, grad4, ends, finals, starts, normed4, part4, tables, tokens):
    rows, states = grad4.shape[1], starts.shape[1] // SUBS
    arrays = [grad4, ends, finals, starts, normed4, part4, *tables]
    outs = [shape_of(count, rows, LANES)] + [shape_of(count, states, LANES)] * 2
    return scan_call(
        back_kernel,
        "back",
        [place_info],
        arrays,
        outs,
        tokens,
        lowest,
        count,
        [pltpu.VMEM((states * SUBS, LANES), F32)],
        10,
    )


def unnorm_call(x4, sums, direct4, gain4, coefs, keeps, omega, ffn, qk, tokens):
    groups, rows, _ = x4.shape
    states = coefs[0].shape[1]
    by_group = pl.BlockSpec((groups, TILE, LANES), lambda i: (0, i, 0))
    halves = [pl.BlockSpec((s.shape[0], TILE, LANES), lambda i: (0, i, 0)) for s in sums]
    height = -(-(groups * states + 2 * groups) // 16) * 16
    return ordered_call(
        unnorm_kernel,
        tokens,
        grid=(rows // TILE,),
        in_specs=[by_group] + halves + [by_group] + [VMEM] * 8,
        out_specs=[by_group, pl.BlockSpec((height, 2 * LANES), lambda i: (0, 0))],
        out_shape=[shape_of(*x4.shape), shape_of(height, 2 * LANES)],
        scratch_shapes=[pltpu.VMEM((SUBS, LANES), F32)],
        compiler_params=params(SMALL),
        cost_estimate=pl.CostEstimate(
            flops=20 * x4.size, bytes_accessed=16 * x4.size, transcendentals=0
        ),
        name="unnorm",
    )(x4, *sums, direct4, gain4, *coefs, *keeps, omega, ffn, qk)


def small_kernel(
    part_a,
    part_b,
    part_c,
    part_d,
    gate_ref,
    decay_ref,
    beta_ref,
    eta_ref,
    gain_out,
    delta_out,
    alpha_out,
    beta_out,
    eta_out,
    omega_out,
    ffn_out,
    scale_out,
    shift_out,
):
    groups, states, _ = gate_ref.shape
    root = math.sqrt(states)
    at = groups * states
    height = -(-(groups * states + 2 * groups) // 16) * 16
    tails = [ref[ref.shape[0] - height :, :] for ref in (part_a, part_b, part_c, part_d)]
    total = (tails[0] + tails[1]) + (tails[2] + tails[3])
    for g in range(groups):
        here = slice(g * states, (g + 1) * states)
        coef, keep = total[here, :LANES], total[here, LANES:]
        gate, decay, beta, eta = gate_ref[g], decay_ref[g], beta_ref[g], eta_ref[g]
        keep = keep * gate * beta * (eta / root)
        gate_grad = coef * beta * (eta / root) - keep * decay
        lanes = slice(g * LANES, (g + 1) * LANES)
        delta_out[:, lanes] = gate_grad * gate * (1.0 - gate)
        alpha_out[:, lanes] = -keep * gate * decay * (1.0 - decay)
        beta_out[:, lanes] = coef * gate * (eta / root)
        eta_out[:, lanes] = coef * gate * beta / root
    gain_out[...] = total[at : at + groups, :LANES]
    omega_out[...] = total[at + groups : at + 2 * groups, :LANES]
    ffn_out[...] = total[at + groups : at + 2 * groups, LANES:]
    scale_out[...] = total[at : at + 2, LANES:]
    shift_out[...] = total[at + 2 : at + 4, LANES:]


def small_call(parts, tables):
    groups, states, _ = tables[0].shape
    row, table = shape_of(groups, LANES), shape_of(states, groups * LANES)
    two = shape_of(2, LANES)
    return pl.pallas_call(
        small_kernel,
        in_specs=[VMEM] * 8,
        out_specs=[VMEM] * 9,
        out_shape=[row, table, table, table, table, row, row, two, two],
        compiler_params=params(SMALL),
        name="small_grads",
    )(*parts, *tables)


QUARTER = 256
EVERY = slice(None)


def columns(total, step=512):
    return [slice(i, min(i + step, total)) for i in range(0, total, step)]


def joined(ref):
    return jnp.concatenate([ref[g] for g in range(ref.shape[0])], 1)


def silu_slope(act, gate):
    return gate + act * (1.0 - gate)


class Attention:
    def __init__(self, z, scale_ref, shift_ref, mask_ref, base_row, length):
        rows, span = z.shape[0], mask_ref.shape[1]
        blocks = rows // span
        self.query = split(z * scale_ref[0:1, :] + shift_ref[0:1, :])
        self.key = split(z * scale_ref[1:2, :] + shift_ref[1:2, :])
        lane = lax.broadcasted_iota(jnp.int32, (1, span), 1)
        valids, counts = [], []
        for b in range(blocks):
            position = base_row + b * span + lane
            last_block = (base_row + b * span) // span == (length - 1) // span
            kept = (position < length) & (jnp.logical_not(last_block) | (mask_ref[...] == 1))
            valid = jnp.where(kept, 1.0, 0.0)
            count = jnp.maximum(rows_sum(valid), 1.0)
            valids.append(valid)
            counts.append(jnp.broadcast_to(count, (1, span)))
        row = lax.broadcasted_iota(jnp.int32, (rows, rows), 0)
        column = lax.broadcasted_iota(jnp.int32, (rows, rows), 1)
        near = (row >= column) & (row // span == column // span)
        self.mask = jnp.where(near, jnp.concatenate(valids, 1), 0.0)
        self.count = jnp.concatenate(counts, 1)
        self.spot = mm3_short(self.query, self.key, NT) / self.count - CENTER

    def weight(self):
        curve = lax.erf(self.spot * (1.0 / (SPREAD * math.sqrt(2.0))))
        return split((0.5 + 0.5 * curve) * self.mask)

    def slope(self):
        return (
            jnp.exp(self.spot * self.spot * (-1.0 / (2.0 * SPREAD * SPREAD)))
            * (self.mask / self.count)
            * (1.0 / (SPREAD * math.sqrt(2.0 * math.pi)))
        )


def add_to(total_ref, quarter, at, pieces, first):
    for piece in pieces:
        here = slice(at, at + piece.shape[0])
        at += piece.shape[0]
        total_ref[quarter, here, :] = jnp.where(first, 0.0, total_ref[quarter, here, :]) + piece
    return at


def packed_rows(value):
    return [value[:, i : i + QUARTER] for i in range(0, value.shape[1], QUARTER)]


class HandOut:
    def __init__(self, own, total, send, keep, sems, last):
        self.own, self.total, self.send, self.keep = own, total, send, keep
        self.sems, self.last = sems, last

    def each(self, quarter, act):
        apart = quarter ^ self.own

        @pl.when(self.last & (apart >= 2))
        def _():
            act(
                pltpu.make_async_copy(
                    self.total.at[quarter], self.send.at[3 - apart], self.sems.at[quarter]
                )
            )

        @pl.when(self.last & (apart < 2))
        def _():
            act(
                pltpu.make_async_copy(
                    self.total.at[quarter], self.keep.at[1 - apart], self.sems.at[quarter]
                )
            )

    def start(self, quarter):
        self.each(quarter, lambda copy: copy.start())

    def wait(self):
        for quarter in range(4):
            self.each(quarter, lambda copy: copy.wait())


def forward_kernel(
    info_ref,
    place_ref,
    mask_ref,
    x_ref,
    normed_ref,
    total_ref,
    cot_ref,
    scale_ref,
    shift_ref,
    gain_ref,
    wv_h,
    wv_l,
    wb_h,
    wb_l,
    wh_h,
    wh_l,
    wu_h,
    wu_l,
    wd_h,
    wd_l,
    out_ref,
    direct_ref,
    vpre,
    rpre,
    zpre,
    grad_u_ref,
    grad_h_ref,
    gain_grad_ref,
    send_a,
    keep_a,
    send_b,
    keep_b,
    v_h,
    v_l,
    upd,
    hpre,
    gr_h,
    gr_l,
    a_h,
    a_l,
    usil,
    du_h,
    du_l,
    acc_a,
    acc_b,
    sems_a,
    sems_b,
):
    tile = pl.program_id(0)
    first = tile == 0
    groups, rows, _ = x_ref.shape
    width = groups * LANES
    zwidth = scale_ref.shape[1]
    values = wv_h.shape[1]
    units = wu_h.shape[1]
    base_row, length = info_ref[0] + tile * rows, info_ref[1]
    last = tile == pl.num_programs(0) - 1
    out_a = HandOut(place_ref[0], acc_a, send_a, keep_a, sems_a, last)
    out_b = HandOut(place_ref[1], acc_b, send_b, keep_b, sems_b, last)

    @pl.when(first)
    def _():
        gain_grad_ref[...] = jnp.zeros_like(gain_grad_ref)

    def put(high_ref, low_ref, where, value):
        high, low = split(value)
        high_ref[where] = high
        low_ref[where] = low
        return high, low

    n_pair = split(joined(normed_ref))
    total = joined(total_ref)
    m_pair = split(total * sigmoid(total))
    for c in columns(values):
        pre = mm3(n_pair, (wv_h[:, c], wv_l[:, c]), NN)
        vpre[:, c] = pre
        put(v_h, v_l, (EVERY, c), pre * sigmoid(pre))
    c = slice(width, width + zwidth)
    pre = mm3(m_pair, (wb_h[:, c], wb_l[:, c]), NN)
    zpre[...] = pre
    attention = Attention(
        pre * sigmoid(pre), scale_ref, shift_ref, mask_ref, base_row, length
    )
    c = slice(0, width)
    upd[...] = sigmoid(mm3(m_pair, (wb_h[:, c], wb_l[:, c]), NN))
    for c in columns(values):
        w = slice(width + zwidth + c.start, width + zwidth + c.stop)
        rpre[:, c] = mm3(m_pair, (wb_h[:, w], wb_l[:, w]), NN)
    w = slice(width + zwidth + values, width + zwidth + values + width)
    hpre[...] = mm3(m_pair, (wb_h[:, w], wb_l[:, w]), NN)
    weight = attention.weight()
    for c in columns(values):
        got = mm3(weight, (v_h[:, c], v_l[:, c]), NN)
        pre = rpre[:, c]
        put(gr_h, gr_l, (EVERY, c), got * (pre * sigmoid(pre)))
    pre = hpre[...] + mm3((gr_h[...], gr_l[...]), (wh_h[...], wh_l[...]), NN)
    s = sigmoid(pre)
    hidden = pre * s
    hpre[...] = silu_slope(hidden, s)
    x = joined(x_ref)
    update = upd[...]
    apart = hidden - x
    gated = x + update * apart
    mean = rows_sum(gated) / width
    square = rows_sum(gated * gated) / width
    scale = lax.rsqrt(square - mean * mean + EPS)
    centered = (gated - mean) * scale
    f_pair = split(centered * gain_ref[...])
    for c in columns(units):
        pre = mm3(f_pair, (wu_h[:, c], wu_l[:, c]), NN)
        s = sigmoid(pre)
        act = pre * s
        put(a_h, a_l, (EVERY, c), act)
        usil[:, c] = silu_slope(act, s)
    live = (base_row + lax.broadcasted_iota(jnp.int32, (rows, 1), 0) < length).astype(F32)
    out_ref[...] = (gated + mm3((a_h[...], a_l[...]), (wd_h[...], wd_l[...]), NN)) * live

    grad_out = cot_ref[...] * live
    do_pair = split(grad_out)
    for c in columns(units):
        put(du_h, du_l, (EVERY, c), mm3(do_pair, (wd_h[c, :], wd_l[c, :]), NT) * usil[:, c])
    grad_f = mm3((du_h[...], du_l[...]), (wu_h[...], wu_l[...]), NT)
    gain_grad_ref[...] += jnp.sum(grad_f * centered, 0, keepdims=True)
    scaled = grad_f * gain_ref[...]
    grad_gated = grad_out + scale * (
        scaled - rows_sum(scaled) / width - centered * (rows_sum(scaled * centered) / width)
    )
    grad_u_ref[...] = grad_gated * apart * update * (1.0 - update)
    grad_h = grad_gated * update * hpre[...]
    grad_h_ref[...] = grad_h
    h_pair = split(grad_h)
    direct = grad_gated * (1.0 - update)
    for g in range(groups):
        direct_ref[g] = direct[:, g * LANES : (g + 1) * LANES]
    for q in range(4):
        c = slice(q * QUARTER, (q + 1) * QUARTER)
        at_a = add_to(acc_a, q, 0, [mm3(f_pair, (du_h[:, c], du_l[:, c]), TN)], first)
        at_b = add_to(acc_b, q, 0, packed_rows(mm3((a_h[:, c], a_l[:, c]), do_pair, TN)), first)
        packed = packed_rows(mm3((gr_h[:, c], gr_l[:, c]), h_pair, TN))
        add_to(acc_a, q, at_a, packed[: len(packed) // 2], first)
        add_to(acc_b, q, at_b, packed[len(packed) // 2 :], first)
        out_a.start(q)
        out_b.start(q)
    out_a.wait()
    out_b.wait()


def backward_kernel(
    info_ref,
    place_ref,
    mask_ref,
    normed_ref,
    total_ref,
    vpre,
    rpre,
    zpre,
    grad_u_ref,
    grad_h_ref,
    scale_ref,
    shift_ref,
    omega_ref,
    wv_h,
    wv_l,
    wb_h,
    wb_l,
    wh_h,
    wh_l,
    grad_ref,
    part_ref,
    qk_grad_ref,
    omega_grad_ref,
    send_b,
    keep_b,
    send_c,
    keep_c,
    v_h,
    v_l,
    vsil,
    rst,
    att,
    da_h,
    da_l,
    dv_h,
    dv_l,
    bz_h,
    bz_l,
    br_h,
    br_l,
    acc_b,
    acc_c,
    sems_b,
    sems_c,
):
    tile = pl.program_id(0)
    first = tile == 0
    groups, rows, _ = normed_ref.shape
    width = groups * LANES
    zwidth = scale_ref.shape[1]
    values = wv_h.shape[1]
    base_row, length = info_ref[0] + tile * rows, info_ref[1]
    last = tile == pl.num_programs(0) - 1
    out_b = HandOut(place_ref[0], acc_b, send_b, keep_b, sems_b, last)
    out_c = HandOut(place_ref[1], acc_c, send_c, keep_c, sems_c, last)

    @pl.when(first)
    def _():
        qk_grad_ref[...] = jnp.zeros_like(qk_grad_ref)
        omega_grad_ref[...] = jnp.zeros_like(omega_grad_ref)

    def put(high_ref, low_ref, where, value):
        high, low = split(value)
        high_ref[where] = high
        low_ref[where] = low
        return high, low

    for c in columns(values):
        pre = vpre[:, c]
        s = sigmoid(pre)
        act = pre * s
        put(v_h, v_l, (EVERY, c), act)
        vsil[:, c] = silu_slope(act, s)
    pre = zpre[...]
    s = sigmoid(pre)
    z = pre * s
    zsil = silu_slope(z, s)
    attention = Attention(z, scale_ref, shift_ref, mask_ref, base_row, length)
    weight = attention.weight()
    for c in columns(values):
        got = mm3(weight, (v_h[:, c], v_l[:, c]), NN)
        pre = rpre[:, c]
        s = sigmoid(pre)
        act = pre * s
        rst[:, c] = act
        att[:, c] = got * silu_slope(act, s)
    u_pair = split(grad_u_ref[...])
    h_pair = split(grad_h_ref[...])
    for c in columns(values):
        got = mm3(h_pair, (wh_h[c, :], wh_l[c, :]), NT)
        put(da_h, da_l, (EVERY, c), got * rst[:, c])
        put(br_h, br_l, (EVERY, c), got * att[:, c])
    grad_scores = split(
        mm3((da_h[...], da_l[...]), (v_h[...], v_l[...]), NT) * attention.slope()
    )
    for c in columns(values):
        got = mm3(weight, (da_h[:, c], da_l[:, c]), TN)
        put(dv_h, dv_l, (EVERY, c), got * vsil[:, c])
    grad_q = mm3(grad_scores, attention.key, NN)
    grad_k = mm3(grad_scores, attention.query, TN)
    qk_grad_ref[0:1, :] += jnp.sum(grad_q * z, 0, keepdims=True)
    qk_grad_ref[1:2, :] += jnp.sum(grad_k * z, 0, keepdims=True)
    qk_grad_ref[2:3, :] += jnp.sum(grad_q, 0, keepdims=True)
    qk_grad_ref[3:4, :] += jnp.sum(grad_k, 0, keepdims=True)
    put(
        bz_h,
        bz_l,
        (EVERY, EVERY),
        (grad_q * scale_ref[0:1, :] + grad_k * scale_ref[1:2, :]) * zsil,
    )

    n_pair = split(joined(normed_ref))
    total = joined(total_ref)
    gate = sigmoid(total)
    mixed = total * gate
    m_pair = split(mixed)
    for q in range(4):
        c = slice(q * QUARTER, (q + 1) * QUARTER)
        at_b = add_to(acc_b, q, 0, [mm3(n_pair, (dv_h[:, c], dv_l[:, c]), TN)], first)
        w = slice(q * width // 4, (q + 1) * width // 4)
        got = mm3((m_pair[0][:, w], m_pair[1][:, w]), (bz_h[...], bz_l[...]), TN)
        half = got.shape[0] // 2
        at_b = add_to(acc_b, q, at_b, [jnp.concatenate([got[:half], got[half:]], 1)], first)
        at_c = add_to(acc_c, q, 0, [mm3(m_pair, (br_h[:, c], br_l[:, c]), TN)], first)
        side_pair = u_pair if q < 2 else h_pair
        c = slice(q % 2 * QUARTER, (q % 2 + 1) * QUARTER)
        got = mm3(m_pair, (side_pair[0][:, c], side_pair[1][:, c]), TN)
        half = got.shape[0] // 2
        add_to(acc_b, q, at_b, [got[:half]], first)
        add_to(acc_c, q, at_c, [got[half:]], first)
        out_b.start(q)
        out_c.start(q)

    grad_n = mm3((dv_h[...], dv_l[...]), (wv_h[...], wv_l[...]), NT)
    at = [0, width, width + zwidth, width + zwidth + values, 2 * width + zwidth + values]
    w = [slice(i, j) for i, j in zip(at[:-1], at[1:])]
    grad = (
        mm3(u_pair, (wb_h[:, w[0]], wb_l[:, w[0]]), NT)
        + mm3_short((bz_h[...], bz_l[...]), (wb_h[:, w[1]], wb_l[:, w[1]]), NT)
        + mm3((br_h[...], br_l[...]), (wb_h[:, w[2]], wb_l[:, w[2]]), NT)
        + mm3(h_pair, (wb_h[:, w[3]], wb_l[:, w[3]]), NT)
    ) * silu_slope(mixed, gate)
    for g in range(groups):
        lanes = slice(g * LANES, (g + 1) * LANES)
        got = grad[:, lanes]
        grad_ref[g] = got
        part_ref[g] = grad_n[:, lanes] + got * omega_ref[g]
        omega_grad_ref[g] += jnp.sum(got * normed_ref[g], 0, keepdims=True)

    out_b.wait()
    out_c.wait()


def by_row(count):
    return pl.BlockSpec((TILE, count), lambda i: (i, 0))


def forward_call(info, place, key_mask, x4, normed4, total4, cot, qk_scale, qk_shift, ffn_gain, pairs, heights):
    groups, rows, _ = x4.shape
    width = groups * LANES
    wv, wb, wh, wu, wd = pairs
    values, units, zwidth = wv[0].shape[1], wu[0].shape[1], qk_scale.shape[1]
    flat = [part for pair in pairs for part in pair]
    by_group = pl.BlockSpec((groups, TILE, LANES), lambda i: (0, i, 0))
    macs = rows * (wv[0].size + wb[0].size + wh[0].size + 3 * wu[0].size + 3 * wd[0].size)
    return pl.pallas_call(
        forward_kernel,
        grid=(rows // TILE,),
        in_specs=[SMEM, SMEM, VMEM, by_group, by_group, by_group, by_row(width)]
        + [VMEM] * (3 + len(flat)),
        out_specs=[
            by_row(width),
            by_group,
            by_row(values),
            by_row(values),
            by_row(zwidth),
            by_row(width),
            by_row(width),
            pl.BlockSpec((1, width), lambda i: (0, 0)),
            HBM,
            HBM,
            HBM,
            HBM,
        ],
        out_shape=[
            shape_of(rows, width),
            shape_of(groups, rows, LANES),
            shape_of(rows, values),
            shape_of(rows, values),
            shape_of(rows, zwidth),
            shape_of(rows, width),
            shape_of(rows, width),
            shape_of(1, width),
        ]
        + [shape_of(2, height, QUARTER) for height in heights for _ in range(2)],
        scratch_shapes=[
            pltpu.VMEM((TILE, values), BF16),
            pltpu.VMEM((TILE, values), BF16),
            pltpu.VMEM((TILE, width), F32),
            pltpu.VMEM((TILE, width), F32),
            pltpu.VMEM((TILE, values), BF16),
            pltpu.VMEM((TILE, values), BF16),
            pltpu.VMEM((TILE, units), BF16),
            pltpu.VMEM((TILE, units), BF16),
            pltpu.VMEM((TILE, units), F32),
            pltpu.VMEM((TILE, units), BF16),
            pltpu.VMEM((TILE, units), BF16),
        ]
        + [pltpu.VMEM((4, height, QUARTER), F32) for height in heights]
        + [pltpu.SemaphoreType.DMA((4,))] * 2,
        compiler_params=params(FORWARD_MIB),
        cost_estimate=pl.CostEstimate(flops=6 * macs, bytes_accessed=48 << 20, transcendentals=0),
        name="forward",
    )(info, place, key_mask, x4, normed4, total4, cot, qk_scale, qk_shift, ffn_gain, *flat)


def backward_call(
    info, place, key_mask, normed4, total4, saved, qk_scale, qk_shift, omega4, pairs, heights, tokens
):
    groups, rows, _ = normed4.shape
    width = groups * LANES
    wv, wb, wh = pairs[:3]
    values, zwidth = wv[0].shape[1], qk_scale.shape[1]
    flat = [part for pair in pairs[:3] for part in pair]
    by_group = pl.BlockSpec((groups, TILE, LANES), lambda i: (0, i, 0))
    macs = 2 * rows * (wv[0].size + wb[0].size + wh[0].size)
    quarters = [shape_of(2, height, QUARTER) for height in heights for _ in range(2)]
    return ordered_call(
        backward_kernel,
        tokens,
        grid=(rows // TILE,),
        in_specs=[SMEM, SMEM, VMEM, by_group, by_group]
        + [by_row(s.shape[1]) for s in saved]
        + [VMEM] * (3 + len(flat)),
        out_specs=[
            by_group,
            by_group,
            pl.BlockSpec((8, zwidth), lambda i: (0, 0)),
            pl.BlockSpec((groups, 1, LANES), lambda i: (0, 0, 0)),
        ]
        + [HBM] * 4,
        out_shape=[
            shape_of(groups, rows, LANES),
            shape_of(groups, rows, LANES),
            shape_of(8, zwidth),
            shape_of(groups, 1, LANES),
        ]
        + quarters,
        scratch_shapes=[
            pltpu.VMEM((TILE, values), BF16),
            pltpu.VMEM((TILE, values), BF16),
            pltpu.VMEM((TILE, values), F32),
            pltpu.VMEM((TILE, values), F32),
            pltpu.VMEM((TILE, values), F32),
            pltpu.VMEM((TILE, values), BF16),
            pltpu.VMEM((TILE, values), BF16),
            pltpu.VMEM((TILE, values), BF16),
            pltpu.VMEM((TILE, values), BF16),
            pltpu.VMEM((TILE, zwidth), BF16),
            pltpu.VMEM((TILE, zwidth), BF16),
            pltpu.VMEM((TILE, values), BF16),
            pltpu.VMEM((TILE, values), BF16),
        ]
        + [pltpu.VMEM((4, height, QUARTER), F32) for height in heights]
        + [pltpu.SemaphoreType.DMA((4,))] * 2,
        compiler_params=params(BACKWARD_MIB),
        cost_estimate=pl.CostEstimate(flops=6 * macs, bytes_accessed=40 << 20, transcendentals=0),
        name="backward",
    )(info, place, key_mask, normed4, total4, *saved, qk_scale, qk_shift, omega4, *flat)


def swap(value, step):
    axis, distance = step
    size = lax.axis_size(axis)
    return lax.ppermute(value, axis, [(i, i ^ distance) for i in range(size)])


def side(step):
    axis, distance = step
    return (lax.axis_index(axis) // distance) % 2


def device_steps():
    def bits(axis):
        size = lax.axis_size(axis)
        return [(axis, 1 << i) for i in range(size.bit_length() - 1)]

    return bits("ch"), bits("seq")


def orders():
    ch, seq = device_steps()
    x, y, z, rest = ch[1:], seq[:1], seq[1:2], seq[2:]
    out = [y + z + x, z + y + x, x + z + y, y + x + z]
    back = [y + x + z, x + z + y, y + z + x, z + x + y]
    return [(ch[:1] + go + rest, rest[::-1] + come + ch[:1]) for go, come in zip(out, back)]


TOKEN = shape_of(SUBS, LANES)


def gate(value, token):
    return lax.optimization_barrier((value, token))


def halve_kernel(own_ref, keep_ref, got_ref, send_ref, next_ref, token_ref):
    own = own_ref[0]
    send_ref[...] = keep_ref[1 - own] + got_ref[1 - own]
    next_ref[...] = keep_ref[own] + got_ref[own]
    token_ref[...] = jnp.zeros_like(token_ref)


def halve(keep, got, own, tokens):
    rows, width = keep.shape[-2] * (keep.shape[0] if keep.ndim == 3 else 1) // 2, keep.shape[-1]
    keep, got = keep.reshape(2, rows, width), got.reshape(2, rows, width)
    return ordered_call(
        halve_kernel,
        tokens,
        in_specs=[SMEM, VMEM, VMEM],
        out_specs=[VMEM] * 3,
        out_shape=[shape_of(rows, width)] * 2 + [TOKEN],
        compiler_params=params(SMALL),
        cost_estimate=pl.CostEstimate(
            flops=2 * rows * width, bytes_accessed=1 << 10, transcendentals=0
        ),
        name="halve",
    )(own.reshape(1), keep, got)


def add_kernel(left_ref, right_ref, out_ref, token_ref):
    out_ref[...] = left_ref[...] + right_ref[...]
    token_ref[...] = jnp.zeros_like(token_ref)


def add(left, right, tokens):
    return ordered_call(
        add_kernel,
        tokens,
        in_specs=[VMEM] * 2,
        out_specs=[VMEM] * 2,
        out_shape=[shape_of(*left.shape), TOKEN],
        compiler_params=params(SMALL),
        cost_estimate=pl.CostEstimate(flops=left.size, bytes_accessed=1 << 10, transcendentals=0),
        name="add",
    )(left, right)


def gather_kernel(counts, riders, *refs):
    parts, refs = refs[: len(counts)], refs[len(counts) :]
    out_ref, token_ref = refs[-2:]
    at = 0
    for part, rows in zip(parts, counts):
        out_ref[at : at + rows, :] = part[:rows, :]
        at += rows
    if riders:
        tails = [ref[ref.shape[0] - riders :, :] for ref in refs[:-2]]
        out_ref[at:, :] = sum(tails)
    token_ref[...] = jnp.zeros_like(token_ref)


def gather_parts(parts, counts, riders, rider_rows, tokens):
    total, width = sum(counts), parts[0].shape[1]
    shape = shape_of(total + (rider_rows if riders else 0), width)
    return ordered_call(
        lambda *refs: gather_kernel(counts, rider_rows if riders else 0, *refs),
        tokens,
        in_specs=[VMEM] * (len(parts) + len(riders)),
        out_specs=[VMEM] * 2,
        out_shape=[shape, TOKEN],
        compiler_params=params(SMALL),
        cost_estimate=pl.CostEstimate(flops=0, bytes_accessed=1 << 10, transcendentals=0),
        name="gather_parts",
    )(*parts, *riders)


def finish_kernel(plans, maps, outs_count, *refs):
    pieces = len(plans)
    places, refs = refs[:pieces], refs[pieces:]
    quarters, refs = refs[: 4 * pieces], refs[4 * pieces :]
    outs, refs = refs[:outs_count], refs[outs_count:]
    scratch, sems = refs[:pieces], refs[pieces:]
    leave = []
    for p, plan in enumerate(plans):
        place_ref, out_sems = places[p], sems[p]
        bits = place_ref.shape[0] - 1
        blocks = 1 << bits
        rows = scratch[p].shape[1] // blocks
        relative = place_ref[1]
        for bit in range(1, bits):
            relative = relative * 2 + place_ref[1 + bit]
        for i in range(4):
            for r in range(blocks):
                quarter, k = maps[p](i, r)
                target = pl.ds(pl.multiple_of((relative ^ k) * rows, SUBS), rows)
                scratch[p][quarter, target, :] = quarters[4 * p + i][r * rows : (r + 1) * rows, :]
        for i in range(4):
            quarter = place_ref[0] ^ i
            number = 0
            for out, moves in plan:
                for row, count, column, width, out_row, out_column in moves(quarter):
                    copy = pltpu.make_async_copy(
                        scratch[p].at[i, pl.ds(row, count), pl.ds(column, width)],
                        outs[out].at[pl.ds(out_row, count), pl.ds(out_column, width)],
                        out_sems.at[i, number],
                    )
                    copy.start()
                    leave.append(copy)
                    number += 1
    for copy in leave:
        copy.wait()


def aligned(value, step):
    return pl.multiple_of(value, step)


def as_columns(first, rows, out_row, out_column):
    return lambda q: [(first, rows, 0, QUARTER, out_row, aligned(out_column(q), LANES))]


def as_rows(first, rows, start, stop):
    def moves(q):
        return [
            (first + (c - start) // QUARTER * rows, rows, 0, QUARTER, aligned(q * rows, SUBS), c)
            for c in range(start, stop, QUARTER)
        ]

    return moves


def as_halves(first, rows, out_column):
    def moves(q):
        at = q * (2 * rows)
        return [
            (first, rows, 0, LANES, aligned(at, SUBS), out_column),
            (first, rows, LANES, LANES, aligned(at + rows, SUBS), out_column),
        ]

    return moves


def finish(pieces, plans, shapes, name, tokens=()):
    args = [v for piece in pieces for v in piece.pair + list(piece.got)]
    places = [piece.place for piece in pieces]
    scratch = [pltpu.VMEM((4,) + piece.quarter_shape(), F32) for piece in pieces]
    sems = []
    for piece, plan in zip(pieces, plans):
        number = sum(len(moves(0)) for _, moves in plan)
        sems.append(pltpu.SemaphoreType.DMA((4, number)))
    return ordered_call(
        lambda *refs: finish_kernel(plans, [p.quarter_and_block for p in pieces], len(shapes), *refs),
        tokens,
        in_specs=[SMEM] * len(places) + [VMEM] * len(args),
        out_specs=[HBM] * len(shapes),
        out_shape=[shape_of(*shape) for shape in shapes],
        scratch_shapes=scratch + sems,
        compiler_params=params(SMALL),
        cost_estimate=pl.CostEstimate(
            flops=0, bytes_accessed=8 * sum(a.size for a in args), transcendentals=0
        ),
        name=name,
    )(*places, *args)


class Piece:
    def __init__(self, plan, back):
        self.plan, self.back = plan, back
        self.sides = [side(step).astype(jnp.int32) for step in plan]
        first, second = self.sides[0], self.sides[1]

        def quarter(a, b):
            return 2 * a + b

        self.own_quarter = quarter(first, second).reshape(1)
        self.place = jnp.concatenate([self.own_quarter, jnp.stack(self.sides[2:])])

    def quarter_and_block(self, array, row):
        apart = {step: (row >> i) & 1 for i, step in enumerate(self.back[:-2])}
        apart[self.back[-2]] = array % 2
        block = 0
        for step in self.plan[2:]:
            block = 2 * block + apart[step]
        return 2 * (array // 2) + apart[self.plan[1]], block

    def open(self, send, keep):
        self.own = keep
        self.got = swap(send, self.plan[0])
        self.rider = None
        self.at = 1
        self.steps = 2 * len(self.plan)

    def quarter_shape(self):
        return (self.pair[0].shape[0] - (0 if self.rider is None else self.rider.shape[0]), QUARTER)

    def step(self, *tokens):
        last = len(self.plan)
        if self.at < last:
            own = self.sides[self.at] if self.at > 1 else jnp.ones((), jnp.int32)
            send, self.own, token = halve(self.own, self.got, own, tokens)
            self.got = swap(send, self.plan[self.at])
            self.at += 1
            return token
        if self.at == last:
            total, token = add(self.own, self.got, tokens)
            self.parts = [total]
            self.riders = [] if self.rider is None else [self.rider]
        else:
            self.parts.append(self.got)
            if self.rider is not None:
                self.riders = [self.whole, self.got]
        index = self.at - last
        self.at += 1
        if index < last - 1:
            rows = self.parts[0].shape[0]
            counts = [rows << max(i - 1, 0) for i in range(len(self.parts))]
            if len(self.parts) == 1 and not self.riders:
                self.whole = self.parts[0]
            else:
                height = 0 if self.rider is None else self.rider.shape[0]
                self.whole, token = gather_parts(
                    self.parts, counts, self.riders, height, tokens
                )
            self.got = swap(self.whole, self.back[index])
            return token
        self.pair = [self.whole, self.parts[-1]]
        self.got = [swap(v, self.plan[0]) for v in self.pair]
        return tokens[0]


def riders_of(piece):
    return piece.pair + piece.got


def run(token, *pieces):
    tokens = token if isinstance(token, tuple) else (token,)
    for piece in pieces:
        if piece.at < piece.steps:
            tokens = (piece.step(*tokens),)
    return tokens[0]


def local(
    inputs,
    cotangent,
    norm_gain,
    delta,
    alpha,
    beta,
    eta,
    omega,
    w_value,
    w_base,
    qk_scale,
    qk_shift,
    w_hidden,
    ffn_gain,
    w_up,
    w_down,
    lengths,
    key_mask,
):
    ways = lax.axis_size("ch")
    place = lax.axis_index("ch").astype(jnp.int32)
    _, length, narrow = inputs.shape
    rows = length // ways
    width = narrow * ways
    groups = width // LANES
    states = delta.shape[1]
    span = rows // SUBS

    x4 = lax.all_to_all(inputs.reshape(ways, rows, narrow), "ch", 0, 0)
    pairs = split_weights((w_value, w_base, w_hidden, w_up, w_down))

    def grouped(table):
        return jnp.transpose(table.reshape(groups, LANES, states), (0, 2, 1))

    gates = jax.nn.sigmoid(delta)
    decay = jax.nn.sigmoid(alpha)
    keep = 1.0 - gates * decay
    root = math.sqrt(states)
    keep4 = grouped(keep)
    coef4 = grouped(gates * beta * (eta / root))
    log_keep = jnp.log(keep4)
    chunk_keep = jnp.exp(span * log_keep)
    device_keep = jnp.exp(rows * log_keep)
    gain4 = norm_gain.reshape(groups, 1, LANES)
    omega4 = omega.reshape(groups, 1, LANES)
    place_info = place.reshape(1)

    ends_shape = jax.ShapeDtypeStruct((groups, states * SUBS, LANES), F32)
    final_shape = jax.ShapeDtypeStruct((groups, states, LANES), F32)
    big = jax.ShapeDtypeStruct((groups, rows, LANES), F32)
    normed4, ends, final = pl.pallas_call(
        norm_kernel,
        in_specs=[VMEM] * 4,
        out_specs=[VMEM] * 3,
        out_shape=[big, ends_shape, final_shape],
        compiler_params=params(NORM_MIB),
        name="norm",
    )(x4, gain4, keep4, chunk_keep)
    finals = lax.all_gather(final, "ch", axis=0)
    total4, starts = pl.pallas_call(
        mix_kernel,
        in_specs=[SMEM] + [VMEM] * 8,
        out_specs=[VMEM] * 2,
        out_shape=[big, ends_shape],
        compiler_params=params(NORM_MIB),
        name="mix",
    )(place_info, normed4, ends, finals, keep4, coef4, chunk_keep, device_keep, omega4)

    info = jnp.stack([place * rows, lengths[0].astype(jnp.int32)])
    zwidth = qk_scale.shape[1]
    plans = orders()
    unit = SUBS << (len(plans[0][0]) - 2)
    one, other, two, three = [Piece(*plan) for plan in plans]

    def height(*counts):
        return -(-sum(counts) // QUARTER // unit) * unit

    quarter_one = height((w_up.size + w_hidden.size // 2) // 4)
    quarter_other = height((w_down.size + w_hidden.size // 2) // 4)
    late = 2 * width * width
    quarter_two = height((w_value.size + width * zwidth + late // 2) // 4)
    quarter_three = height((width * w_value.shape[1] + late // 2) // 4)
    (
        output,
        direct4,
        vpre,
        rpre,
        zpre,
        grad_u,
        grad_h,
        ffn_gain_part,
        *ffn_parts,
    ) = forward_call(
        info,
        jnp.concatenate([one.own_quarter, other.own_quarter]),
        key_mask,
        x4,
        normed4,
        total4,
        cotangent.reshape(rows, width),
        qk_scale,
        qk_shift,
        ffn_gain.reshape(1, width),
        pairs,
        (quarter_one, quarter_other),
    )
    one.open(*ffn_parts[:2])
    other.open(*ffn_parts[2:])
    t = run(ffn_gain_part, one, other)
    grad4, part4, qk_part, omega_part, send_b, keep_b, send_c, keep_c = backward_call(
        info,
        jnp.concatenate([two.own_quarter, three.own_quarter]),
        key_mask,
        normed4,
        total4,
        (vpre, rpre, zpre, grad_u, grad_h),
        qk_scale,
        qk_shift,
        omega4,
        pairs,
        (quarter_two, quarter_three),
        [t],
    )
    t = run(qk_part, one, other)
    (send_b, send_c), t = gate((send_b, send_c), t)
    two.open(send_b, keep_b)
    three.open(send_c, keep_c)
    back_ends, back_final = scan_call(
        back_ends_kernel,
        "back_ends",
        [],
        [grad4, keep4, chunk_keep],
        [ends_shape, final_shape],
        [t],
        work=2,
    )
    back_finals = lax.all_gather(back_final, "ch", axis=0)
    t = run(back_finals, two, three)
    sums, coef_parts, keep_parts = [], [], []
    tables = (keep4, coef4, chunk_keep, device_keep)
    for lowest in range(0, groups, 2):
        done, coef_part, keep_part = back_call(
            lowest, 2, place_info, grad4, back_ends, back_finals, starts, normed4, part4, tables, [t]
        )
        sums.append(done)
        coef_parts.append(coef_part)
        keep_parts.append(keep_part)
        t = run(coef_part, two, three, one, other)
    back4, two.rider = unnorm_call(
        x4,
        sums,
        direct4,
        gain4,
        coef_parts,
        keep_parts,
        omega_part,
        ffn_gain_part,
        qk_part,
        [t],
    )
    back4, t = gate(back4, two.rider[:SUBS, :LANES])
    returned = lax.all_to_all(back4, "ch", 0, 0)
    input_grad = returned.reshape(inputs.shape)
    t = run(t, two, three, one, other)
    t = run(t, two, three, one, other)
    t = run((t, returned[0, :SUBS]), two, three, one, other)
    while three.at < three.steps:
        t = run(t, two, three, one, other)
    up_rows, quarter_rows = w_up.shape[0], w_down.shape[0] // 4
    half = w_hidden.shape[1] // 2
    hidden_rows = w_hidden.shape[0] // 4
    up_grad, down_grad, hidden_grad = finish(
        [one, other],
        [
            [
                (0, as_columns(0, up_rows, 0, lambda q: q * QUARTER)),
                (2, as_rows(up_rows, hidden_rows, 0, half)),
            ],
            [
                (1, as_rows(0, quarter_rows, 0, w_down.shape[1])),
                (
                    2,
                    as_rows(
                        quarter_rows * w_down.shape[1] // QUARTER, hidden_rows, half, 2 * half
                    ),
                ),
            ],
        ],
        [w_up.shape, w_down.shape, w_hidden.shape],
        "finish_one",
        [t],
    )
    z_at, z_rows = w_value.shape[0], width * zwidth // QUARTER // 4
    reset_at = width + zwidth
    hidden_in_at = reset_at + w_value.shape[1]

    def rest_column(q):
        return jnp.where(q < 2, q * QUARTER, hidden_in_at + (q - 2) * QUARTER)

    value_grad, base_grad = finish(
        [two, three],
        [
            [
                (0, as_columns(0, width, 0, lambda q: q * QUARTER)),
                (1, as_halves(z_at, z_rows, width)),
                (1, as_columns(z_at + z_rows, width // 2, 0, rest_column)),
            ],
            [
                (1, as_columns(0, width, 0, lambda q: reset_at + q * QUARTER)),
                (1, as_columns(width, width // 2, width // 2, rest_column)),
            ],
        ],
        [w_value.shape, w_base.shape],
        "finish_rest",
    )

    tables = [grouped(table) for table in (gates, decay, beta, eta)]
    gains = small_call(riders_of(two), tables)
    return (
        output.reshape(cotangent.shape),
        input_grad,
        gains[0].reshape(width),
        gains[1].T,
        gains[2].T,
        gains[3].T,
        gains[4].T,
        gains[5].reshape(width),
        value_grad,
        base_grad,
        gains[7],
        gains[8],
        hidden_grad,
        gains[6].reshape(width),
        up_grad,
        down_grad,
    )


def solution(mesh):
    whole = P()
    placed = (
        (P("seq", None, "ch"), P("seq", "ch", None))
        + (whole,) * 14
        + (P("seq"), P("seq", None))
    )
    return jax.shard_map(
        local,
        mesh=mesh,
        in_specs=placed,
        out_specs=(P("seq", "ch", None), P("seq", None, "ch")) + (whole,) * 14,
        check_vma=False,
    )
```

profile of v0, /device:TPU:0, one launch (start us, length us, event | category | flops | bytes accessed | tf_op | source)
XLA Modules:
  0.0 333.7 jit_solution(529851142583275420)
XLA Ops:
  0.7 4.4 %all-to-all-start = ((f32[4,1024,128]{2,1,0:T(8,128)}), f32[4,1024,128]{2,1,0:T(8,128)S(1)}, u32[]{:S(2)}, u32[]{:S(2)}) async-start(f32[4,1024,128]{2,1,0:T(8,128)} %bitcast.138), calls=%async_computation | async-start | bytes 4194304 | tf_op jit(solution)/shard_map/all_to_all | solution.py:1310
  8.0 1.6 copy-done.10
  9.6 1.6 copy-done.11
  12.8 5.8 %split_weights.1 = (bf16[512,1024]{1,0:T(8,128)(2,1)S(1)}, bf16[512,1024]{1,0:T(8,128)(2,1)S(1)}, bf16[512,2176]{1,0:T(8,128)(2,1)S(1)}, bf16[512,2176]{1,0:T(8,...) custom-call(f32[512,1024]{1,0:T(8,128)S(1)} %copy-done.9, ...), custom_call_target="tpu_custom_call" | custom-call | flops 12845056 | bytes 25690112 | tf_op jit(solution)/shard_map/split_weights/pallas_call | solution.py:101
  32.1 1.6 copy-done.5
  33.7 3.9 %norm.1 = (f32[4,1024,128]{2,1,0:T(8,128)S(1)}, f32[4,128,128]{2,1,0:T(8,128)S(1)}, f32[4,16,128]{2,1,0:T(8,128)S(1)}) custom-call(f32[4,1024,128]{2,1,0:T(8,128)S(1)} %copy-done.5, f32[4,1,128]{2,1,0:T(1,128)S(1)} %bitcast.133, f32[4,16,128]{2,1,0:T(8,128)S(1)} %bitcast.104, f32[4,16,128]{2,1,0:T(8,128)S(1)} %get-tuple-element.311.chunk_keep_ref.refs_2_.refs_9_), custom_call_target="tpu_custom_call" | custom-call | tf_op jit(solution)/shard_map/norm/pallas_call | solution.py:1332
  37.6 5.4 %all-gather = f32[16,16,128]{2,1,0:T(8,128)S(1)} all-gather(f32[4,16,128]{2,1,0:T(8,128)S(1)} %get-tuple-element.163), channel_id=2, replica_groups=mesh['seq'=8,'ch'=4] {'ch'}, dimensions={0}, use_global_device_ids=true | all-gather | bytes 163840 | tf_op jit(solution)/shard_map/all_gather | solution.py:1340
  43.0 5.6 %mix.1 = (f32[4,1024,128]{2,1,0:T(8,128)S(1)}, f32[4,128,128]{2,1,0:T(8,128)S(1)}) custom-call(s32[1]{0:T(128)} %bitcast.6.place_ref.refs_0_, f32[4,1024,128]{2,1,0:T(8,128)S(1)} %get-tuple-element.161.normed_ref.refs_3_.refs_5_, f32[4,128,128]{2,1,0:T(8,128)S(1)} %get-tuple-element.162.ends_ref, f32[4,4,16,128]{3,2,1,0:T(8,128)S(1)} %bitcast.120, ...), custom_call_target="tpu_custom_call" | custom-call | tf_op jit(solution)/shard_map/mix/pallas_call | solution.py:1341
  53.7 50.3 %forward.1 = (f32[1024,512]{1,0:T(8,128)}, f32[4,1024,128]{2,1,0:T(8,128)}, f32[1024,1024]{1,0:T(8,128)}, f32[1024,1024]{1,0:T(8,128)}, f32[1024,128]{1,0:T(8,12...) custom-call(s32[2]{0:T(128)S(1)} %get-tuple-element.314.info_ref.ref, ...), custom_call_target="tpu_custom_call" | custom-call | flops 32614907904 | bytes 50331648 | tf_op jit(solution)/shard_map/forward/pallas_call | solution.py:905
  105.4 3.0 collective-permute-done.1.refs_2_
  110.1 2.4 collective-permute-start.3
  112.7 1.6 collective-permute-start.2
  114.3 44.7 %backward.1 = (f32[4,1024,128]{2,1,0:T(8,128)}, f32[4,1024,128]{2,1,0:T(8,128)}, f32[8,128]{1,0:T(8,128)S(1)}, f32[4,1,128]{2,1,0:T(1,128)S(1)}, f32[2,832,256]{...) custom-call(s32[2]{0:T(128)S(1)} %get-tuple-element.314.info_ref.refs_0_, ...), custom_call_target="tpu_custom_call" | custom-call | flops 26575110144 | bytes 41943040 | tf_op jit(solution)/shard_map/backward/pallas_call | solution.py:48
  160.7 2.8 back_ends.1
  163.6 5.4 %all-gather.1 = f32[16,16,128]{2,1,0:T(8,128)S(1)} all-gather(f32[4,16,128]{2,1,0:T(8,128)S(1)} %get-tuple-element.200), channel_id=3, replica_groups=mesh['seq'=8,'ch'=4] {'ch'}, dimensions={0}, use_global_device_ids=true | all-gather | bytes 163840 | tf_op jit(solution)/shard_map/all_gather | solution.py:1418
  172.8 7.7 %back.2 = (f32[2,1024,128]{2,1,0:T(8,128)S(1)}, f32[2,16,128]{2,1,0:T(8,128)S(1)}, f32[2,16,128]{2,1,0:T(8,128)S(1)}) custom-call(s32[1]{0:T(128)} %bitcast.6.place_ref.refs_0_, f32[4,1024,128]{2,1,0:T(8,128)S(1)} %copy-done.2, f32[4,128,128]{2,1,0:T(8,128)S(1)} %get-tuple-element.199.refs_2_, f32[4,4,16,128]{3,2,1,0:T(8,128)S(1)} %bitcast.102, ...), custom_call_target="tpu_custom_call" | custom-call | flops 41943040 | bytes 3145728 | tf_op jit(solution)/shard_map/back/pallas_call | solution.py:48
  180.5 9.9 %collective-permute-done.9 = f32[832,256]{1,0:T(8,128)S(1)} collective-permute-done((f32[832,256]{1,0:T(8,128)S(1)}, f32[832,256]{1,0:T(8,128)S(1)}, u32[]{:S(2)}, u32[]{:S(2)}) %collective-permute-start.9) | collective-permute-done | bytes 852000 | tf_op jit(solution)/shard_map/ppermute | solution.py:1014
  195.6 2.4 collective-permute-done.6
  200.9 1.6 copy-done.3
  204.8 7.7 %back.3 = (f32[2,1024,128]{2,1,0:T(8,128)S(1)}, f32[2,16,128]{2,1,0:T(8,128)S(1)}, f32[2,16,128]{2,1,0:T(8,128)S(1)}) custom-call(s32[1]{0:T(128)} %bitcast.6.place_ref.refs_0_, f32[4,1024,128]{2,1,0:T(8,128)S(1)} %copy-done.3, f32[4,128,128]{2,1,0:T(8,128)S(1)} %get-tuple-element.199.refs_2_, f32[4,4,16,128]{3,2,1,0:T(8,128)S(1)} %bitcast.103, ...), custom_call_target="tpu_custom_call" | custom-call | flops 41943040 | bytes 3145728 | tf_op jit(solution)/shard_map/back/pallas_call | solution.py:48
  216.8 3.1 unnorm.1
  219.9 4.7 %all-to-all-start.1 = ((f32[4,1024,128]{2,1,0:T(8,128)}), f32[4,1024,128]{2,1,0:T(8,128)}, u32[]{:S(2)}, u32[]{:S(2)}) async-start(f32[4,1024,128]{2,1,0:T(8,128)} %get-tuple-element.243), calls=%async_computation.1 | async-start | bytes 4194304 | tf_op jit(solution)/shard_map/all_to_all | solution.py:1443
  226.9 2.6 collective-permute-start.17
  229.9 2.3 collective-permute-done.14
  232.2 2.7 collective-permute-start.15
  234.9 1.9 collective-permute-done.18
  236.9 3.0 collective-permute-start.21
  239.9 5.0 %collective-permute-done.16.refs_1_ = f32[96,256]{1,0:T(8,128)S(1)} collective-permute-done((f32[96,256]{1,0:T(8,128)S(1)}, f32[96,256]{1,0:T(8,128)S(1)}, u32[]{:S(2)}, u32[]{:S(2)}) %collective-permute-start.16) | collective-permute-done | bytes 98336 | tf_op jit(solution)/shard_map/ppermute | solution.py:1014
  245.0 2.2 collective-permute-done.15.refs_1_
  248.6 2.8 collective-permute-done.22.refs_1_
  251.5 5.1 %collective-permute-done.21.refs_1_ = f32[96,256]{1,0:T(8,128)S(1)} collective-permute-done((f32[96,256]{1,0:T(8,128)S(1)}, f32[96,256]{1,0:T(8,128)S(1)}, u32[]{:S(2)}, u32[]{:S(2)}) %collective-permute-start.21) | collective-permute-done | bytes 98336 | tf_op jit(solution)/shard_map/ppermute | solution.py:1014
  256.7 2.0 collective-permute-done.20.refs_1_
  258.7 2.0 collective-permute-start.24
  261.4 5.4 %collective-permute-done.19.refs_1_.refs_3_ = f32[184,256]{1,0:T(8,128)S(1)} collective-permute-done((f32[184,256]{1,0:T(8,128)S(1)}, f32[184,256]{1,0:T(8,128)S(1)}, u32[]{:S(2)}, u32[]{:S(2)}) %collective-permute-start.19) | collective-permute-done | bytes 188448 | tf_op jit(solution)/shard_map/ppermute | solution.py:1014
  266.9 1.8 collective-permute-done.26.refs_1_
  268.8 1.7 collective-permute-start.29
  271.4 1.9 collective-permute-start.30
  273.3 5.6 %collective-permute-done.23.refs_2_.refs_4_ = f32[288,256]{1,0:T(8,128)S(1)} collective-permute-done((f32[288,256]{1,0:T(8,128)S(1)}, f32[288,256]{1,0:T(8,128)S(1)}, u32[]{:S(2)}, u32[]{:S(2)}) %collective-permute-start.23) | collective-permute-done | bytes 294944 | tf_op jit(solution)/shard_map/ppermute | solution.py:1014
  278.9 1.7 collective-permute-start.27
  280.6 6.2 %collective-permute-done.30.refs_2_ = f32[192,256]{1,0:T(8,128)S(1)} collective-permute-done((f32[192,256]{1,0:T(8,128)S(1)}, f32[192,256]{1,0:T(8,128)S(1)}, u32[]{:S(2)}, u32[]{:S(2)}) %collective-permute-start.30) | collective-permute-done | bytes 196640 | tf_op jit(solution)/shard_map/ppermute | solution.py:1014
  289.0 8.7 %collective-permute-done.27.refs_3_.refs_5_ = f32[496,256]{1,0:T(8,128)S(1)} collective-permute-done((f32[496,256]{1,0:T(8,128)S(1)}, f32[496,256]{1,0:T(8,128)S(1)}, u32[]{:S(2)}, u32[]{:S(2)}) %collective-permute-start.27) | collective-permute-done | bytes 507936 | tf_op jit(solution)/shard_map/ppermute | solution.py:1014
  298.8 5.5 %collective-permute-done.41.refs_7_ = f32[768,256]{1,0:T(8,128)S(1)} collective-permute-done((f32[768,256]{1,0:T(8,128)S(1)}, f32[768,256]{1,0:T(8,128)S(1)}, u32[]{:S(2)}, u32[]{:S(2)}) %collective-permute-start.41) | collective-permute-done | bytes 786464 | tf_op jit(solution)/shard_map/ppermute | solution.py:1014
  305.5 7.3 %collective-permute-done.38.refs_3_ = f32[768,256]{1,0:T(8,128)S(1)} collective-permute-done((f32[768,256]{1,0:T(8,128)S(1)}, f32[768,256]{1,0:T(8,128)S(1)}, u32[]{:S(2)}, u32[]{:S(2)}) %collective-permute-start.38) | collective-permute-done | bytes 786464 | tf_op jit(solution)/shard_map/ppermute | solution.py:1014
  313.4 3.7 %collective-permute-done.31.part_b.refs_3_ = f32[912,256]{1,0:T(8,128)S(1)} collective-permute-done((f32[912,256]{1,0:T(8,128)S(1)}, f32[912,256]{1,0:T(8,128)S(1)}, u32[]{:S(2)}, u32[]{:S(2)}) %collective-permute-start.31) | collective-permute-done | bytes 933920 | tf_op jit(solution)/shard_map/ppermute | solution.py:1014
  317.7 2.4 collective-permute-done.35.refs_7_
  322.3 3.7 %finish_one.1 = (f32[512,1024]{1,0:T(8,128)}, f32[1024,512]{1,0:T(8,128)}, f32[1024,512]{1,0:T(8,128)}) custom-call(s32[4]{0:T(128)S(1)} %add_add_fusion.2.refs_0_, s32[4]{0:T(128)S(1)} %add_add_fusion.3.refs_1_, f32[768,256]{1,0:T(8,128)S(1)} %get-tuple-element.299.refs_2_, f32[768,256]{1,0:T(8,128)S(1)} %collective-permute-done.38.refs_3_, ...), custom_call_target="tpu_custom_call" | custom-call | bytes 12582912 | tf_op jit(solution)/shard_map/finish_one/pallas_call | solution.py:48
  326.1 3.8 %finish_rest.1 = (f32[512,1024]{1,0:T(8,128)}, f32[512,2176]{1,0:T(8,128)}) custom-call(s32[4]{0:T(128)S(1)} %add_add_fusion.refs_0_, s32[4]{0:T(128)S(1)} %add_add_fusion.1.refs_1_, f32[912,256]{1,0:T(8,128)S(1)} %get-tuple-element.285.part_a.refs_2_, f32[912,256]{1,0:T(8,128)S(1)} %collective-permute-done.31.part_b.refs_3_, ...), custom_call_target="tpu_custom_call" | custom-call | bytes 13762560 | tf_op jit(solution)/shard_map/finish_rest/pallas_call | solution.py:48
  330.6 3.0 copy.66
  (250 shorter events, 60.0 us)
Async XLA Ops:
  0.7 30.1 %all-to-all-start = ((f32[4,1024,128]{2,1,0:T(8,128)}), f32[4,1024,128]{2,1,0:T(8,128)S(1)}, u32[]{:S(2)}, u32[]{:S(2)}) async-start(f32[4,1024,128]{2,1,0:T(8,128)} %bitcast.138), calls=%async_computation | async-start | bytes 4194304 | tf_op jit(solution)/shard_map/all_to_all | solution.py:1310
  104.8 3.6 %collective-permute-start.1 = (f32[2,768,256]{2,1,0:T(8,128)}, f32[2,768,256]{2,1,0:T(8,128)S(1)}, u32[]{:S(2)}, u32[]{:S(2)}) collective-permute-start(f32[2,768,256]{2,1,0:T(8,128)} %get-tuple-element.184), channel_id=1, source_target_pairs={{0,1},{1,0},{2,3},{3,2},{4,5},{5,4},{6,7},{7,6},{8,9},{9,8},{10,11... | collective-permute-start | bytes 4718600 | tf_op jit(solution)/shard_map/ppermute | solution.py:1014
  105.1 7.4 %collective-permute-start = (f32[2,768,256]{2,1,0:T(8,128)}, f32[2,768,256]{2,1,0:T(8,128)S(1)}, u32[]{:S(2)}, u32[]{:S(2)}) collective-permute-start(f32[2,768,256]{2,1,0:T(8,128)} %get-tuple-element.182), channel_id=1, source_target_pairs={{0,1},{1,0},{2,3},{3,2},{4,5},{5,4},{6,7},{7,6},{8,9},{9,8},{10,11... | collective-permute-start | bytes 4718600 | tf_op jit(solution)/shard_map/ppermute | solution.py:1014
  110.1 49.1 %collective-permute-start.3 = (f32[768,256]{1,0:T(8,128)S(1)}, f32[768,256]{1,0:T(8,128)S(1)}, u32[]{:S(2)}, u32[]{:S(2)}) collective-permute-start(f32[768,256]{1,0:T(8,128)S(1)} %get-tuple-element.194), channel_id=1, source_target_pairs={{0,4},{4,0},{8,12},{12,8},{16,20},{20,16},{24,28},{28,24},{1,5},{5... | collective-permute-start | bytes 2359304 | tf_op jit(solution)/shard_map/ppermute | solution.py:1014
  112.7 46.6 %collective-permute-start.2 = (f32[768,256]{1,0:T(8,128)S(1)}, f32[768,256]{1,0:T(8,128)S(1)}, u32[]{:S(2)}, u32[]{:S(2)}) collective-permute-start(f32[768,256]{1,0:T(8,128)S(1)} %get-tuple-element.192), channel_id=1, source_target_pairs={{0,8},{4,12},{8,0},{12,4},{16,24},{20,28},{24,16},{28,20},{1,9},{5... | collective-permute-start | bytes 2359304 | tf_op jit(solution)/shard_map/ppermute | solution.py:1014
  159.4 9.6 %collective-permute-start.5 = (f32[2,832,256]{2,1,0:T(8,128)}, f32[2,832,256]{2,1,0:T(8,128)S(1)}, u32[]{:S(2)}, u32[]{:S(2)}) collective-permute-start(f32[2,832,256]{2,1,0:T(8,128)} %get-tuple-element.206), channel_id=1, source_target_pairs={{0,1},{1,0},{2,3},{3,2},{4,5},{5,4},{6,7},{7,6},{8,9},{9,8},{10,11... | collective-permute-start | bytes 5111816 | tf_op jit(solution)/shard_map/ppermute | solution.py:1014
  159.4 10.4 %collective-permute-start.4 = (f32[2,768,256]{2,1,0:T(8,128)S(1)}, f32[2,768,256]{2,1,0:T(8,128)S(1)}, u32[]{:S(2)}, u32[]{:S(2)}) collective-permute-start(f32[2,768,256]{2,1,0:T(8,128)S(1)} %get-tuple-element.204), channel_id=1, source_target_pairs={{0,1},{1,0},{2,3},{3,2},{4,5},{5,4},{6,7},{7,6},{8,9},{9,8},{10,11... | collective-permute-start | bytes 4718600 | tf_op jit(solution)/shard_map/ppermute | solution.py:1014
  169.2 21.3 %collective-permute-start.9 = (f32[832,256]{1,0:T(8,128)S(1)}, f32[832,256]{1,0:T(8,128)S(1)}, u32[]{:S(2)}, u32[]{:S(2)}) collective-permute-start(f32[832,256]{1,0:T(8,128)S(1)} %get-tuple-element.217), channel_id=1, source_target_pairs={{0,2},{1,3},{2,0},{3,1},{4,6},{5,7},{6,4},{7,5},{8,10},{9,11},{10,... | collective-permute-start | bytes 2555912 | tf_op jit(solution)/shard_map/ppermute | solution.py:1014
  170.0 22.0 %collective-permute-start.8 = (f32[768,256]{1,0:T(8,128)S(1)}, f32[768,256]{1,0:T(8,128)S(1)}, u32[]{:S(2)}, u32[]{:S(2)}) collective-permute-start(f32[768,256]{1,0:T(8,128)S(1)} %get-tuple-element.215), channel_id=1, source_target_pairs={{0,4},{4,0},{8,12},{12,8},{16,20},{20,16},{24,28},{28,24},{1,5},{5... | collective-permute-start | bytes 2359304 | tf_op jit(solution)/shard_map/ppermute | solution.py:1014
  171.2 22.2 %collective-permute-start.7 = (f32[384,256]{1,0:T(8,128)S(1)}, f32[384,256]{1,0:T(8,128)S(1)}, u32[]{:S(2)}, u32[]{:S(2)}) collective-permute-start(f32[384,256]{1,0:T(8,128)S(1)} %get-tuple-element.213), channel_id=1, source_target_pairs={{0,8},{4,12},{8,0},{12,4},{16,24},{20,28},{24,16},{28,20},{1,9},{5... | collective-permute-start | bytes 1179656 | tf_op jit(solution)/shard_map/ppermute | solution.py:1014
  172.3 25.7 %collective-permute-start.6 = (f32[384,256]{1,0:T(8,128)S(1)}, f32[384,256]{1,0:T(8,128)S(1)}, u32[]{:S(2)}, u32[]{:S(2)}) collective-permute-start(f32[384,256]{1,0:T(8,128)S(1)} %get-tuple-element.211), channel_id=1, source_target_pairs={{0,4},{4,0},{8,12},{12,8},{16,20},{20,16},{24,28},{28,24},{1,5},{5... | collective-permute-start | bytes 1179656 | tf_op jit(solution)/shard_map/ppermute | solution.py:1014
  191.3 21.3 %collective-permute-start.13 = (f32[416,256]{1,0:T(8,128)}, f32[416,256]{1,0:T(8,128)}, u32[]{:S(2)}, u32[]{:S(2)}) collective-permute-start(f32[416,256]{1,0:T(8,128)} %get-tuple-element.236), channel_id=1, source_target_pairs={{0,8},{4,12},{8,0},{12,4},{16,24},{20,28},{24,16},{28,20},{1,9},{5... | collective-permute-start | bytes 1277960 | tf_op jit(solution)/shard_map/ppermute | solution.py:1014
  192.9 20.9 %collective-permute-start.12 = (f32[384,256]{1,0:T(8,128)}, f32[384,256]{1,0:T(8,128)}, u32[]{:S(2)}, u32[]{:S(2)}) collective-permute-start(f32[384,256]{1,0:T(8,128)} %get-tuple-element.234), channel_id=1, source_target_pairs={{0,2},{1,3},{2,0},{3,1},{4,6},{5,7},{6,4},{7,5},{8,10},{9,11},{10,... | collective-permute-start | bytes 1179656 | tf_op jit(solution)/shard_map/ppermute | solution.py:1014
  194.1 20.7 %collective-permute-start.11 = (f32[192,256]{1,0:T(8,128)}, f32[192,256]{1,0:T(8,128)}, u32[]{:S(2)}, u32[]{:S(2)}) collective-permute-start(f32[192,256]{1,0:T(8,128)} %get-tuple-element.232), channel_id=1, source_target_pairs={{0,2},{1,3},{2,0},{3,1},{4,6},{5,7},{6,4},{7,5},{8,10},{9,11},{10,... | collective-permute-start | bytes 589832 | tf_op jit(solution)/shard_map/ppermute | solution.py:1014
  199.4 16.4 %collective-permute-start.10 = (f32[192,256]{1,0:T(8,128)}, f32[192,256]{1,0:T(8,128)}, u32[]{:S(2)}, u32[]{:S(2)}) collective-permute-start(f32[192,256]{1,0:T(8,128)} %get-tuple-element.230), channel_id=1, source_target_pairs={{0,2},{1,3},{2,0},{3,1},{4,6},{5,7},{6,4},{7,5},{8,10},{9,11},{10,... | collective-permute-start | bytes 589832 | tf_op jit(solution)/shard_map/ppermute | solution.py:1014
  219.9 40.8 %all-to-all-start.1 = ((f32[4,1024,128]{2,1,0:T(8,128)}), f32[4,1024,128]{2,1,0:T(8,128)}, u32[]{:S(2)}, u32[]{:S(2)}) async-start(f32[4,1024,128]{2,1,0:T(8,128)} %get-tuple-element.243), calls=%async_computation.1 | async-start | bytes 4194304 | tf_op jit(solution)/shard_map/all_to_all | solution.py:1443
  224.6 7.6 %collective-permute-start.14 = (f32[208,256]{1,0:T(8,128)S(1)}, f32[208,256]{1,0:T(8,128)S(1)}, u32[]{:S(2)}, u32[]{:S(2)}) collective-permute-start(f32[208,256]{1,0:T(8,128)S(1)} %get-tuple-element.245), channel_id=1, source_target_pairs={{0,4},{4,0},{8,12},{12,8},{16,20},{20,16},{24,28},{28,24},{1,5},{5... | collective-permute-start | bytes 638984 | tf_op jit(solution)/shard_map/ppermute | solution.py:1014
  225.8 11.0 %collective-permute-start.18 = (f32[192,256]{1,0:T(8,128)S(1)}, f32[192,256]{1,0:T(8,128)S(1)}, u32[]{:S(2)}, u32[]{:S(2)}) collective-permute-start(f32[192,256]{1,0:T(8,128)S(1)} %get-tuple-element.254), channel_id=1, source_target_pairs={{0,8},{4,12},{8,0},{12,4},{16,24},{20,28},{24,16},{28,20},{1,9},{5... | collective-permute-start | bytes 589832 | tf_op jit(solution)/shard_map/ppermute | solution.py:1014
  226.9 9.9 %collective-permute-start.17 = (f32[96,256]{1,0:T(8,128)S(1)}, f32[96,256]{1,0:T(8,128)S(1)}, u32[]{:S(2)}, u32[]{:S(2)}) collective-permute-start(f32[96,256]{1,0:T(8,128)S(1)} %get-tuple-element.252), channel_id=1, source_target_pairs={{0,16},{4,20},{8,24},{12,28},{16,0},{20,4},{24,8},{28,12},{1,17},{... | collective-permute-start | bytes 294920 | tf_op jit(solution)/shard_map/ppermute | solution.py:1014
  229.5 15.4 %collective-permute-start.16 = (f32[96,256]{1,0:T(8,128)S(1)}, f32[96,256]{1,0:T(8,128)S(1)}, u32[]{:S(2)}, u32[]{:S(2)}) collective-permute-start(f32[96,256]{1,0:T(8,128)S(1)} %get-tuple-element.250), channel_id=1, source_target_pairs={{0,16},{4,20},{8,24},{12,28},{16,0},{20,4},{24,8},{28,12},{1,17},{... | collective-permute-start | bytes 294920 | tf_op jit(solution)/shard_map/ppermute | solution.py:1014
  232.2 14.9 %collective-permute-start.15 = (f32[104,256]{1,0:T(8,128)S(1)}, f32[104,256]{1,0:T(8,128)S(1)}, u32[]{:S(2)}, u32[]{:S(2)}) collective-permute-start(f32[104,256]{1,0:T(8,128)S(1)} %get-tuple-element.248), channel_id=1, source_target_pairs={{0,16},{4,20},{8,24},{12,28},{16,0},{20,4},{24,8},{28,12},{1,17},{... | collective-permute-start | bytes 319496 | tf_op jit(solution)/shard_map/ppermute | solution.py:1014
  236.8 14.6 %collective-permute-start.22 = (f32[96,256]{1,0:T(8,128)S(1)}, f32[96,256]{1,0:T(8,128)S(1)}, u32[]{:S(2)}, u32[]{:S(2)}) collective-permute-start(f32[96,256]{1,0:T(8,128)S(1)} %get-tuple-element.264), channel_id=1, source_target_pairs={{0,16},{4,20},{8,24},{12,28},{16,0},{20,4},{24,8},{28,12},{1,17},{... | collective-permute-start | bytes 294920 | tf_op jit(solution)/shard_map/ppermute | solution.py:1014
  236.9 19.7 %collective-permute-start.21 = (f32[96,256]{1,0:T(8,128)S(1)}, f32[96,256]{1,0:T(8,128)S(1)}, u32[]{:S(2)}, u32[]{:S(2)}) collective-permute-start(f32[96,256]{1,0:T(8,128)S(1)} %get-tuple-element.262.refs_0_), channel_id=1, source_target_pairs={{0,16},{4,20},{8,24},{12,28},{16,0},{20,4},{24,8},{28,12},{1,17},{... | collective-permute-start | bytes 294920 | tf_op jit(solution)/shard_map/ppermute | solution.py:1014
  244.9 13.8 %collective-permute-start.20 = (f32[96,256]{1,0:T(8,128)S(1)}, f32[96,256]{1,0:T(8,128)S(1)}, u32[]{:S(2)}, u32[]{:S(2)}) collective-permute-start(f32[96,256]{1,0:T(8,128)S(1)} %get-tuple-element.261.refs_0_), channel_id=1, source_target_pairs={{0,16},{4,20},{8,24},{12,28},{16,0},{20,4},{24,8},{28,12},{1,17},{... | collective-permute-start | bytes 294920 | tf_op jit(solution)/shard_map/ppermute | solution.py:1014
  247.8 19.0 %collective-permute-start.19 = (f32[184,256]{1,0:T(8,128)S(1)}, f32[184,256]{1,0:T(8,128)S(1)}, u32[]{:S(2)}, u32[]{:S(2)}) collective-permute-start(f32[184,256]{1,0:T(8,128)S(1)} %get-tuple-element.260.refs_2_), channel_id=1, source_target_pairs={{0,16},{4,20},{8,24},{12,28},{16,0},{20,4},{24,8},{28,12},{1,17},{... | collective-permute-start | bytes 565256 | tf_op jit(solution)/shard_map/ppermute | solution.py:1014
  251.4 17.3 %collective-permute-start.26 = (f32[96,256]{1,0:T(8,128)S(1)}, f32[96,256]{1,0:T(8,128)S(1)}, u32[]{:S(2)}, u32[]{:S(2)}) collective-permute-start(f32[96,256]{1,0:T(8,128)S(1)} %get-tuple-element.272.refs_0_), channel_id=1, source_target_pairs={{0,16},{4,20},{8,24},{12,28},{16,0},{20,4},{24,8},{28,12},{1,17},{... | collective-permute-start | bytes 294920 | tf_op jit(solution)/shard_map/ppermute | solution.py:1014
  256.6 12.1 %collective-permute-start.25 = (f32[192,256]{1,0:T(8,128)S(1)}, f32[192,256]{1,0:T(8,128)S(1)}, u32[]{:S(2)}, u32[]{:S(2)}) collective-permute-start(f32[192,256]{1,0:T(8,128)S(1)} %get-tuple-element.271), channel_id=1, source_target_pairs={{0,4},{4,0},{8,12},{12,8},{16,20},{20,16},{24,28},{28,24},{1,5},{5... | collective-permute-start | bytes 589832 | tf_op jit(solution)/shard_map/ppermute | solution.py:1014
  258.7 11.8 %collective-permute-start.24 = (f32[192,256]{1,0:T(8,128)S(1)}, f32[192,256]{1,0:T(8,128)S(1)}, u32[]{:S(2)}, u32[]{:S(2)}) collective-permute-start(f32[192,256]{1,0:T(8,128)S(1)} %get-tuple-element.270), channel_id=1, source_target_pairs={{0,2},{1,3},{2,0},{3,1},{4,6},{5,7},{6,4},{7,5},{8,10},{9,11},{10,... | collective-permute-start | bytes 589832 | tf_op jit(solution)/shard_map/ppermute | solution.py:1014
  268.8 18.1 %collective-permute-start.29 = (f32[384,256]{1,0:T(8,128)S(1)}, f32[384,256]{1,0:T(8,128)S(1)}, u32[]{:S(2)}, u32[]{:S(2)}) collective-permute-start(f32[384,256]{1,0:T(8,128)S(1)} %get-tuple-element.279), channel_id=1, source_target_pairs={{0,2},{1,3},{2,0},{3,1},{4,6},{5,7},{6,4},{7,5},{8,10},{9,11},{10,... | collective-permute-start | bytes 1179656 | tf_op jit(solution)/shard_map/ppermute | solution.py:1014
  270.5 16.5 %collective-permute-start.28 = (f32[384,256]{1,0:T(8,128)S(1)}, f32[384,256]{1,0:T(8,128)S(1)}, u32[]{:S(2)}, u32[]{:S(2)}) collective-permute-start(f32[384,256]{1,0:T(8,128)S(1)} %get-tuple-element.278), channel_id=1, source_target_pairs={{0,8},{4,12},{8,0},{12,4},{16,24},{20,28},{24,16},{28,20},{1,9},{5... | collective-permute-start | bytes 1179656 | tf_op jit(solution)/shard_map/ppermute | solution.py:1014
  270.6 8.3 %collective-permute-start.23 = (f32[288,256]{1,0:T(8,128)S(1)}, f32[288,256]{1,0:T(8,128)S(1)}, u32[]{:S(2)}, u32[]{:S(2)}) collective-permute-start(f32[288,256]{1,0:T(8,128)S(1)} %get-tuple-element.269.refs_3_), channel_id=1, source_target_pairs={{0,4},{4,0},{8,12},{12,8},{16,20},{20,16},{24,28},{28,24},{1,5},{5... | collective-permute-start | bytes 884744 | tf_op jit(solution)/shard_map/ppermute | solution.py:1014
  271.4 15.5 %collective-permute-start.30 = (f32[192,256]{1,0:T(8,128)S(1)}, f32[192,256]{1,0:T(8,128)S(1)}, u32[]{:S(2)}, u32[]{:S(2)}) collective-permute-start(f32[192,256]{1,0:T(8,128)S(1)} %get-tuple-element.280), channel_id=1, source_target_pairs={{0,8},{4,12},{8,0},{12,4},{16,24},{20,28},{24,16},{28,20},{1,9},{5... | collective-permute-start | bytes 589832 | tf_op jit(solution)/shard_map/ppermute | solution.py:1014
  278.9 18.8 %collective-permute-start.27 = (f32[496,256]{1,0:T(8,128)S(1)}, f32[496,256]{1,0:T(8,128)S(1)}, u32[]{:S(2)}, u32[]{:S(2)}) collective-permute-start(f32[496,256]{1,0:T(8,128)S(1)} %get-tuple-element.277.refs_4_), channel_id=1, source_target_pairs={{0,8},{4,12},{8,0},{12,4},{16,24},{20,28},{24,16},{28,20},{1,9},{5... | collective-permute-start | bytes 1523720 | tf_op jit(solution)/shard_map/ppermute | solution.py:1014
  286.9 33.9 %copy-start.65 = (f32[512,16]{0,1:T(8,128)S(1)}, f32[512,16]{0,1:T(8,128)}, u32[]{:S(2)}) copy-start(f32[512,16]{0,1:T(8,128)} %param.24) | copy-start | bytes 98308
  286.9 33.9 %copy-start.67 = (f32[512,16]{0,1:T(8,128)S(1)}, f32[512,16]{0,1:T(8,128)}, u32[]{:S(2)}) copy-start(f32[512,16]{0,1:T(8,128)} %param.23) | copy-start | bytes 98308
  287.1 17.2 %collective-permute-start.41 = (f32[768,256]{1,0:T(8,128)S(1)}, f32[768,256]{1,0:T(8,128)S(1)}, u32[]{:S(2)}, u32[]{:S(2)}) collective-permute-start(f32[768,256]{1,0:T(8,128)S(1)} %get-tuple-element.300.refs_6_), channel_id=1, source_target_pairs={{0,4},{4,0},{8,12},{12,8},{16,20},{20,16},{24,28},{28,24},{1,5},{5... | collective-permute-start | bytes 2359304 | tf_op jit(solution)/shard_map/ppermute | solution.py:1014
  287.8 25.0 %collective-permute-start.38 = (f32[768,256]{1,0:T(8,128)S(1)}, f32[768,256]{1,0:T(8,128)S(1)}, u32[]{:S(2)}, u32[]{:S(2)}) collective-permute-start(f32[768,256]{1,0:T(8,128)S(1)} %get-tuple-element.299.refs_2_), channel_id=1, source_target_pairs={{0,8},{4,12},{8,0},{12,4},{16,24},{20,28},{24,16},{28,20},{1,9},{5... | collective-permute-start | bytes 2359304 | tf_op jit(solution)/shard_map/ppermute | solution.py:1014
  287.8 10.4 %collective-permute-start.34 = (f32[384,256]{1,0:T(8,128)S(1)}, f32[384,256]{1,0:T(8,128)S(1)}, u32[]{:S(2)}, u32[]{:S(2)}) collective-permute-start(f32[384,256]{1,0:T(8,128)S(1)} %get-tuple-element.292), channel_id=1, source_target_pairs={{0,2},{1,3},{2,0},{3,1},{4,6},{5,7},{6,4},{7,5},{8,10},{9,11},{10,... | collective-permute-start | bytes 1179656 | tf_op jit(solution)/shard_map/ppermute | solution.py:1014
  297.8 19.3 %collective-permute-start.31 = (f32[912,256]{1,0:T(8,128)S(1)}, f32[912,256]{1,0:T(8,128)S(1)}, u32[]{:S(2)}, u32[]{:S(2)}) collective-permute-start(f32[912,256]{1,0:T(8,128)S(1)} %get-tuple-element.285.part_a.refs_2_), channel_id=1, source_target_pairs={{0,2},{1,3},{2,0},{3,1},{4,6},{5,7},{6,4},{7,5},{8,10},{9,11},{10,... | collective-permute-start | bytes 2801672 | tf_op jit(solution)/shard_map/ppermute | solution.py:1014
  298.2 14.6 %collective-permute-start.42 = (f32[768,256]{1,0:T(8,128)S(1)}, f32[768,256]{1,0:T(8,128)S(1)}, u32[]{:S(2)}, u32[]{:S(2)}) collective-permute-start(f32[768,256]{1,0:T(8,128)S(1)} %get-tuple-element.300.refs_6_), channel_id=1, source_target_pairs={{0,1},{1,0},{2,3},{3,2},{4,5},{5,4},{6,7},{7,6},{8,9},{9,8},{10,11... | collective-permute-start | bytes 2359304 | tf_op jit(solution)/shard_map/ppermute | solution.py:1014
  298.2 18.9 %collective-permute-start.39 = (f32[768,256]{1,0:T(8,128)S(1)}, f32[768,256]{1,0:T(8,128)S(1)}, u32[]{:S(2)}, u32[]{:S(2)}) collective-permute-start(f32[768,256]{1,0:T(8,128)S(1)} %get-tuple-element.299.refs_2_), channel_id=1, source_target_pairs={{0,1},{1,0},{2,3},{3,2},{4,5},{5,4},{6,7},{7,6},{8,9},{9,8},{10,11... | collective-permute-start | bytes 2359304 | tf_op jit(solution)/shard_map/ppermute | solution.py:1014
  304.3 15.8 %collective-permute-start.35 = (f32[768,256]{1,0:T(8,128)S(1)}, f32[768,256]{1,0:T(8,128)S(1)}, u32[]{:S(2)}, u32[]{:S(2)}) collective-permute-start(f32[768,256]{1,0:T(8,128)S(1)} %get-tuple-element.294.refs_6_), channel_id=1, source_target_pairs={{0,4},{4,0},{8,12},{12,8},{16,20},{20,16},{24,28},{28,24},{1,5},{5... | collective-permute-start | bytes 2359304 | tf_op jit(solution)/shard_map/ppermute | solution.py:1014
  312.8 7.2 %collective-permute-start.43 = (f32[768,256]{1,0:T(8,128)S(1)}, f32[768,256]{1,0:T(8,128)S(1)}, u32[]{:S(2)}, u32[]{:S(2)}) collective-permute-start(f32[768,256]{1,0:T(8,128)S(1)} %collective-permute-done.41.refs_7_), channel_id=1, source_target_pairs={{0,1},{1,0},{2,3},{3,2},{4,5},{5,4},{6,7},{7,6},{8,9},{9,8},{10,11... | collective-permute-start | bytes 2359304 | tf_op jit(solution)/shard_map/ppermute | solution.py:1014
  312.8 13.2 %collective-permute-start.32 = (f32[912,256]{1,0:T(8,128)S(1)}, f32[912,256]{1,0:T(8,128)S(1)}, u32[]{:S(2)}, u32[]{:S(2)}) collective-permute-start(f32[912,256]{1,0:T(8,128)S(1)} %get-tuple-element.285.part_a.refs_2_), channel_id=1, source_target_pairs={{0,1},{1,0},{2,3},{3,2},{4,5},{5,4},{6,7},{7,6},{8,9},{9,8},{10,11... | collective-permute-start | bytes 2801672 | tf_op jit(solution)/shard_map/ppermute | solution.py:1014
  317.1 9.0 %collective-permute-start.33 = (f32[912,256]{1,0:T(8,128)S(1)}, f32[912,256]{1,0:T(8,128)S(1)}, u32[]{:S(2)}, u32[]{:S(2)}) collective-permute-start(f32[912,256]{1,0:T(8,128)S(1)} %collective-permute-done.31.part_b.refs_3_), channel_id=1, source_target_pairs={{0,1},{1,0},{2,3},{3,2},{4,5},{5,4},{6,7},{7,6},{8,9},{9,8},{10,11... | collective-permute-start | bytes 2801672 | tf_op jit(solution)/shard_map/ppermute | solution.py:1014
  317.2 8.9 %collective-permute-start.36 = (f32[768,256]{1,0:T(8,128)S(1)}, f32[768,256]{1,0:T(8,128)S(1)}, u32[]{:S(2)}, u32[]{:S(2)}) collective-permute-start(f32[768,256]{1,0:T(8,128)S(1)} %get-tuple-element.294.refs_6_), channel_id=1, source_target_pairs={{0,1},{1,0},{2,3},{3,2},{4,5},{5,4},{6,7},{7,6},{8,9},{9,8},{10,11... | collective-permute-start | bytes 2359304 | tf_op jit(solution)/shard_map/ppermute | solution.py:1014
  320.1 2.3 collective-permute-start.40
  320.1 6.0 %collective-permute-start.37 = (f32[768,256]{1,0:T(8,128)S(1)}, f32[768,256]{1,0:T(8,128)S(1)}, u32[]{:S(2)}, u32[]{:S(2)}) collective-permute-start(f32[768,256]{1,0:T(8,128)S(1)} %collective-permute-done.35.refs_7_), channel_id=1, source_target_pairs={{0,1},{1,0},{2,3},{3,2},{4,5},{5,4},{6,7},{7,6},{8,9},{9,8},{10,11... | collective-permute-start | bytes 2359304 | tf_op jit(solution)/shard_map/ppermute | solution.py:1014
  (70 other events, 455.6 us)
where the time goes:
time: 335 us; the launch traced here: 334 us
  Pallas kernels  149 us (44%)
  waiting for transfers between devices  86.4 us (26%)
  starting transfers between devices  47.6 us (14%)
  local copies, waits for them, and re-layouts  36.4 us (11%)
  blocking collectives  10.9 us (3%)
    ppermute x44, waiting for transfers between devices, swap(): return lax.ppermute(value, axis, [(i, i ^ distance) for i in range(size)])  84.9 us
    pallas_call x40, Pallas kernels, ordered_call(): return lambda *args: run(*args, *tokens)  82.8 us
    pallas_call x1, Pallas kernels, forward_call(): pl.pallas_call(forward_kernel, grid=(rows // TILE,), in_specs=[SMEM, SMEM...  50.3 us
    ppermute x44, starting transfers between devices, swap(): return lax.ppermute(value, axis, [(i, i ^ distance) for i in range(size)])  38.6 us
    unnamed x145, local copies, waits for them, and re-layouts  35.7 us
  transfers between devices with their start and end apart: 46, of which 21 were waited for; matrix products, arithmetic and copies ran while one was open for 1% of the time, Pallas kernels for 24%

commit v1 on v0

--- a/solution.py
+++ b/solution.py
@@ -313,25 +313,17 @@
 
 
 def unnorm_kernel(
+    calls,
     x_ref,
-    sum_a,
-    sum_b,
-    direct_ref,
-    gain_ref,
-    coef_a,
-    coef_b,
-    keep_a,
-    keep_b,
-    omega_ref,
-    ffn_ref,
-    qk_ref,
-    out_ref,
-    small_ref,
-    gain_grad,
+    *refs,
 ):
+    sums, refs = refs[:calls], refs[calls:]
+    direct_ref, gain_ref, refs = refs[0], refs[1], refs[2:]
+    coefs, keeps, refs = refs[:calls], refs[calls : 2 * calls], refs[2 * calls :]
+    omega_ref, ffn_ref, qk_ref, out_ref, small_ref, gain_grad = refs
     groups, rows, _ = x_ref.shape
     width = groups * LANES
-    share = sum_a.shape[0]
+    share = groups // calls
     tile = pl.program_id(0)
 
     @pl.when(tile == 0)
@@ -343,7 +335,7 @@
     square = rows_sum(sum(p * p for p in pieces)) / width
     scale = lax.rsqrt(square - mean * mean + EPS)
     centered = [(p - mean) * scale for p in pieces]
-    grads = [(sum_a, sum_b)[g // share][g % share] for g in range(groups)]
+    grads = [sums[g // share][g % share] for g in range(groups)]
     for g in range(groups):
         gain_grad[g : g + 1, :] += jnp.sum(grads[g] * centered[g], 0, keepdims=True)
     scaled = [grads[g] * gain_ref[g] for g in range(groups)]
@@ -354,8 +346,8 @@
 
     @pl.when(tile == pl.num_programs(0) - 1)
     def _():
-        states = coef_a.shape[1]
-        for i, refs in enumerate(((coef_a, coef_b), (keep_a, keep_b))):
+        states = coefs[0].shape[1]
+        for i, refs in enumerate((coefs, keeps)):
             for g in range(groups):
                 at = slice(g * states, (g + 1) * states)
                 small_ref[at, i * LANES : (i + 1) * LANES] = refs[g // share][g % share]
@@ -421,10 +413,10 @@
     halves = [pl.BlockSpec((s.shape[0], TILE, LANES), lambda i: (0, i, 0)) for s in sums]
     height = -(-(groups * states + 2 * groups) // 16) * 16
     return ordered_call(
-        unnorm_kernel,
+        lambda *refs: unnorm_kernel(len(sums), *refs),
         tokens,
         grid=(rows // TILE,),
-        in_specs=[by_group] + halves + [by_group] + [VMEM] * 8,
+        in_specs=[by_group] + halves + [by_group] + [VMEM] * (4 + 2 * len(sums)),
         out_specs=[by_group, pl.BlockSpec((height, 2 * LANES), lambda i: (0, 0))],
         out_shape=[shape_of(*x4.shape), shape_of(height, 2 * LANES)],
         scratch_shapes=[pltpu.VMEM((SUBS, LANES), F32)],
@@ -433,7 +425,7 @@
             flops=20 * x4.size, bytes_accessed=16 * x4.size, transcendentals=0
         ),
         name="unnorm",
-    )(x4, *sums, direct4, gain4, *coefs, *keeps, omega, ffn, qk)
+    )(x4, *sums, direct4, gain4, *coefs, *keeps, *omega, ffn, *qk)
 
 
 def small_kernel(
@@ -556,9 +548,30 @@
     return [value[:, i : i + QUARTER] for i in range(0, value.shape[1], QUARTER)]
 
 
+class Fetch:
+    def __init__(self, sources, targets, sems, first):
+        self.first = first
+        self.copies = [
+            pltpu.make_async_copy(source, target, sems.at[i])
+            for i, (source, target) in enumerate(zip(sources, targets))
+        ]
+
+        @pl.when(first)
+        def _():
+            for copy in self.copies:
+                copy.start()
+
+    def wait(self, *which):
+        @pl.when(self.first)
+        def _():
+            for i in which:
+                self.copies[i].wait()
+
+
 class HandOut:
-    def __init__(self, own, total, send, keep, sems, last):
+    def __init__(self, own, total, send, keep, row, sems, last):
         self.own, self.total, self.send, self.keep = own, total, send, keep
+        self.rows = pl.ds(row, total.shape[1])
         self.sems, self.last = sems, last
 
     def each(self, quarter, act):
@@ -568,7 +581,7 @@
         def _():
             act(
                 pltpu.make_async_copy(
-                    self.total.at[quarter], self.send.at[3 - apart], self.sems.at[quarter]
+                    self.total.at[quarter], self.send.at[3 - apart, self.rows], self.sems.at[quarter]
                 )
             )
 
@@ -576,7 +589,7 @@
         def _():
             act(
                 pltpu.make_async_copy(
-                    self.total.at[quarter], self.keep.at[1 - apart], self.sems.at[quarter]
+                    self.total.at[quarter], self.keep.at[1 - apart, self.rows], self.sems.at[quarter]
                 )
             )
 
@@ -611,18 +624,20 @@
     wd_l,
     out_ref,
     direct_ref,
-    vpre,
-    rpre,
+    v_h,
+    v_l,
+    vsil,
+    rst,
+    attr,
+    weight_h,
+    weight_l,
+    slope_ref,
     zpre,
     grad_u_ref,
     grad_h_ref,
     gain_grad_ref,
-    send_a,
-    keep_a,
-    send_b,
-    keep_b,
-    v_h,
-    v_l,
+    send_ref,
+    keep_ref,
     upd,
     hpre,
     gr_h,
@@ -646,8 +661,8 @@
     units = wu_h.shape[1]
     base_row, length = info_ref[0] + tile * rows, info_ref[1]
     last = tile == pl.num_programs(0) - 1
-    out_a = HandOut(place_ref[0], acc_a, send_a, keep_a, sems_a, last)
-    out_b = HandOut(place_ref[1], acc_b, send_b, keep_b, sems_b, last)
+    out_a = HandOut(place_ref[0], acc_a, send_ref, keep_ref, 0, sems_a, last)
+    out_b = HandOut(place_ref[1], acc_b, send_ref, keep_ref, acc_a.shape[1], sems_b, last)
 
     @pl.when(first)
     def _():
@@ -664,8 +679,10 @@
     m_pair = split(total * sigmoid(total))
     for c in columns(values):
         pre = mm3(n_pair, (wv_h[:, c], wv_l[:, c]), NN)
-        vpre[:, c] = pre
-        put(v_h, v_l, (EVERY, c), pre * sigmoid(pre))
+        s = sigmoid(pre)
+        act = pre * s
+        put(v_h, v_l, (EVERY, c), act)
+        vsil[:, c] = silu_slope(act, s)
     c = slice(width, width + zwidth)
     pre = mm3(m_pair, (wb_h[:, c], wb_l[:, c]), NN)
     zpre[...] = pre
@@ -676,14 +693,20 @@
     upd[...] = sigmoid(mm3(m_pair, (wb_h[:, c], wb_l[:, c]), NN))
     for c in columns(values):
         w = slice(width + zwidth + c.start, width + zwidth + c.stop)
-        rpre[:, c] = mm3(m_pair, (wb_h[:, w], wb_l[:, w]), NN)
+        pre = mm3(m_pair, (wb_h[:, w], wb_l[:, w]), NN)
+        s = sigmoid(pre)
+        act = pre * s
+        rst[:, c] = act
+        attr[:, c] = silu_slope(act, s)
     w = slice(width + zwidth + values, width + zwidth + values + width)
     hpre[...] = mm3(m_pair, (wb_h[:, w], wb_l[:, w]), NN)
     weight = attention.weight()
+    weight_h[...], weight_l[...] = weight
+    slope_ref[...] = attention.slope()
     for c in columns(values):
         got = mm3(weight, (v_h[:, c], v_l[:, c]), NN)
-        pre = rpre[:, c]
-        put(gr_h, gr_l, (EVERY, c), got * (pre * sigmoid(pre)))
+        put(gr_h, gr_l, (EVERY, c), got * rst[:, c])
+        attr[:, c] = got * attr[:, c]
     pre = hpre[...] + mm3((gr_h[...], gr_l[...]), (wh_h[...], wh_l[...]), NN)
     s = sigmoid(pre)
     hidden = pre * s
@@ -716,82 +739,99 @@
     grad_gated = grad_out + scale * (
         scaled - rows_sum(scaled) / width - centered * (rows_sum(scaled * centered) / width)
     )
-    grad_u_ref[...] = grad_gated * apart * update * (1.0 - update)
+    grad_u = grad_gated * apart * update * (1.0 - update)
+    grad_u_ref[...] = grad_u
+    u_pair = split(grad_u)
     grad_h = grad_gated * update * hpre[...]
     grad_h_ref[...] = grad_h
     h_pair = split(grad_h)
     direct = grad_gated * (1.0 - update)
     for g in range(groups):
         direct_ref[g] = direct[:, g * LANES : (g + 1) * LANES]
-    for q in range(4):
-        c = slice(q * QUARTER, (q + 1) * QUARTER)
-        at_a = add_to(acc_a, q, 0, [mm3(f_pair, (du_h[:, c], du_l[:, c]), TN)], first)
-        at_b = add_to(acc_b, q, 0, packed_rows(mm3((a_h[:, c], a_l[:, c]), do_pair, TN)), first)
-        packed = packed_rows(mm3((gr_h[:, c], gr_l[:, c]), h_pair, TN))
-        add_to(acc_a, q, at_a, packed[: len(packed) // 2], first)
-        add_to(acc_b, q, at_b, packed[len(packed) // 2 :], first)
-        out_a.start(q)
-        out_b.start(q)
+    for q in range(0, 4, 2):
+        c = slice(q * QUARTER, (q + 2) * QUARTER)
+        up = mm3(f_pair, (du_h[:, c], du_l[:, c]), TN)
+        rest = mm3(m_pair, u_pair if q == 0 else h_pair, TN)
+        down = mm3((a_h[:, c], a_l[:, c]), do_pair, TN)
+        hid = mm3((gr_h[:, c], gr_l[:, c]), h_pair, TN)
+        for i in range(2):
+            c = slice(i * QUARTER, (i + 1) * QUARTER)
+            at = add_to(acc_a, q + i, 0, [up[:, c]], first)
+            add_to(acc_a, q + i, at, [rest[:, c]], first)
+            at = add_to(acc_b, q + i, 0, packed_rows(down[c]), first)
+            add_to(acc_b, q + i, at, packed_rows(hid[c]), first)
+            out_a.start(q + i)
+            out_b.start(q + i)
     out_a.wait()
     out_b.wait()
 
 
 def backward_kernel(
-    info_ref,
+    continued,
     place_ref,
-    mask_ref,
     normed_ref,
     total_ref,
-    vpre,
-    rpre,
+    v_h,
+    v_l,
+    vsil,
+    rst,
+    attr,
+    weight_h,
+    weight_l,
+    slope_ref,
     zpre,
     grad_u_ref,
     grad_h_ref,
     scale_ref,
     shift_ref,
     omega_ref,
-    wv_h,
-    wv_l,
-    wb_h,
-    wb_l,
     wh_h,
     wh_l,
-    grad_ref,
-    part_ref,
-    qk_grad_ref,
-    omega_grad_ref,
-    send_b,
-    keep_b,
-    send_c,
-    keep_c,
-    v_h,
-    v_l,
-    vsil,
-    rst,
-    att,
-    da_h,
-    da_l,
-    dv_h,
-    dv_l,
-    bz_h,
-    bz_l,
-    br_h,
-    br_l,
-    acc_b,
-    acc_c,
-    sems_b,
-    sems_c,
+    wv_h_hbm,
+    wv_l_hbm,
+    wb_h_hbm,
+    wb_l_hbm,
+    *refs,
 ):
+    (
+        grad_ref,
+        part_ref,
+        qk_grad_ref,
+        omega_grad_ref,
+        send_ref,
+        keep_ref,
+        da_h,
+        da_l,
+        dv_h,
+        dv_l,
+        bz_h,
+        bz_l,
+        br_h,
+        br_l,
+        acc_b,
+        acc_c,
+        wv_h,
+        wv_l,
+        wb_h,
+        wb_l,
+        sems_b,
+        sems_c,
+        weight_sems,
+    ) = refs[2 if continued else 0 :]
     tile = pl.program_id(0)
-    first = tile == 0
-    groups, rows, _ = normed_ref.shape
+    first, last = tile == 0, tile == pl.num_programs(0) - 1
+    groups = normed_ref.shape[0]
     width = groups * LANES
     zwidth = scale_ref.shape[1]
-    values = wv_h.shape[1]
-    base_row, length = info_ref[0] + tile * rows, info_ref[1]
-    last = tile == pl.num_programs(0) - 1
-    out_b = HandOut(place_ref[0], acc_b, send_b, keep_b, sems_b, last)
-    out_c = HandOut(place_ref[1], acc_c, send_c, keep_c, sems_c, last)
+    values = vsil.shape[1]
+    fetch = Fetch(
+        [wv_h_hbm, wv_l_hbm, wb_h_hbm, wb_l_hbm],
+        [wv_h, wv_l, wb_h, wb_l],
+        weight_sems,
+        first,
+    )
+    out_b = HandOut(place_ref[0], acc_b, send_ref, keep_ref, 0, sems_b, last)
+    out_c = HandOut(place_ref[1], acc_c, send_ref, keep_ref, acc_b.shape[1], sems_c, last)
 
     @pl.when(first)
     def _():
@@ -802,41 +842,26 @@
         high, low = split(value)
         high_ref[where] = high
         low_ref[where] = low
-        return high, low
-
-    for c in columns(values):
-        pre = vpre[:, c]
-        s = sigmoid(pre)
-        act = pre * s
-        put(v_h, v_l, (EVERY, c), act)
-        vsil[:, c] = silu_slope(act, s)
-    pre = zpre[...]
-    s = sigmoid(pre)
-    z = pre * s
-    zsil = silu_slope(z, s)
-    attention = Attention(z, scale_ref, shift_ref, mask_ref, base_row, length)
-    weight = attention.weight()
-    for c in columns(values):
-        got = mm3(weight, (v_h[:, c], v_l[:, c]), NN)
-        pre = rpre[:, c]
-        s = sigmoid(pre)
-        act = pre * s
-        rst[:, c] = act
-        att[:, c] = got * silu_slope(act, s)
+
     u_pair = split(grad_u_ref[...])
     h_pair = split(grad_h_ref[...])
     for c in columns(values):
         got = mm3(h_pair, (wh_h[c, :], wh_l[c, :]), NT)
         put(da_h, da_l, (EVERY, c), got * rst[:, c])
-        put(br_h, br_l, (EVERY, c), got * att[:, c])
-    grad_scores = split(
-        mm3((da_h[...], da_l[...]), (v_h[...], v_l[...]), NT) * attention.slope()
-    )
+        put(br_h, br_l, (EVERY, c), got * attr[:, c])
+    pre = zpre[...]
+    s = sigmoid(pre)
+    z = pre * s
+    zsil = silu_slope(z, s)
+    query = split(z * scale_ref[0:1, :] + shift_ref[0:1, :])
+    key = split(z * scale_ref[1:2, :] + shift_ref[1:2, :])
+    weight = (weight_h[...], weight_l[...])
+    grad_scores = split(mm3((da_h[...], da_l[...]), (v_h[...], v_l[...]), NT) * slope_ref[...])
     for c in columns(values):
         got = mm3(weight, (da_h[:, c], da_l[:, c]), TN)
         put(dv_h, dv_l, (EVERY, c), got * vsil[:, c])
-    grad_q = mm3(grad_scores, attention.key, NN)
-    grad_k = mm3(grad_scores, attention.query, TN)
+    grad_q = mm3(grad_scores, key, NN)
+    grad_k = mm3(grad_scores, query, TN)
     qk_grad_ref[0:1, :] += jnp.sum(grad_q * z, 0, keepdims=True)
     qk_grad_ref[1:2, :] += jnp.sum(grad_k * z, 0, keepdims=True)
     qk_grad_ref[2:3, :] += jnp.sum(grad_q, 0, keepdims=True)
@@ -850,26 +875,25 @@
 
     n_pair = split(joined(normed_ref))
     total = joined(total_ref)
-    gate = sigmoid(total)
-    mixed = total * gate
+    gate_here = sigmoid(total)
+    mixed = total * gate_here
     m_pair = split(mixed)
-    for q in range(4):
-        c = slice(q * QUARTER, (q + 1) * QUARTER)
-        at_b = add_to(acc_b, q, 0, [mm3(n_pair, (dv_h[:, c], dv_l[:, c]), TN)], first)
-        w = slice(q * width // 4, (q + 1) * width // 4)
-        got = mm3((m_pair[0][:, w], m_pair[1][:, w]), (bz_h[...], bz_l[...]), TN)
-        half = got.shape[0] // 2
-        at_b = add_to(acc_b, q, at_b, [jnp.concatenate([got[:half], got[half:]], 1)], first)
-        at_c = add_to(acc_c, q, 0, [mm3(m_pair, (br_h[:, c], br_l[:, c]), TN)], first)
-        side_pair = u_pair if q < 2 else h_pair
-        c = slice(q % 2 * QUARTER, (q % 2 + 1) * QUARTER)
-        got = mm3(m_pair, (side_pair[0][:, c], side_pair[1][:, c]), TN)
-        half = got.shape[0] // 2
-        add_to(acc_b, q, at_b, [got[:half]], first)
-        add_to(acc_c, q, at_c, [got[half:]], first)
-        out_b.start(q)
-        out_c.start(q)
-
+    grad_bz = mm3(m_pair, (bz_h[...], bz_l[...]), TN)
+    for q in range(0, 4, 2):
+        c = slice(q * QUARTER, (q + 2) * QUARTER)
+        value = mm3(n_pair, (dv_h[:, c], dv_l[:, c]), TN)
+        reset = mm3(m_pair, (br_h[:, c], br_l[:, c]), TN)
+        for i in range(2):
+            c = slice(i * QUARTER, (i + 1) * QUARTER)
+            at = add_to(acc_b, q + i, 0, [value[:, c]], first)
+            got = grad_bz[(q + i) * width // 4 : (q + i + 1) * width // 4]
+            half = got.shape[0] // 2
+            add_to(acc_b, q + i, at, [jnp.concatenate([got[:half], got[half:]], 1)], first)
+            add_to(acc_c, q + i, 0, [reset[:, c]], first)
+            out_b.start(q + i)
+            out_c.start(q + i)
+
+    fetch.wait(0, 1, 2, 3)
     grad_n = mm3((dv_h[...], dv_l[...]), (wv_h[...], wv_l[...]), NT)
     at = [0, width, width + zwidth, width + zwidth + values, 2 * width + zwidth + values]
     w = [slice(i, j) for i, j in zip(at[:-1], at[1:])]
@@ -878,20 +902,19 @@
         + mm3_short((bz_h[...], bz_l[...]), (wb_h[:, w[1]], wb_l[:, w[1]]), NT)
         + mm3((br_h[...], br_l[...]), (wb_h[:, w[2]], wb_l[:, w[2]]), NT)
         + mm3(h_pair, (wb_h[:, w[3]], wb_l[:, w[3]]), NT)
-    ) * silu_slope(mixed, gate)
+    ) * silu_slope(mixed, gate_here)
     for g in range(groups):
         lanes = slice(g * LANES, (g + 1) * LANES)
         got = grad[:, lanes]
         grad_ref[g] = got
         part_ref[g] = grad_n[:, lanes] + got * omega_ref[g]
         omega_grad_ref[g] += jnp.sum(got * normed_ref[g], 0, keepdims=True)
-
     out_b.wait()
     out_c.wait()
 
 
-def by_row(count):
-    return pl.BlockSpec((TILE, count), lambda i: (i, 0))
+def by_row(count, lowest=0):
+    return pl.BlockSpec((TILE, count), lambda i: (lowest + i, 0))
 
 
 def forward_call(info, place, key_mask, x4, normed4, total4, cot, qk_scale, qk_shift, ffn_gain, pairs, heights):
@@ -912,29 +935,37 @@
             by_group,
             by_row(values),
             by_row(values),
+            by_row(values),
+            by_row(values),
+            by_row(values),
+            by_row(TILE),
+            by_row(TILE),
+            by_row(TILE),
             by_row(zwidth),
             by_row(width),
             by_row(width),
             pl.BlockSpec((1, width), lambda i: (0, 0)),
             HBM,
             HBM,
-            HBM,
-            HBM,
         ],
         out_shape=[
             shape_of(rows, width),
             shape_of(groups, rows, LANES),
+            shape_of(rows, values, dtype=BF16),
+            shape_of(rows, values, dtype=BF16),
             shape_of(rows, values),
             shape_of(rows, values),
+            shape_of(rows, values),
+            shape_of(rows, TILE, dtype=BF16),
+            shape_of(rows, TILE, dtype=BF16),
+            shape_of(rows, TILE),
             shape_of(rows, zwidth),
             shape_of(rows, width),
             shape_of(rows, width),
             shape_of(1, width),
         ]
-        + [shape_of(2, height, QUARTER) for height in heights for _ in range(2)],
+        + [shape_of(2, sum(heights), QUARTER)] * 2,
         scratch_shapes=[
-            pltpu.VMEM((TILE, values), BF16),
-            pltpu.VMEM((TILE, values), BF16),
             pltpu.VMEM((TILE, width), F32),
             pltpu.VMEM((TILE, width), F32),
             pltpu.VMEM((TILE, values), BF16),
@@ -954,30 +985,31 @@
 
 
 def backward_call(
-    info, place, key_mask, normed4, total4, saved, qk_scale, qk_shift, omega4, pairs, heights, tokens
+    place, normed4, total4, saved, qk_scale, qk_shift, omega4, pairs, heights, lowest, tiles, before, tokens
 ):
     groups, rows, _ = normed4.shape
     width = groups * LANES
     wv, wb, wh = pairs[:3]
     values, zwidth = wv[0].shape[1], qk_scale.shape[1]
-    flat = [part for pair in pairs[:3] for part in pair]
-    by_group = pl.BlockSpec((groups, TILE, LANES), lambda i: (0, i, 0))
-    macs = 2 * rows * (wv[0].size + wb[0].size + wh[0].size)
-    quarters = [shape_of(2, height, QUARTER) for height in heights for _ in range(2)]
+    by_group = pl.BlockSpec((groups, TILE, LANES), lambda i: (0, lowest + i, 0))
+    fetched = [*wv, *wb]
+    args = [place, normed4, total4, *saved, qk_scale, qk_shift, omega4, *wh, *fetched]
+    quarters = [shape_of(2, sum(heights), QUARTER)] * 2
     return ordered_call(
-        backward_kernel,
+        lambda *refs: backward_kernel(bool(before), *refs),
         tokens,
-        grid=(rows // TILE,),
-        in_specs=[SMEM, SMEM, VMEM, by_group, by_group]
-        + [by_row(s.shape[1]) for s in saved]
-        + [VMEM] * (3 + len(flat)),
+        grid=(tiles,),
+        in_specs=[SMEM, by_group, by_group]
+        + [by_row(s.shape[1], lowest) for s in saved]
+        + [VMEM] * (3 + len(wh))
+        + [HBM] * (len(fetched) + len(before)),
         out_specs=[
             by_group,
             by_group,
             pl.BlockSpec((8, zwidth), lambda i: (0, 0)),
             pl.BlockSpec((groups, 1, LANES), lambda i: (0, 0, 0)),
         ]
-        + [HBM] * 4,
+        + [HBM] * 2,
         out_shape=[
             shape_of(groups, rows, LANES),
             shape_of(groups, rows, LANES),
@@ -985,27 +1017,22 @@
             shape_of(groups, 1, LANES),
         ]
         + quarters,
-        scratch_shapes=[
-            pltpu.VMEM((TILE, values), BF16),
-            pltpu.VMEM((TILE, values), BF16),
-            pltpu.VMEM((TILE, values), F32),
-            pltpu.VMEM((TILE, values), F32),
-            pltpu.VMEM((TILE, values), F32),
-            pltpu.VMEM((TILE, values), BF16),
-            pltpu.VMEM((TILE, values), BF16),
-            pltpu.VMEM((TILE, values), BF16),
-            pltpu.VMEM((TILE, values), BF16),
-            pltpu.VMEM((TILE, zwidth), BF16),
-            pltpu.VMEM((TILE, zwidth), BF16),
-            pltpu.VMEM((TILE, values), BF16),
-            pltpu.VMEM((TILE, values), BF16),
-        ]
+        input_output_aliases={len(args): 0, len(args) + 1: 1} if before else {},
+        scratch_shapes=[pltpu.VMEM((TILE, values), BF16)] * 4
+        + [pltpu.VMEM((TILE, zwidth), BF16)] * 2
+        + [pltpu.VMEM((TILE, values), BF16)] * 2
         + [pltpu.VMEM((4, height, QUARTER), F32) for height in heights]
-        + [pltpu.SemaphoreType.DMA((4,))] * 2,
+        + [pltpu.VMEM(w.shape, BF16) for w in fetched]
+        + [pltpu.SemaphoreType.DMA((4,))] * 2
+        + [pltpu.SemaphoreType.DMA((len(fetched),))],
         compiler_params=params(BACKWARD_MIB),
-        cost_estimate=pl.CostEstimate(flops=6 * macs, bytes_accessed=40 << 20, transcendentals=0),
+        cost_estimate=pl.CostEstimate(
+            flops=12 * tiles * TILE * (wv[0].size + wb[0].size + wh[0].size),
+            bytes_accessed=40 << 20,
+            transcendentals=0,
+        ),
         name="backward",
-    )(info, place, key_mask, normed4, total4, *saved, qk_scale, qk_shift, omega4, *flat)
+    )(*args, *before)
 
 
 def swap(value, step):
@@ -1030,9 +1057,19 @@
 def orders():
     ch, seq = device_steps()
     x, y, z, rest = ch[1:], seq[:1], seq[1:2], seq[2:]
-    out = [y + z + x, z + y + x, x + z + y, y + x + z]
-    back = [y + x + z, x + z + y, y + z + x, z + x + y]
-    return [(ch[:1] + go + rest, rest[::-1] + come + ch[:1]) for go, come in zip(out, back)]
+    out = [
+        y + z + x + rest,
+        z + y + x + rest,
+        z + y + x + rest,
+        y + z + x + rest,
+    ]
+    back = [
+        rest[::-1] + z + x + y,
+        rest[::-1] + y + x + z,
+        rest[::-1] + y + z + x,
+        rest[::-1] + z + y + x,
+    ]
+    return [(ch[:1] + go, come + ch[:1]) for go, come in zip(out, back)]
 
 
 TOKEN = shape_of(SUBS, LANES)
@@ -1042,20 +1079,24 @@
     return lax.optimization_barrier((value, token))
 
 
-def halve_kernel(own_ref, keep_ref, got_ref, send_ref, next_ref, token_ref):
+def halve_kernel(count, first, own_ref, *refs):
     own = own_ref[0]
-    send_ref[...] = keep_ref[1 - own] + got_ref[1 - own]
-    next_ref[...] = keep_ref[own] + got_ref[own]
+    parts, (send_ref, next_ref, token_ref) = refs[:count], refs[count:]
+    rows = pl.ds(first, send_ref.shape[0])
+    send_ref[...] = sum(part[1 - own, rows, :] for part in parts)
+    next_ref[...] = sum(part[own, rows, :] for part in parts)
     token_ref[...] = jnp.zeros_like(token_ref)
 
 
-def halve(keep, got, own, tokens):
-    rows, width = keep.shape[-2] * (keep.shape[0] if keep.ndim == 3 else 1) // 2, keep.shape[-1]
-    keep, got = keep.reshape(2, rows, width), got.reshape(2, rows, width)
+def halve(parts, window, own, tokens):
+    width = parts[0].shape[-1]
+    height = parts[0].size // width // 2
+    first, rows = window or (0, height)
+    parts = [part.reshape(2, height, width) for part in parts]
     return ordered_call(
-        halve_kernel,
+        lambda *refs: halve_kernel(len(parts), first, *refs),
         tokens,
-        in_specs=[SMEM, VMEM, VMEM],
+        in_specs=[SMEM] + [VMEM] * len(parts),
         out_specs=[VMEM] * 3,
         out_shape=[shape_of(rows, width)] * 2 + [TOKEN],
         compiler_params=params(SMALL),
@@ -1063,7 +1104,7 @@
             flops=2 * rows * width, bytes_accessed=1 << 10, transcendentals=0
         ),
         name="halve",
-    )(own.reshape(1), keep, got)
+    )(own.reshape(1), *parts)
 
 
 def add_kernel(left_ref, right_ref, out_ref, token_ref):
@@ -1112,11 +1153,13 @@
     )(*parts, *riders)
 
 
-def finish_kernel(plans, maps, outs_count, *refs):
+def finish_kernel(plans, maps, given, outs_count, *refs):
     pieces = len(plans)
     places, refs = refs[:pieces], refs[pieces:]
     quarters, refs = refs[: 4 * pieces], refs[4 * pieces :]
-    outs, refs = refs[:outs_count], refs[outs_count:]
+    outs, refs = refs[given : given + outs_count], refs[given + outs_count :]
+    token_ref, refs = refs[0], refs[1:]
+    token_ref[...] = jnp.zeros_like(token_ref)
     scratch, sems = refs[:pieces], refs[pieces:]
     leave = []
     for p, plan in enumerate(plans):
@@ -1178,7 +1221,7 @@
     return moves
 
 
-def finish(pieces, plans, shapes, name, tokens=()):
+def finish(pieces, plans, shapes, name, tokens=(), into=None):
     args = [v for piece in pieces for v in piece.pair + list(piece.got)]
     places = [piece.place for piece in pieces]
     scratch = [pltpu.VMEM((4,) + piece.quarter_shape(), F32) for piece in pieces]
@@ -1186,19 +1229,21 @@
     for piece, plan in zip(pieces, plans):
         number = sum(len(moves(0)) for _, moves in plan)
         sems.append(pltpu.SemaphoreType.DMA((4, number)))
+    extra = [] if into is None else [into]
     return ordered_call(
-        lambda *refs: finish_kernel(plans, [p.quarter_and_block for p in pieces], len(shapes), *refs),
+        lambda *refs: finish_kernel(plans, [p.quarter_and_block for p in pieces], len(extra), len(shapes), *refs),
         tokens,
-        in_specs=[SMEM] * len(places) + [VMEM] * len(args),
-        out_specs=[HBM] * len(shapes),
-        out_shape=[shape_of(*shape) for shape in shapes],
+        in_specs=[SMEM] * len(places) + [VMEM] * len(args) + [HBM] * len(extra),
+        out_specs=[HBM] * len(shapes) + [VMEM],
+        input_output_aliases={len(places) + len(args): len(shapes) - 1} if extra else {},
+        out_shape=[shape_of(*shape) for shape in shapes] + [TOKEN],
         scratch_shapes=scratch + sems,
         compiler_params=params(SMALL),
         cost_estimate=pl.CostEstimate(
-            flops=0, bytes_accessed=8 * sum(a.size for a in args), transcendentals=0
+            flops=0, bytes_accessed=1 << 10, transcendentals=0
         ),
         name=name,
-    )(*places, *args)
+    )(*places, *args, *extra)
 
 
 class Piece:
@@ -1212,6 +1257,8 @@
 
         self.own_quarter = quarter(first, second).reshape(1)
         self.place = jnp.concatenate([self.own_quarter, jnp.stack(self.sides[2:])])
+        self.rider, self.waiting = None, []
+        self.at, self.steps = 1, 2 * len(plan)
 
     def quarter_and_block(self, array, row):
         apart = {step: (row >> i) & 1 for i, step in enumerate(self.back[:-2])}
@@ -1221,13 +1268,6 @@
             block = 2 * block + apart[step]
         return 2 * (array // 2) + apart[self.plan[1]], block
 
-    def open(self, send, keep):
-        self.own = keep
-        self.got = swap(send, self.plan[0])
-        self.rider = None
-        self.at = 1
-        self.steps = 2 * len(self.plan)
-
     def quarter_shape(self):
         return (self.pair[0].shape[0] - (0 if self.rider is None else self.rider.shape[0]), QUARTER)
 
@@ -1235,8 +1275,9 @@
         last = len(self.plan)
         if self.at < last:
             own = self.sides[self.at] if self.at > 1 else jnp.ones((), jnp.int32)
-            send, self.own, token = halve(self.own, self.got, own, tokens)
+            send, self.own, token = halve(self.waiting, self.window if self.at == 1 else None, own, tokens)
             self.got = swap(send, self.plan[self.at])
+            self.waiting = [self.own, self.got]
             self.at += 1
             return token
         if self.at == last:
@@ -1266,8 +1307,37 @@
         return tokens[0]
 
 
+def open_pieces(pieces, heights, send, keep):
+    got = swap(send, pieces[0].plan[0])
+    first = 0
+    for piece, rows in zip(pieces, heights):
+        piece.window = (first, rows)
+        piece.waiting += [keep, got]
+        first += rows
+
+
 def riders_of(piece):
     return piece.pair + piece.got
+
+
+def copy_out_kernel(in_ref, out_ref, sem):
+    copy = pltpu.make_async_copy(in_ref, out_ref, sem)
+    copy.start()
+    copy.wait()
+
+
+def copy_out(value, token):
+    return ordered_call(
+        copy_out_kernel,
+        [token],
+        in_specs=[VMEM],
+        out_specs=HBM,
+        out_shape=shape_of(*value.shape),
+        scratch_shapes=[pltpu.SemaphoreType.DMA(())],
+        compiler_params=params(SMALL),
+        cost_estimate=pl.CostEstimate(flops=0, bytes_accessed=1 << 10, transcendentals=0),
+        name="copy_out",
+    )(value)
 
 
 def run(token, *pieces):
@@ -1356,21 +1426,18 @@
     def height(*counts):
         return -(-sum(counts) // QUARTER // unit) * unit
 
-    quarter_one = height((w_up.size + w_hidden.size // 2) // 4)
-    quarter_other = height((w_down.size + w_hidden.size // 2) // 4)
-    late = 2 * width * width
-    quarter_two = height((w_value.size + width * zwidth + late // 2) // 4)
-    quarter_three = height((width * w_value.shape[1] + late // 2) // 4)
+    early_heights = (
+        height((w_up.size + 2 * width * width) // 4),
+        height((w_down.size + w_hidden.size) // 4),
+    )
+    late_heights = (
+        height((w_value.size + width * zwidth) // 4),
+        height(width * w_value.shape[1] // 4),
+    )
     (
         output,
         direct4,
-        vpre,
-        rpre,
-        zpre,
-        grad_u,
-        grad_h,
-        ffn_gain_part,
-        *ffn_parts,
+        *forward_rest,
     ) = forward_call(
         info,
         jnp.concatenate([one.own_quarter, other.own_quarter]),
@@ -1383,29 +1450,36 @@
         qk_shift,
         ffn_gain.reshape(1, width),
         pairs,
-        (quarter_one, quarter_other),
-    )
-    one.open(*ffn_parts[:2])
-    other.open(*ffn_parts[2:])
+        early_heights,
+    )
+    saved, ffn_gain_part, ffn_parts = forward_rest[:11], forward_rest[11], forward_rest[12:]
+    open_pieces((one, other), early_heights, *ffn_parts)
     t = run(ffn_gain_part, one, other)
-    grad4, part4, qk_part, omega_part, send_b, keep_b, send_c, keep_c = backward_call(
-        info,
-        jnp.concatenate([two.own_quarter, three.own_quarter]),
-        key_mask,
-        normed4,
-        total4,
-        (vpre, rpre, zpre, grad_u, grad_h),
-        qk_scale,
-        qk_shift,
-        omega4,
-        pairs,
-        (quarter_two, quarter_three),
-        [t],
-    )
-    t = run(qk_part, one, other)
-    (send_b, send_c), t = gate((send_b, send_c), t)
-    two.open(send_b, keep_b)
-    three.open(send_c, keep_c)
+    own_quarters = jnp.concatenate([two.own_quarter, three.own_quarter])
+    before, omega_parts, qk_parts = (), [], []
+    tiles = rows // TILE
+    for lowest, count in ((0, tiles),):
+        *before, qk_part, omega_part, send, keep = backward_call(
+            own_quarters,
+            normed4,
+            total4,
+            saved,
+            qk_scale,
+            qk_shift,
+            omega4,
+            pairs,
+            late_heights,
+            lowest,
+            count,
+            before,
+            [t],
+        )
+        omega_parts.append(omega_part)
+        qk_parts.append(qk_part)
+        t = run(qk_part, one, other)
+        send, t = gate(send, t)
+        open_pieces((two, three), late_heights, send, keep)
+    grad4, part4 = before
     back_ends, back_final = scan_call(
         back_ends_kernel,
         "back_ends",
@@ -1416,17 +1490,18 @@
         work=2,
     )
     back_finals = lax.all_gather(back_final, "ch", axis=0)
-    t = run(back_finals, two, three)
+    t = run(back_finals, two, one, three, other)
     sums, coef_parts, keep_parts = [], [], []
     tables = (keep4, coef4, chunk_keep, device_keep)
-    for lowest in range(0, groups, 2):
+    between = [(), (two, three, one, other), (two, three, one, other), (two, three)]
+    for g in range(groups):
         done, coef_part, keep_part = back_call(
-            lowest, 2, place_info, grad4, back_ends, back_finals, starts, normed4, part4, tables, [t]
+            g, 1, place_info, grad4, back_ends, back_finals, starts, normed4, part4, tables, [t]
         )
         sums.append(done)
         coef_parts.append(coef_part)
         keep_parts.append(keep_part)
-        t = run(coef_part, two, three, one, other)
+        t = run((coef_part, t), *between[g % 4])
     back4, two.rider = unnorm_call(
         x4,
         sums,
@@ -1434,66 +1509,66 @@
         gain4,
         coef_parts,
         keep_parts,
-        omega_part,
+        omega_parts,
         ffn_gain_part,
-        qk_part,
+        qk_parts,
         [t],
     )
     back4, t = gate(back4, two.rider[:SUBS, :LANES])
     returned = lax.all_to_all(back4, "ch", 0, 0)
-    input_grad = returned.reshape(inputs.shape)
-    t = run(t, two, three, one, other)
-    t = run(t, two, three, one, other)
-    t = run((t, returned[0, :SUBS]), two, three, one, other)
-    while three.at < three.steps:
+    t = run(t, one, other, two)
+    t = run(t, one, other, three)
+    t = run(t, two, three)
+    t = run(t, two, three)
+    t = run(t, one, other, two, three)
+    while three.at < three.steps or one.at < one.steps or other.at < other.steps:
         t = run(t, two, three, one, other)
     up_rows, quarter_rows = w_up.shape[0], w_down.shape[0] // 4
-    half = w_hidden.shape[1] // 2
-    hidden_rows = w_hidden.shape[0] // 4
-    up_grad, down_grad, hidden_grad = finish(
+    reset_at = width + zwidth
+    hidden_in_at = reset_at + w_value.shape[1]
+
+    def rest_column(q):
+        return jnp.where(q < 2, q * QUARTER, hidden_in_at + (q - 2) * QUARTER)
+
+    up_grad, down_grad, hidden_grad, base_grad, t = finish(
         [one, other],
         [
             [
                 (0, as_columns(0, up_rows, 0, lambda q: q * QUARTER)),
-                (2, as_rows(up_rows, hidden_rows, 0, half)),
+                (3, as_columns(up_rows, width, 0, rest_column)),
             ],
             [
                 (1, as_rows(0, quarter_rows, 0, w_down.shape[1])),
                 (
                     2,
                     as_rows(
-                        quarter_rows * w_down.shape[1] // QUARTER, hidden_rows, half, 2 * half
+                        quarter_rows * w_down.shape[1] // QUARTER,
+                        w_hidden.shape[0] // 4,
+                        0,
+                        w_hidden.shape[1],
                     ),
                 ),
             ],
         ],
-        [w_up.shape, w_down.shape, w_hidden.shape],
+        [w_up.shape, w_down.shape, w_hidden.shape, w_base.shape],
         "finish_one",
         [t],
     )
-    z_at, z_rows = w_value.shape[0], width * zwidth // QUARTER // 4
-    reset_at = width + zwidth
-    hidden_in_at = reset_at + w_value.shape[1]
-
-    def rest_column(q):
-        return jnp.where(q < 2, q * QUARTER, hidden_in_at + (q - 2) * QUARTER)
-
-    value_grad, base_grad = finish(
+    value_grad, base_grad, t = finish(
         [two, three],
         [
             [
                 (0, as_columns(0, width, 0, lambda q: q * QUARTER)),
-                (1, as_halves(z_at, z_rows, width)),
-                (1, as_columns(z_at + z_rows, width // 2, 0, rest_column)),
+                (1, as_halves(w_value.shape[0], width * zwidth // QUARTER // 4, width)),
             ],
-            [
-                (1, as_columns(0, width, 0, lambda q: reset_at + q * QUARTER)),
-                (1, as_columns(width, width // 2, width // 2, rest_column)),
-            ],
+            [(1, as_columns(0, width, 0, lambda q: reset_at + q * QUARTER))],
         ],
         [w_value.shape, w_base.shape],
         "finish_rest",
-    )
+        tokens=[t],
+        into=base_grad,
+    )
+    input_grad = copy_out(returned, t).reshape(inputs.shape)
 
     tables = [grouped(table) for table in (gates, decay, beta, eta)]
     gains = small_call(riders_of(two), tables)

time: 335 us -> 326 us (0.973)
  waiting for transfers between devices: 86.4 us -> 61 us
  local copies, waits for them, and re-layouts: 36.4 us -> 45.4 us
  Pallas kernels: 149 us -> 156 us
    ppermute x44 -> x42, waiting for transfers between devices: 84.9 us -> 55.7 us  [swap(): return lax.ppermute(value, axis, [(i, i ^ distance) for i in range(size)])]
    unnamed x145 -> x146, local copies, waits for them, and re-layouts: 35.7 us -> 44.6 us
    pallas_call x1, Pallas kernels: 50.3 us -> 57.3 us  [forward_call(): pl.pallas_call(forward_kernel, grid=(rows // TILE,), in_specs=[SMEM, SMEM...]
    ppermute x44 -> x42, starting transfers between devices: 38.6 us -> 40.4 us  [swap(): return lax.ppermute(value, axis, [(i, i ^ distance) for i in range(size)])]
    pallas_call x40 -> x43, Pallas kernels: 82.8 us -> 81.7 us  [ordered_call(): return lambda *args: run(*args, *tokens)]
  transfers between devices with their start and end apart: 46 -> 44, of which waited for: 21 -> 15; matrix products, arithmetic and copies ran while one was open for 1% -> 1% of each run, Pallas kernels for 24% -> 26%
where the time goes in v1:
time: 326 us; the launch traced here: 325 us
  Pallas kernels  156 us (48%)
  waiting for transfers between devices  61 us (19%)
  starting transfers between devices  48.4 us (15%)
  local copies, waits for them, and re-layouts  45.4 us (14%)
  blocking collectives  10.9 us (3%)
    pallas_call x43, Pallas kernels, ordered_call(): return lambda *args: run(*args, *tokens)  81.7 us
    pallas_call x1, Pallas kernels, forward_call(): pl.pallas_call(forward_kernel, grid=(rows // TILE,), in_specs=[SMEM, SMEM...  57.3 us
    ppermute x42, waiting for transfers between devices, swap(): return lax.ppermute(value, axis, [(i, i ^ distance) for i in range(size)])  55.7 us
    unnamed x146, local copies, waits for them, and re-layouts  44.6 us
    ppermute x42, starting transfers between devices, swap(): return lax.ppermute(value, axis, [(i, i ^ distance) for i in range(size)])  40.4 us
  transfers between devices with their start and end apart: 44, of which 15 were waited for; matrix products, arithmetic and copies ran while one was open for 1% of the time, Pallas kernels for 26%

profile of v1, /device:TPU:0, one launch (start us, length us, event | category | flops | bytes accessed | tf_op | source)
XLA Modules:
  0.0 324.8 jit_solution(8738821000010260769)
XLA Ops:
  0.7 4.4 %all-to-all-start = ((f32[4,1024,128]{2,1,0:T(8,128)}), f32[4,1024,128]{2,1,0:T(8,128)S(1)}, u32[]{:S(2)}, u32[]{:S(2)}) async-start(f32[4,1024,128]{2,1,0:T(8,128)} %bitcast.141), calls=%async_computation | async-start | bytes 4194304 | tf_op jit(solution)/shard_map/all_to_all | solution.py:1380
  12.8 5.8 %split_weights.1 = (bf16[512,1024]{1,0:T(8,128)(2,1)S(1)}, bf16[512,1024]{1,0:T(8,128)(2,1)S(1)}, bf16[512,2176]{1,0:T(8,128)(2,1)S(1)}, bf16[512,2176]{1,0:T(8,...) custom-call(f32[512,1024]{1,0:T(8,128)S(1)} %copy-done.17, ...), custom_call_target="tpu_custom_call" | custom-call | flops 12845056 | bytes 25690112 | tf_op jit(solution)/shard_map/split_weights/pallas_call | solution.py:101
  28.3 2.4 all-to-all-done.x_ref.refs_0_
  33.7 3.9 %norm.1 = (f32[4,1024,128]{2,1,0:T(8,128)S(1)}, f32[4,128,128]{2,1,0:T(8,128)S(1)}, f32[4,16,128]{2,1,0:T(8,128)S(1)}) custom-call(f32[4,1024,128]{2,1,0:T(8,128)S(1)} %copy-done.9, f32[4,1,128]{2,1,0:T(1,128)S(1)} %bitcast.135, f32[4,16,128]{2,1,0:T(8,128)S(1)} %bitcast.103, f32[4,16,128]{2,1,0:T(8,128)S(1)} %get-tuple-element.331.chunk_keep_ref.refs_2_.refs_9_), custom_call_target="tpu_custom_call" | custom-call | tf_op jit(solution)/shard_map/norm/pallas_call | solution.py:1402
  37.6 5.4 %all-gather = f32[16,16,128]{2,1,0:T(8,128)S(1)} all-gather(f32[4,16,128]{2,1,0:T(8,128)S(1)} %get-tuple-element.173), channel_id=2, replica_groups=mesh['seq'=8,'ch'=4] {'ch'}, dimensions={0}, use_global_device_ids=true | all-gather | bytes 163840 | tf_op jit(solution)/shard_map/all_gather | solution.py:1410
  43.0 5.6 %mix.1 = (f32[4,1024,128]{2,1,0:T(8,128)S(1)}, f32[4,128,128]{2,1,0:T(8,128)S(1)}) custom-call(s32[1]{0:T(128)} %bitcast.6.place_ref.refs_0_, f32[4,1024,128]{2,1,0:T(8,128)S(1)} %get-tuple-element.171.normed_ref.refs_1_.refs_5_, f32[4,128,128]{2,1,0:T(8,128)S(1)} %get-tuple-element.172.ends_ref, f32[4,4,16,128]{3,2,1,0:T(8,128)S(1)} %bitcast.120, ...), custom_call_target="tpu_custom_call" | custom-call | tf_op jit(solution)/shard_map/mix/pallas_call | solution.py:1411
  50.0 57.3 %forward.1 = (f32[1024,512]{1,0:T(8,128)}, f32[4,1024,128]{2,1,0:T(8,128)}, bf16[1024,1024]{1,0:T(8,128)(2,1)}, bf16[1024,1024]{1,0:T(8,128)(2,1)}, f32[1024,102...) custom-call(s32[2]{0:T(128)S(1)} %get-tuple-element.334.info_ref, ...), custom_call_target="tpu_custom_call" | custom-call | flops 32614907904 | bytes 50331648 | tf_op jit(solution)/shard_map/forward/pallas_call | solution.py:928
  109.6 6.9 %collective-permute-done.refs_2_ = f32[2,2048,256]{2,1,0:T(8,128)S(1)} collective-permute-done((f32[2,2048,256]{2,1,0:T(8,128)}, f32[2,2048,256]{2,1,0:T(8,128)S(1)}, u32[]{:S(2)}, u32[]{:S(2)}) %collective-permute-start) | collective-permute-done | bytes 4194336 | tf_op jit(solution)/shard_map/ppermute | solution.py:1041
  116.6 2.2 copy-done.11
  120.0 2.3 collective-permute-start.2
  123.5 1.6 collective-permute-start.1
  127.4 33.0 %backward.1 = (f32[4,1024,128]{2,1,0:T(8,128)}, f32[4,1024,128]{2,1,0:T(8,128)}, f32[8,128]{1,0:T(8,128)S(1)}, f32[4,1,128]{2,1,0:T(1,128)S(1)}, f32[2,1088,256]{2,1,0:T(8,128)}, /*index=5*/f32[2,1088,256]{2,1,0:T(8,128)}) custom-call(s32[2]{0:T(128)S(1)} %pad_add_fusion.2.refs_0_, f32[4,1024,128]{2,1,0:T(8,128)} %copy-done, f32[4,1024,128]{2,1,0:T(8,128)} %copy-done.47, ...), custom_call_target="tpu_custom_call" | custom-call | flops 26575110144 | bytes 41943040 | tf_op jit(solution)/shard_map/backward/pallas_call | solution.py:48
  164.9 2.8 back_ends.1
  167.7 5.4 %all-gather.1 = f32[16,16,128]{2,1,0:T(8,128)S(1)} all-gather(f32[4,16,128]{2,1,0:T(8,128)S(1)} %get-tuple-element.213), channel_id=3, replica_groups=mesh['seq'=8,'ch'=4] {'ch'}, dimensions={0}, use_global_device_ids=true | all-gather | bytes 163840 | tf_op jit(solution)/shard_map/all_gather | solution.py:1492
  174.7 1.6 collective-permute-start.9
  182.0 1.6 copy-done.14
  183.6 1.6 copy-done.16
  185.3 1.7 collective-permute-start.8
  188.5 1.8 halve.23
  190.3 1.7 collective-permute-start.6
  192.0 4.0 %back.4 = (f32[1,1024,128]{2,1,0:T(8,128)S(1)}, f32[1,16,128]{2,1,0:T(8,128)S(1)}, f32[1,16,128]{2,1,0:T(8,128)S(1)}) custom-call(s32[1]{0:T(128)} %bitcast.6.place_ref.refs_0_, f32[4,1024,128]{2,1,0:T(8,128)S(1)} %copy-done.3, f32[4,128,128]{2,1,0:T(8,128)S(1)} %get-tuple-element.212.refs_2_, f32[4,4,16,128]{3,2,1,0:T(8,128)S(1)} %bitcast.99, ...), custom_call_target="tpu_custom_call" | custom-call | flops 20971520 | bytes 1572864 | tf_op jit(solution)/shard_map/back/pallas_call | solution.py:48
  196.8 3.8 %back.5 = (f32[1,1024,128]{2,1,0:T(8,128)S(1)}, f32[1,16,128]{2,1,0:T(8,128)S(1)}, f32[1,16,128]{2,1,0:T(8,128)S(1)}) custom-call(s32[1]{0:T(128)} %bitcast.6.place_ref.refs_0_, f32[4,1024,128]{2,1,0:T(8,128)S(1)} %copy-done.3, f32[4,128,128]{2,1,0:T(8,128)S(1)} %get-tuple-element.212.refs_2_, f32[4,4,16,128]{3,2,1,0:T(8,128)S(1)} %bitcast.100, ...), custom_call_target="tpu_custom_call" | custom-call | flops 20971520 | bytes 1572864 | tf_op jit(solution)/shard_map/back/pallas_call | solution.py:48
  200.7 2.0 halve.24
  206.9 2.7 collective-permute-start.11
  215.1 3.8 %back.6 = (f32[1,1024,128]{2,1,0:T(8,128)S(1)}, f32[1,16,128]{2,1,0:T(8,128)S(1)}, f32[1,16,128]{2,1,0:T(8,128)S(1)}) custom-call(s32[1]{0:T(128)} %bitcast.6.place_ref.refs_0_, f32[4,1024,128]{2,1,0:T(8,128)S(1)} %copy-done.4, f32[4,128,128]{2,1,0:T(8,128)S(1)} %get-tuple-element.212.refs_2_, f32[4,4,16,128]{3,2,1,0:T(8,128)S(1)} %bitcast.101, ...), custom_call_target="tpu_custom_call" | custom-call | flops 20971520 | bytes 1572864 | tf_op jit(solution)/shard_map/back/pallas_call | solution.py:48
  220.4 1.7 collective-permute-start.14
  222.1 2.7 collective-permute-start.18
  225.2 3.8 %back.7 = (f32[1,1024,128]{2,1,0:T(8,128)S(1)}, f32[1,16,128]{2,1,0:T(8,128)S(1)}, f32[1,16,128]{2,1,0:T(8,128)S(1)}) custom-call(s32[1]{0:T(128)} %bitcast.6.place_ref.refs_0_, f32[4,1024,128]{2,1,0:T(8,128)S(1)} %copy-done.5, f32[4,128,128]{2,1,0:T(8,128)S(1)} %get-tuple-element.212.refs_2_, f32[4,4,16,128]{3,2,1,0:T(8,128)S(1)} %bitcast.102, ...), custom_call_target="tpu_custom_call" | custom-call | flops 20971520 | bytes 1572864 | tf_op jit(solution)/shard_map/back/pallas_call | solution.py:48
  229.2 2.0 unnorm.1
  234.4 1.6 collective-permute-start.21
  236.0 2.6 collective-permute-start.16
  238.6 2.8 collective-permute-done.16.refs_1_
  242.0 2.6 collective-permute-start.19
  245.1 7.0 %collective-permute-done.20.refs_1_ = f32[64,256]{1,0:T(8,128)S(1)} collective-permute-done((f32[64,256]{1,0:T(8,128)S(1)}, f32[64,256]{1,0:T(8,128)S(1)}, u32[]{:S(2)}, u32[]{:S(2)}) %collective-permute-start.20) | collective-permute-done | bytes 65568 | tf_op jit(solution)/shard_map/ppermute | solution.py:1041
  252.2 1.9 collective-permute-start.27
  254.3 5.3 %collective-permute-done.24.refs_1_ = f32[64,256]{1,0:T(8,128)S(1)} collective-permute-done((f32[64,256]{1,0:T(8,128)S(1)}, f32[64,256]{1,0:T(8,128)S(1)}, u32[]{:S(2)}, u32[]{:S(2)}) %collective-permute-start.24) | collective-permute-done | bytes 65568 | tf_op jit(solution)/shard_map/ppermute | solution.py:1041
  259.6 3.2 collective-permute-start.28
  262.9 2.8 collective-permute-done.28.refs_2_
  268.2 6.6 %collective-permute-done.26.refs_3_ = f32[512,256]{1,0:T(8,128)S(1)} collective-permute-done((f32[512,256]{1,0:T(8,128)S(1)}, f32[512,256]{1,0:T(8,128)S(1)}, u32[]{:S(2)}, u32[]{:S(2)}) %collective-permute-start.26) | collective-permute-done | bytes 524320 | tf_op jit(solution)/shard_map/ppermute | solution.py:1041
  276.0 1.8 collective-permute-start.33
  279.3 11.6 %collective-permute-done.33.refs_7_ = f32[512,256]{1,0:T(8,128)S(1)} collective-permute-done((f32[512,256]{1,0:T(8,128)S(1)}, f32[512,256]{1,0:T(8,128)S(1)}, u32[]{:S(2)}, u32[]{:S(2)}) %collective-permute-start.33) | collective-permute-done | bytes 524320 | tf_op jit(solution)/shard_map/ppermute | solution.py:1041
  291.7 3.6 %all-to-all-start.1 = ((f32[4,1024,128]{2,1,0:T(8,128)}), f32[4,1024,128]{2,1,0:T(8,128)S(1)}, u32[]{:S(2)}, u32[]{:S(2)}) async-start(f32[4,1024,128]{2,1,0:T(8,128)} %copy-done.22), calls=%async_computation.1 | async-start | bytes 4194304 | tf_op jit(solution)/shard_map/all_to_all | solution.py:1518
  295.4 8.0 %collective-permute-done.29.refs_3_.part_b = f32[656,256]{1,0:T(8,128)S(1)} collective-permute-done((f32[656,256]{1,0:T(8,128)S(1)}, f32[656,256]{1,0:T(8,128)S(1)}, u32[]{:S(2)}, u32[]{:S(2)}) %collective-permute-start.29) | collective-permute-done | bytes 671776 | tf_op jit(solution)/shard_map/ppermute | solution.py:1041
  304.5 1.8 collective-permute-done.31.refs_5_.part_d
  307.4 1.8 small_grads.1
  310.2 6.5 %finish_one.1 = (f32[512,1024]{1,0:T(8,128)}, f32[1024,512]{1,0:T(8,128)}, f32[1024,512]{1,0:T(8,128)}, f32[512,2176]{1,0:T(8,128)}, f32[8,128]{1,0:T(8,128)S(1)}) custom-call(s32[4]{0:T(128)S(1)} %add_add_fusion.1.refs_0_.refs_1_, s32[4]{0:T(128)S(1)} %add_add_fusion.refs_1_.refs_0_, f32[1024,256]{1,0:T(8,128)} %get-tuple-element.306.refs_2_, ...), custom_call_target="tpu_custom_call" | custom-call | bytes 1024 | tf_op jit(solution)/shard_map/finish_one/pallas_call | solution.py:48
  316.8 3.6 %finish_rest.1 = (f32[512,1024]{1,0:T(8,128)}, f32[512,2176]{1,0:T(8,128)}, f32[8,128]{1,0:T(8,128)S(1)}) custom-call(s32[4]{0:T(128)S(1)} %add_add_fusion.refs_1_.refs_0_, s32[4]{0:T(128)S(1)} %add_add_fusion.1.refs_0_.refs_1_, f32[656,256]{1,0:T(8,128)S(1)} %get-tuple-element.302.refs_2_.part_a, ...), custom_call_target="tpu_custom_call", output_to_operand_aliasing={{1}: (10, {})} | custom-call | bytes 1024 | tf_op jit(solution)/shard_map/finish_rest/pallas_call | solution.py:48
  320.4 2.9 all-to-all-done.1.refs_0_
  (247 shorter events, 68.8 us)
Async XLA Ops:
  0.7 30.1 %all-to-all-start = ((f32[4,1024,128]{2,1,0:T(8,128)}), f32[4,1024,128]{2,1,0:T(8,128)S(1)}, u32[]{:S(2)}, u32[]{:S(2)}) async-start(f32[4,1024,128]{2,1,0:T(8,128)} %bitcast.141), calls=%async_computation | async-start | bytes 4194304 | tf_op jit(solution)/shard_map/all_to_all | solution.py:1380
  12.8 19.3 %copy-start.43 = (f32[512]{0:T(512)S(1)}, f32[512]{0:T(512)}, u32[]{:S(2)}) copy-start(f32[512]{0:T(512)} %param.20) | copy-start | bytes 6148
  33.7 16.3 %copy-start.59 = (f32[512]{0:T(512)S(1)}, f32[512]{0:T(512)}, u32[]{:S(2)}) copy-start(f32[512]{0:T(512)} %param.31) | copy-start | bytes 6148
  109.2 7.4 %collective-permute-start = (f32[2,2048,256]{2,1,0:T(8,128)}, f32[2,2048,256]{2,1,0:T(8,128)S(1)}, u32[]{:S(2)}, u32[]{:S(2)}) collective-permute-start(f32[2,2048,256]{2,1,0:T(8,128)} %get-tuple-element.198), channel_id=1, source_target_pairs={{0,1},{1,0},{2,3},{3,2},{4,5},{5,4},{6,7},{7,6},{8,9},{9,8},{10,11... | collective-permute-start | bytes 12582920 | tf_op jit(solution)/shard_map/ppermute | solution.py:1041
  120.0 40.4 %collective-permute-start.2 = (f32[1024,256]{1,0:T(8,128)}, f32[1024,256]{1,0:T(8,128)S(1)}, u32[]{:S(2)}, u32[]{:S(2)}) collective-permute-start(f32[1024,256]{1,0:T(8,128)} %get-tuple-element.207), channel_id=1, source_target_pairs={{0,4},{4,0},{8,12},{12,8},{16,20},{20,16},{24,28},{28,24},{1,5},{5... | collective-permute-start | bytes 3145736 | tf_op jit(solution)/shard_map/ppermute | solution.py:1041
  123.5 38.6 %collective-permute-start.1 = (f32[1024,256]{1,0:T(8,128)}, f32[1024,256]{1,0:T(8,128)S(1)}, u32[]{:S(2)}, u32[]{:S(2)}) collective-permute-start(f32[1024,256]{1,0:T(8,128)} %get-tuple-element.205), channel_id=1, source_target_pairs={{0,8},{4,12},{8,0},{12,4},{16,24},{20,28},{24,16},{28,20},{1,9},{5... | collective-permute-start | bytes 3145736 | tf_op jit(solution)/shard_map/ppermute | solution.py:1041
  163.1 10.1 %collective-permute-start.4 = (f32[2,1088,256]{2,1,0:T(8,128)}, f32[2,1088,256]{2,1,0:T(8,128)S(1)}, u32[]{:S(2)}, u32[]{:S(2)}) collective-permute-start(f32[2,1088,256]{2,1,0:T(8,128)} %get-tuple-element.219), channel_id=1, source_target_pairs={{0,1},{1,0},{2,3},{3,2},{4,5},{5,4},{6,7},{7,6},{8,9},{9,8},{10,11... | collective-permute-start | bytes 6684680 | tf_op jit(solution)/shard_map/ppermute | solution.py:1041
  163.1 14.5 %collective-permute-start.5 = (f32[512,256]{1,0:T(8,128)}, f32[512,256]{1,0:T(8,128)S(1)}, u32[]{:S(2)}, u32[]{:S(2)}) collective-permute-start(f32[512,256]{1,0:T(8,128)} %get-tuple-element.221), channel_id=1, source_target_pairs={{0,8},{4,12},{8,0},{12,4},{16,24},{20,28},{24,16},{28,20},{1,9},{5... | collective-permute-start | bytes 1572872 | tf_op jit(solution)/shard_map/ppermute | solution.py:1041
  163.5 23.9 %collective-permute-start.3 = (f32[512,256]{1,0:T(8,128)}, f32[512,256]{1,0:T(8,128)}, u32[]{:S(2)}, u32[]{:S(2)}) collective-permute-start(f32[512,256]{1,0:T(8,128)} %get-tuple-element.217), channel_id=1, source_target_pairs={{0,4},{4,0},{8,12},{12,8},{16,20},{20,16},{24,28},{28,24},{1,5},{5... | collective-permute-start | bytes 1572872 | tf_op jit(solution)/shard_map/ppermute | solution.py:1041
  174.7 25.9 %collective-permute-start.9 = (f32[576,256]{1,0:T(8,128)}, f32[576,256]{1,0:T(8,128)}, u32[]{:S(2)}, u32[]{:S(2)}) collective-permute-start(f32[576,256]{1,0:T(8,128)} %get-tuple-element.236), channel_id=1, source_target_pairs={{0,8},{4,12},{8,0},{12,4},{16,24},{20,28},{24,16},{28,20},{1,9},{5... | collective-permute-start | bytes 1769480 | tf_op jit(solution)/shard_map/ppermute | solution.py:1041
  185.3 18.4 %collective-permute-start.8 = (f32[512,256]{1,0:T(8,128)S(1)}, f32[512,256]{1,0:T(8,128)S(1)}, u32[]{:S(2)}, u32[]{:S(2)}) collective-permute-start(f32[512,256]{1,0:T(8,128)S(1)} %get-tuple-element.234), channel_id=1, source_target_pairs={{0,4},{4,0},{8,12},{12,8},{16,20},{20,16},{24,28},{28,24},{1,5},{5... | collective-permute-start | bytes 1572872 | tf_op jit(solution)/shard_map/ppermute | solution.py:1041
  187.1 17.9 %collective-permute-start.7 = (f32[256,256]{1,0:T(8,128)}, f32[256,256]{1,0:T(8,128)}, u32[]{:S(2)}, u32[]{:S(2)}) collective-permute-start(f32[256,256]{1,0:T(8,128)} %get-tuple-element.232), channel_id=1, source_target_pairs={{0,2},{1,3},{2,0},{3,1},{4,6},{5,7},{6,4},{7,5},{8,10},{9,11},{10,... | collective-permute-start | bytes 786440 | tf_op jit(solution)/shard_map/ppermute | solution.py:1041
  190.3 19.3 %collective-permute-start.6 = (f32[256,256]{1,0:T(8,128)}, f32[256,256]{1,0:T(8,128)}, u32[]{:S(2)}, u32[]{:S(2)}) collective-permute-start(f32[256,256]{1,0:T(8,128)} %get-tuple-element.230), channel_id=1, source_target_pairs={{0,2},{1,3},{2,0},{3,1},{4,6},{5,7},{6,4},{7,5},{8,10},{9,11},{10,... | collective-permute-start | bytes 786440 | tf_op jit(solution)/shard_map/ppermute | solution.py:1041
  203.4 15.5 %collective-permute-start.13 = (f32[288,256]{1,0:T(8,128)}, f32[288,256]{1,0:T(8,128)S(1)}, u32[]{:S(2)}, u32[]{:S(2)}) collective-permute-start(f32[288,256]{1,0:T(8,128)} %get-tuple-element.250), channel_id=1, source_target_pairs={{0,4},{4,0},{8,12},{12,8},{16,20},{20,16},{24,28},{28,24},{1,5},{5... | collective-permute-start | bytes 884744 | tf_op jit(solution)/shard_map/ppermute | solution.py:1041
  204.5 14.9 %collective-permute-start.12 = (f32[256,256]{1,0:T(8,128)}, f32[256,256]{1,0:T(8,128)}, u32[]{:S(2)}, u32[]{:S(2)}) collective-permute-start(f32[256,256]{1,0:T(8,128)} %get-tuple-element.248), channel_id=1, source_target_pairs={{0,8},{4,12},{8,0},{12,4},{16,24},{20,28},{24,16},{28,20},{1,9},{5... | collective-permute-start | bytes 786440 | tf_op jit(solution)/shard_map/ppermute | solution.py:1041
  206.9 15.2 %collective-permute-start.11 = (f32[128,256]{1,0:T(8,128)S(1)}, f32[128,256]{1,0:T(8,128)S(1)}, u32[]{:S(2)}, u32[]{:S(2)}) collective-permute-start(f32[128,256]{1,0:T(8,128)S(1)} %get-tuple-element.246), channel_id=1, source_target_pairs={{0,16},{4,20},{8,24},{12,28},{16,0},{20,4},{24,8},{28,12},{1,17},{... | collective-permute-start | bytes 393224 | tf_op jit(solution)/shard_map/ppermute | solution.py:1041
  211.5 13.3 %collective-permute-start.10 = (f32[128,256]{1,0:T(8,128)S(1)}, f32[128,256]{1,0:T(8,128)S(1)}, u32[]{:S(2)}, u32[]{:S(2)}) collective-permute-start(f32[128,256]{1,0:T(8,128)S(1)} %get-tuple-element.244), channel_id=1, source_target_pairs={{0,16},{4,20},{8,24},{12,28},{16,0},{20,4},{24,8},{28,12},{1,17},{... | collective-permute-start | bytes 393224 | tf_op jit(solution)/shard_map/ppermute | solution.py:1041
  219.0 10.1 %collective-permute-start.15 = (f32[144,256]{1,0:T(8,128)S(1)}, f32[144,256]{1,0:T(8,128)S(1)}, u32[]{:S(2)}, u32[]{:S(2)}) collective-permute-start(f32[144,256]{1,0:T(8,128)S(1)} %get-tuple-element.267), channel_id=1, source_target_pairs={{0,2},{1,3},{2,0},{3,1},{4,6},{5,7},{6,4},{7,5},{8,10},{9,11},{10,... | collective-permute-start | bytes 442376 | tf_op jit(solution)/shard_map/ppermute | solution.py:1041
  220.4 8.7 %collective-permute-start.14 = (f32[128,256]{1,0:T(8,128)S(1)}, f32[128,256]{1,0:T(8,128)S(1)}, u32[]{:S(2)}, u32[]{:S(2)}) collective-permute-start(f32[128,256]{1,0:T(8,128)S(1)} %get-tuple-element.265), channel_id=1, source_target_pairs={{0,2},{1,3},{2,0},{3,1},{4,6},{5,7},{6,4},{7,5},{8,10},{9,11},{10,... | collective-permute-start | bytes 393224 | tf_op jit(solution)/shard_map/ppermute | solution.py:1041
  222.1 10.8 %collective-permute-start.18 = (f32[128,256]{1,0:T(8,128)S(1)}, f32[128,256]{1,0:T(8,128)S(1)}, u32[]{:S(2)}, u32[]{:S(2)}) collective-permute-start(f32[128,256]{1,0:T(8,128)S(1)} %get-tuple-element.276.refs_0_), channel_id=1, source_target_pairs={{0,16},{4,20},{8,24},{12,28},{16,0},{20,4},{24,8},{28,12},{1,17},{... | collective-permute-start | bytes 393224 | tf_op jit(solution)/shard_map/ppermute | solution.py:1041
  224.8 9.5 %collective-permute-start.17 = (f32[128,256]{1,0:T(8,128)S(1)}, f32[128,256]{1,0:T(8,128)S(1)}, u32[]{:S(2)}, u32[]{:S(2)}) collective-permute-start(f32[128,256]{1,0:T(8,128)S(1)} %get-tuple-element.275.refs_0_), channel_id=1, source_target_pairs={{0,16},{4,20},{8,24},{12,28},{16,0},{20,4},{24,8},{28,12},{1,17},{... | collective-permute-start | bytes 393224 | tf_op jit(solution)/shard_map/ppermute | solution.py:1041
  232.9 12.0 %collective-permute-start.22 = (f32[256,256]{1,0:T(8,128)S(1)}, f32[256,256]{1,0:T(8,128)S(1)}, u32[]{:S(2)}, u32[]{:S(2)}) collective-permute-start(f32[256,256]{1,0:T(8,128)S(1)} %get-tuple-element.285), channel_id=1, source_target_pairs={{0,8},{4,12},{8,0},{12,4},{16,24},{20,28},{24,16},{28,20},{1,9},{5... | collective-permute-start | bytes 786440 | tf_op jit(solution)/shard_map/ppermute | solution.py:1041
  234.4 10.6 %collective-permute-start.21 = (f32[256,256]{1,0:T(8,128)S(1)}, f32[256,256]{1,0:T(8,128)S(1)}, u32[]{:S(2)}, u32[]{:S(2)}) collective-permute-start(f32[256,256]{1,0:T(8,128)S(1)} %get-tuple-element.284), channel_id=1, source_target_pairs={{0,4},{4,0},{8,12},{12,8},{16,20},{20,16},{24,28},{28,24},{1,5},{5... | collective-permute-start | bytes 786440 | tf_op jit(solution)/shard_map/ppermute | solution.py:1041
  236.0 5.4 %collective-permute-start.16 = (f32[72,256]{1,0:T(8,128)S(1)}, f32[72,256]{1,0:T(8,128)S(1)}, u32[]{:S(2)}, u32[]{:S(2)}) collective-permute-start(f32[72,256]{1,0:T(8,128)S(1)} %get-tuple-element.274), channel_id=1, source_target_pairs={{0,16},{4,20},{8,24},{12,28},{16,0},{20,4},{24,8},{28,12},{1,17},{... | collective-permute-start | bytes 221192 | tf_op jit(solution)/shard_map/ppermute | solution.py:1041
  242.0 10.1 %collective-permute-start.19 = (f32[152,256]{1,0:T(8,128)S(1)}, f32[152,256]{1,0:T(8,128)S(1)}, u32[]{:S(2)}, u32[]{:S(2)}) collective-permute-start(f32[152,256]{1,0:T(8,128)S(1)} %get-tuple-element.281.refs_2_), channel_id=1, source_target_pairs={{0,16},{4,20},{8,24},{12,28},{16,0},{20,4},{24,8},{28,12},{1,17},{... | collective-permute-start | bytes 466952 | tf_op jit(solution)/shard_map/ppermute | solution.py:1041
  244.6 7.5 %collective-permute-start.20 = (f32[64,256]{1,0:T(8,128)S(1)}, f32[64,256]{1,0:T(8,128)S(1)}, u32[]{:S(2)}, u32[]{:S(2)}) collective-permute-start(f32[64,256]{1,0:T(8,128)S(1)} %get-tuple-element.283), channel_id=1, source_target_pairs={{0,16},{4,20},{8,24},{12,28},{16,0},{20,4},{24,8},{28,12},{1,17},{... | collective-permute-start | bytes 196616 | tf_op jit(solution)/shard_map/ppermute | solution.py:1041
  252.1 10.7 %collective-permute-start.23 = (f32[224,256]{1,0:T(8,128)S(1)}, f32[224,256]{1,0:T(8,128)S(1)}, u32[]{:S(2)}, u32[]{:S(2)}) collective-permute-start(f32[224,256]{1,0:T(8,128)S(1)} %get-tuple-element.290.refs_3_), channel_id=1, source_target_pairs={{0,4},{4,0},{8,12},{12,8},{16,20},{20,16},{24,28},{28,24},{1,5},{5... | collective-permute-start | bytes 688136 | tf_op jit(solution)/shard_map/ppermute | solution.py:1041
  252.2 14.9 %collective-permute-start.27 = (f32[512,256]{1,0:T(8,128)S(1)}, f32[512,256]{1,0:T(8,128)S(1)}, u32[]{:S(2)}, u32[]{:S(2)}) collective-permute-start(f32[512,256]{1,0:T(8,128)S(1)} %get-tuple-element.296), channel_id=1, source_target_pairs={{0,2},{1,3},{2,0},{3,1},{4,6},{5,7},{6,4},{7,5},{8,10},{9,11},{10,... | collective-permute-start | bytes 1572872 | tf_op jit(solution)/shard_map/ppermute | solution.py:1041
  254.1 20.6 %collective-permute-start.26 = (f32[512,256]{1,0:T(8,128)S(1)}, f32[512,256]{1,0:T(8,128)S(1)}, u32[]{:S(2)}, u32[]{:S(2)}) collective-permute-start(f32[512,256]{1,0:T(8,128)S(1)} %get-tuple-element.295), channel_id=1, source_target_pairs={{0,2},{1,3},{2,0},{3,1},{4,6},{5,7},{6,4},{7,5},{8,10},{9,11},{10,... | collective-permute-start | bytes 1572872 | tf_op jit(solution)/shard_map/ppermute | solution.py:1041
  254.3 5.3 %collective-permute-start.24 = (f32[64,256]{1,0:T(8,128)S(1)}, f32[64,256]{1,0:T(8,128)S(1)}, u32[]{:S(2)}, u32[]{:S(2)}) collective-permute-start(f32[64,256]{1,0:T(8,128)S(1)} %get-tuple-element.291.refs_0_), channel_id=1, source_target_pairs={{0,16},{4,20},{8,24},{12,28},{16,0},{20,4},{24,8},{28,12},{1,17},{... | collective-permute-start | bytes 196616 | tf_op jit(solution)/shard_map/ppermute | solution.py:1041
  259.6 6.2 %collective-permute-start.28 = (f32[128,256]{1,0:T(8,128)S(1)}, f32[128,256]{1,0:T(8,128)S(1)}, u32[]{:S(2)}, u32[]{:S(2)}) collective-permute-start(f32[128,256]{1,0:T(8,128)S(1)} %get-tuple-element.297), channel_id=1, source_target_pairs={{0,8},{4,12},{8,0},{12,4},{16,24},{20,28},{24,16},{28,20},{1,9},{5... | collective-permute-start | bytes 393224 | tf_op jit(solution)/shard_map/ppermute | solution.py:1041
  262.8 13.0 %collective-permute-start.25 = (f32[368,256]{1,0:T(8,128)S(1)}, f32[368,256]{1,0:T(8,128)S(1)}, u32[]{:S(2)}, u32[]{:S(2)}) collective-permute-start(f32[368,256]{1,0:T(8,128)S(1)} %get-tuple-element.294.refs_4_), channel_id=1, source_target_pairs={{0,8},{4,12},{8,0},{12,4},{16,24},{20,28},{24,16},{28,20},{1,9},{5... | collective-permute-start | bytes 1130504 | tf_op jit(solution)/shard_map/ppermute | solution.py:1041
  265.8 10.1 %collective-permute-start.32 = (f32[256,256]{1,0:T(8,128)S(1)}, f32[256,256]{1,0:T(8,128)S(1)}, u32[]{:S(2)}, u32[]{:S(2)}) collective-permute-start(f32[256,256]{1,0:T(8,128)S(1)} %get-tuple-element.303), channel_id=1, source_target_pairs={{0,4},{4,0},{8,12},{12,8},{16,20},{20,16},{24,28},{28,24},{1,5},{5... | collective-permute-start | bytes 786440 | tf_op jit(solution)/shard_map/ppermute | solution.py:1041
  276.0 14.9 %collective-permute-start.33 = (f32[512,256]{1,0:T(8,128)S(1)}, f32[512,256]{1,0:T(8,128)S(1)}, u32[]{:S(2)}, u32[]{:S(2)}) collective-permute-start(f32[512,256]{1,0:T(8,128)S(1)} %get-tuple-element.305.refs_6_), channel_id=1, source_target_pairs={{0,2},{1,3},{2,0},{3,1},{4,6},{5,7},{6,4},{7,5},{8,10},{9,11},{10,... | collective-permute-start | bytes 1572872 | tf_op jit(solution)/shard_map/ppermute | solution.py:1041
  277.8 26.1 %collective-permute-start.39 = (f32[1024,256]{1,0:T(8,128)}, f32[1024,256]{1,0:T(8,128)}, u32[]{:S(2)}, u32[]{:S(2)}) collective-permute-start(f32[1024,256]{1,0:T(8,128)} %get-tuple-element.307.refs_6_), channel_id=1, source_target_pairs={{0,8},{4,12},{8,0},{12,4},{16,24},{20,28},{24,16},{28,20},{1,9},{5... | collective-permute-start | bytes 3145736 | tf_op jit(solution)/shard_map/ppermute | solution.py:1041
  278.7 25.3 %collective-permute-start.36 = (f32[1024,256]{1,0:T(8,128)}, f32[1024,256]{1,0:T(8,128)}, u32[]{:S(2)}, u32[]{:S(2)}) collective-permute-start(f32[1024,256]{1,0:T(8,128)} %get-tuple-element.306.refs_2_), channel_id=1, source_target_pairs={{0,4},{4,0},{8,12},{12,8},{16,20},{20,16},{24,28},{28,24},{1,5},{5... | collective-permute-start | bytes 3145736 | tf_op jit(solution)/shard_map/ppermute | solution.py:1041
  279.0 27.5 %copy-start.69 = (f32[512,16]{0,1:T(8,128)S(1)}, f32[512,16]{0,1:T(8,128)}, u32[]{:S(2)}) copy-start(f32[512,16]{0,1:T(8,128)} %param.23) | copy-start | bytes 98308
  279.0 27.5 %copy-start.70 = (f32[2,4,8,128]{3,2,1,0:T(8,128)S(1)}, f32[2,4,8,128]{3,2,1,0:T(8,128)}, u32[]{:S(2)}) copy-start(f32[2,4,8,128]{3,2,1,0:T(8,128)} %get-tuple-element.326) | copy-start | bytes 98308
  279.0 24.3 %collective-permute-start.29 = (f32[656,256]{1,0:T(8,128)S(1)}, f32[656,256]{1,0:T(8,128)S(1)}, u32[]{:S(2)}, u32[]{:S(2)}) collective-permute-start(f32[656,256]{1,0:T(8,128)S(1)} %get-tuple-element.302.refs_2_.part_a), channel_id=1, source_target_pairs={{0,2},{1,3},{2,0},{3,1},{4,6},{5,7},{6,4},{7,5},{8,10},{9,11},{10,... | collective-permute-start | bytes 2015240 | tf_op jit(solution)/shard_map/ppermute | solution.py:1041
  279.3 24.0 %collective-permute-start.30 = (f32[656,256]{1,0:T(8,128)S(1)}, f32[656,256]{1,0:T(8,128)}, u32[]{:S(2)}, u32[]{:S(2)}) collective-permute-start(f32[656,256]{1,0:T(8,128)S(1)} %get-tuple-element.302.refs_2_.part_a), channel_id=1, source_target_pairs={{0,1},{1,0},{2,3},{3,2},{4,5},{5,4},{6,7},{7,6},{8,9},{9,8},{10,11... | collective-permute-start | bytes 2015240 | tf_op jit(solution)/shard_map/ppermute | solution.py:1041
  291.7 12.7 %collective-permute-start.40 = (f32[1024,256]{1,0:T(8,128)}, f32[1024,256]{1,0:T(8,128)}, u32[]{:S(2)}, u32[]{:S(2)}) collective-permute-start(f32[1024,256]{1,0:T(8,128)} %get-tuple-element.307.refs_6_), channel_id=1, source_target_pairs={{0,1},{1,0},{2,3},{3,2},{4,5},{5,4},{6,7},{7,6},{8,9},{9,8},{10,11... | collective-permute-start | bytes 3145736 | tf_op jit(solution)/shard_map/ppermute | solution.py:1041
  291.7 31.5 %all-to-all-start.1 = ((f32[4,1024,128]{2,1,0:T(8,128)}), f32[4,1024,128]{2,1,0:T(8,128)S(1)}, u32[]{:S(2)}, u32[]{:S(2)}) async-start(f32[4,1024,128]{2,1,0:T(8,128)} %copy-done.22), calls=%async_computation.1 | async-start | bytes 4194304 | tf_op jit(solution)/shard_map/all_to_all | solution.py:1518
  303.4 3.0 collective-permute-start.31
  303.4 5.8 %collective-permute-start.37 = (f32[1024,256]{1,0:T(8,128)}, f32[1024,256]{1,0:T(8,128)S(1)}, u32[]{:S(2)}, u32[]{:S(2)}) collective-permute-start(f32[1024,256]{1,0:T(8,128)} %get-tuple-element.306.refs_2_), channel_id=1, source_target_pairs={{0,1},{1,0},{2,3},{3,2},{4,5},{5,4},{6,7},{7,6},{8,9},{9,8},{10,11... | collective-permute-start | bytes 3145736 | tf_op jit(solution)/shard_map/ppermute | solution.py:1041
  303.9 5.3 %collective-permute-start.41 = (f32[1024,256]{1,0:T(8,128)}, f32[1024,256]{1,0:T(8,128)S(1)}, u32[]{:S(2)}, u32[]{:S(2)}) collective-permute-start(f32[1024,256]{1,0:T(8,128)} %collective-permute-done.39.refs_7_), channel_id=1, source_target_pairs={{0,1},{1,0},{2,3},{3,2},{4,5},{5,4},{6,7},{7,6},{8,9},{9,8},{10,11... | collective-permute-start | bytes 3145736 | tf_op jit(solution)/shard_map/ppermute | solution.py:1041
  303.9 6.2 %collective-permute-start.38 = (f32[1024,256]{1,0:T(8,128)}, f32[1024,256]{1,0:T(8,128)S(1)}, u32[]{:S(2)}, u32[]{:S(2)}) collective-permute-start(f32[1024,256]{1,0:T(8,128)} %collective-permute-done.36.refs_3_), channel_id=1, source_target_pairs={{0,1},{1,0},{2,3},{3,2},{4,5},{5,4},{6,7},{7,6},{8,9},{9,8},{10,11... | collective-permute-start | bytes 3145736 | tf_op jit(solution)/shard_map/ppermute | solution.py:1041
  304.5 12.3 %collective-permute-start.34 = (f32[512,256]{1,0:T(8,128)}, f32[512,256]{1,0:T(8,128)S(1)}, u32[]{:S(2)}, u32[]{:S(2)}) collective-permute-start(f32[512,256]{1,0:T(8,128)} %copy-done.27), channel_id=1, source_target_pairs={{0,1},{1,0},{2,3},{3,2},{4,5},{5,4},{6,7},{7,6},{8,9},{9,8},{10,11... | collective-permute-start | bytes 1572872 | tf_op jit(solution)/shard_map/ppermute | solution.py:1041
  306.4 10.4 %collective-permute-start.35 = (f32[512,256]{1,0:T(8,128)}, f32[512,256]{1,0:T(8,128)S(1)}, u32[]{:S(2)}, u32[]{:S(2)}) collective-permute-start(f32[512,256]{1,0:T(8,128)} %copy-done.29), channel_id=1, source_target_pairs={{0,1},{1,0},{2,3},{3,2},{4,5},{5,4},{6,7},{7,6},{8,9},{9,8},{10,11... | collective-permute-start | bytes 1572872 | tf_op jit(solution)/shard_map/ppermute | solution.py:1041
  (69 other events, 316.0 us)

commit v2 on v1

--- a/solution.py
+++ b/solution.py
@@ -636,8 +636,10 @@
     grad_u_ref,
     grad_h_ref,
     gain_grad_ref,
-    send_ref,
-    keep_ref,
+    send_a,
+    keep_a,
+    send_b,
+    keep_b,
     upd,
     hpre,
     gr_h,
@@ -661,8 +663,8 @@
     units = wu_h.shape[1]
     base_row, length = info_ref[0] + tile * rows, info_ref[1]
     last = tile == pl.num_programs(0) - 1
-    out_a = HandOut(place_ref[0], acc_a, send_ref, keep_ref, 0, sems_a, last)
-    out_b = HandOut(place_ref[1], acc_b, send_ref, keep_ref, acc_a.shape[1], sems_b, last)
+    out_a = HandOut(place_ref[0], acc_a, send_a, keep_a, 0, sems_a, last)
+    out_b = HandOut(place_ref[1], acc_b, send_b, keep_b, 0, sems_b, last)
 
     @pl.when(first)
     def _():
@@ -947,6 +949,8 @@
             pl.BlockSpec((1, width), lambda i: (0, 0)),
             HBM,
             HBM,
+            HBM,
+            HBM,
         ],
         out_shape=[
             shape_of(rows, width),
@@ -964,7 +968,7 @@
             shape_of(rows, width),
             shape_of(1, width),
         ]
-        + [shape_of(2, sum(heights), QUARTER)] * 2,
+        + [shape_of(2, height, QUARTER) for height in heights for _ in range(2)],
         scratch_shapes=[
             pltpu.VMEM((TILE, width), F32),
             pltpu.VMEM((TILE, width), F32),
@@ -1065,7 +1069,7 @@
     ]
     back = [
         rest[::-1] + z + x + y,
-        rest[::-1] + y + x + z,
+        rest[::-1] + x + y + z,
         rest[::-1] + y + z + x,
         rest[::-1] + z + y + x,
     ]
@@ -1453,7 +1457,8 @@
         early_heights,
     )
     saved, ffn_gain_part, ffn_parts = forward_rest[:11], forward_rest[11], forward_rest[12:]
-    open_pieces((one, other), early_heights, *ffn_parts)
+    open_pieces((one,), early_heights[:1], *ffn_parts[:2])
+    open_pieces((other,), early_heights[1:], *ffn_parts[2:])
     t = run(ffn_gain_part, one, other)
     own_quarters = jnp.concatenate([two.own_quarter, three.own_quarter])
     before, omega_parts, qk_parts = (), [], []
@@ -1521,8 +1526,10 @@
     t = run(t, two, three)
     t = run(t, two, three)
     t = run(t, one, other, two, three)
-    while three.at < three.steps or one.at < one.steps or other.at < other.steps:
-        t = run(t, two, three, one, other)
+    while one.at < one.steps or other.at < other.steps:
+        t = run(t, one, other)
+    while three.at < three.steps or two.at < two.steps:
+        t = run(t, two, three)
     up_rows, quarter_rows = w_up.shape[0], w_down.shape[0] // 4
     reset_at = width + zwidth
     hidden_in_at = reset_at + w_value.shape[1]

time: 326 us -> 311 us (0.954)
  waiting for transfers between devices: 61 us -> 53.8 us
  local copies, waits for them, and re-layouts: 45.4 us -> 38.3 us
    unnamed x146 -> x126, local copies, waits for them, and re-layouts: 44.6 us -> 37.5 us
    ppermute x42 -> x43, waiting for transfers between devices: 55.7 us -> 48.9 us  [swap(): return lax.ppermute(value, axis, [(i, i ^ distance) for i in range(size)])]
    ppermute x42 -> x43, starting transfers between devices: 40.4 us -> 39.8 us  [swap(): return lax.ppermute(value, axis, [(i, i ^ distance) for i in range(size)])]
  transfers between devices with their start and end apart: 44 -> 45, of which waited for: 15 -> 16; matrix products, arithmetic and copies ran while one was open for 1% -> 1% of each run, Pallas kernels for 26% -> 27%
where the time goes in v2:
time: 311 us; the launch traced here: 308 us
  Pallas kernels  154 us (50%)
  waiting for transfers between devices  53.8 us (17%)
  starting transfers between devices  47.8 us (15%)
  local copies, waits for them, and re-layouts  38.3 us (12%)
  blocking collectives  10.9 us (4%)
    pallas_call x43, Pallas kernels, ordered_call(): return lambda *args: run(*args, *tokens)  80 us
    pallas_call x1, Pallas kernels, forward_call(): pl.pallas_call(forward_kernel, grid=(rows // TILE,), in_specs=[SMEM, SMEM...  57.4 us
    ppermute x43, waiting for transfers between devices, swap(): return lax.ppermute(value, axis, [(i, i ^ distance) for i in range(size)])  48.9 us
    ppermute x43, starting transfers between devices, swap(): return lax.ppermute(value, axis, [(i, i ^ distance) for i in range(size)])  39.8 us
    unnamed x126, local copies, waits for them, and re-layouts  37.5 us
  transfers between devices with their start and end apart: 45, of which 16 were waited for; matrix products, arithmetic and copies ran while one was open for 1% of the time, Pallas kernels for 27%

profile of v2, /device:TPU:0, one launch (start us, length us, event | category | flops | bytes accessed | tf_op | source)
XLA Modules:
  0.0 308.3 jit_solution(67457168528431862)
XLA Ops:
  0.7 4.4 %all-to-all-start = ((f32[4,1024,128]{2,1,0:T(8,128)}), f32[4,1024,128]{2,1,0:T(8,128)S(1)}, u32[]{:S(2)}, u32[]{:S(2)}) async-start(f32[4,1024,128]{2,1,0:T(8,128)} %bitcast.141), calls=%async_computation | async-start | bytes 4194304 | tf_op jit(solution)/shard_map/all_to_all | solution.py:1384
  8.0 1.6 copy-done.16
  9.6 1.6 copy-done.17
  11.2 1.6 copy-done.18
  12.8 5.8 %split_weights.1 = (bf16[512,1024]{1,0:T(8,128)(2,1)S(1)}, bf16[512,1024]{1,0:T(8,128)(2,1)S(1)}, bf16[512,2176]{1,0:T(8,128)(2,1)S(1)}, bf16[512,2176]{1,0:T(8,...) custom-call(f32[512,1024]{1,0:T(8,128)S(1)} %copy-done.15, ...), custom_call_target="tpu_custom_call" | custom-call | flops 12845056 | bytes 25690112 | tf_op jit(solution)/shard_map/split_weights/pallas_call | solution.py:101
  32.1 1.6 copy-done.9
  33.7 3.9 %norm.1 = (f32[4,1024,128]{2,1,0:T(8,128)S(1)}, f32[4,128,128]{2,1,0:T(8,128)S(1)}, f32[4,16,128]{2,1,0:T(8,128)S(1)}) custom-call(f32[4,1024,128]{2,1,0:T(8,128)S(1)} %copy-done.9, f32[4,1,128]{2,1,0:T(1,128)S(1)} %bitcast.135, f32[4,16,128]{2,1,0:T(8,128)S(1)} %bitcast.103, f32[4,16,128]{2,1,0:T(8,128)S(1)} %get-tuple-element.335.chunk_keep_ref.refs_2_.refs_9_), custom_call_target="tpu_custom_call" | custom-call | tf_op jit(solution)/shard_map/norm/pallas_call | solution.py:1406
  37.6 5.4 %all-gather = f32[16,16,128]{2,1,0:T(8,128)S(1)} all-gather(f32[4,16,128]{2,1,0:T(8,128)S(1)} %get-tuple-element.175), channel_id=2, replica_groups=mesh['seq'=8,'ch'=4] {'ch'}, dimensions={0}, use_global_device_ids=true | all-gather | bytes 163840 | tf_op jit(solution)/shard_map/all_gather | solution.py:1414
  43.0 5.6 %mix.1 = (f32[4,1024,128]{2,1,0:T(8,128)S(1)}, f32[4,128,128]{2,1,0:T(8,128)S(1)}) custom-call(s32[1]{0:T(128)} %bitcast.6.place_ref.refs_0_, f32[4,1024,128]{2,1,0:T(8,128)S(1)} %get-tuple-element.173.normed_ref.refs_1_.refs_5_, f32[4,128,128]{2,1,0:T(8,128)S(1)} %get-tuple-element.174.ends_ref, f32[4,4,16,128]{3,2,1,0:T(8,128)S(1)} %bitcast.120, ...), custom_call_target="tpu_custom_call" | custom-call | tf_op jit(solution)/shard_map/mix/pallas_call | solution.py:1415
  51.2 57.4 %forward.1 = (f32[1024,512]{1,0:T(8,128)}, f32[4,1024,128]{2,1,0:T(8,128)}, bf16[1024,1024]{1,0:T(8,128)(2,1)}, bf16[1024,1024]{1,0:T(8,128)(2,1)}, f32[1024,102...) custom-call(s32[2]{0:T(128)S(1)} %get-tuple-element.338.info_ref, ...), custom_call_target="tpu_custom_call" | custom-call | flops 32614907904 | bytes 50331648 | tf_op jit(solution)/shard_map/forward/pallas_call | solution.py:930
  109.3 3.8 %collective-permute-done.1.refs_2_ = f32[2,1024,256]{2,1,0:T(8,128)S(1)} collective-permute-done((f32[2,1024,256]{2,1,0:T(8,128)}, f32[2,1024,256]{2,1,0:T(8,128)S(1)}, u32[]{:S(2)}, u32[]{:S(2)}) %collective-permute-start.1) | collective-permute-done | bytes 2097184 | tf_op jit(solution)/shard_map/ppermute | solution.py:1045
  113.1 1.6 copy-done.22
  115.0 2.3 collective-permute-start.3
  117.5 1.6 collective-permute-start.2
  119.1 33.0 %backward.1 = (f32[4,1024,128]{2,1,0:T(8,128)}, f32[4,1024,128]{2,1,0:T(8,128)}, f32[8,128]{1,0:T(8,128)S(1)}, f32[4,1,128]{2,1,0:T(1,128)S(1)}, f32[2,1088,256]{2,1,0:T(8,128)}, /*index=5*/f32[2,1088,256]{2,1,0:T(8,128)}) custom-call(s32[2]{0:T(128)S(1)} %pad_add_fusion.2.refs_0_, f32[4,1024,128]{2,1,0:T(8,128)} %copy-done, f32[4,1024,128]{2,1,0:T(8,128)} %copy-done.39, ...), custom_call_target="tpu_custom_call" | custom-call | flops 26575110144 | bytes 41943040 | tf_op jit(solution)/shard_map/backward/pallas_call | solution.py:48
  155.0 2.8 back_ends.1
  157.9 5.4 %all-gather.1 = f32[16,16,128]{2,1,0:T(8,128)S(1)} all-gather(f32[4,16,128]{2,1,0:T(8,128)S(1)} %get-tuple-element.217), channel_id=3, replica_groups=mesh['seq'=8,'ch'=4] {'ch'}, dimensions={0}, use_global_device_ids=true | all-gather | bytes 163840 | tf_op jit(solution)/shard_map/all_gather | solution.py:1497
  169.0 1.6 copy-done.12
  170.7 1.6 copy-done.14
  175.3 1.8 halve.23
  178.6 4.0 %back.4 = (f32[1,1024,128]{2,1,0:T(8,128)S(1)}, f32[1,16,128]{2,1,0:T(8,128)S(1)}, f32[1,16,128]{2,1,0:T(8,128)S(1)}) custom-call(s32[1]{0:T(128)} %bitcast.6.place_ref.refs_0_, f32[4,1024,128]{2,1,0:T(8,128)S(1)} %copy-done.3, f32[4,128,128]{2,1,0:T(8,128)S(1)} %get-tuple-element.216.refs_2_, f32[4,4,16,128]{3,2,1,0:T(8,128)S(1)} %bitcast.99, ...), custom_call_target="tpu_custom_call" | custom-call | flops 20971520 | bytes 1572864 | tf_op jit(solution)/shard_map/back/pallas_call | solution.py:48
  183.5 3.8 %back.5 = (f32[1,1024,128]{2,1,0:T(8,128)S(1)}, f32[1,16,128]{2,1,0:T(8,128)S(1)}, f32[1,16,128]{2,1,0:T(8,128)S(1)}) custom-call(s32[1]{0:T(128)} %bitcast.6.place_ref.refs_0_, f32[4,1024,128]{2,1,0:T(8,128)S(1)} %copy-done.3, f32[4,128,128]{2,1,0:T(8,128)S(1)} %get-tuple-element.216.refs_2_, f32[4,4,16,128]{3,2,1,0:T(8,128)S(1)} %bitcast.100, ...), custom_call_target="tpu_custom_call" | custom-call | flops 20971520 | bytes 1572864 | tf_op jit(solution)/shard_map/back/pallas_call | solution.py:48
  187.3 2.0 halve.24
  194.0 2.7 collective-permute-start.12
  199.0 1.6 copy-done.4
  202.2 3.8 %back.6 = (f32[1,1024,128]{2,1,0:T(8,128)S(1)}, f32[1,16,128]{2,1,0:T(8,128)S(1)}, f32[1,16,128]{2,1,0:T(8,128)S(1)}) custom-call(s32[1]{0:T(128)} %bitcast.6.place_ref.refs_0_, f32[4,1024,128]{2,1,0:T(8,128)S(1)} %copy-done.4, f32[4,128,128]{2,1,0:T(8,128)S(1)} %get-tuple-element.216.refs_2_, f32[4,4,16,128]{3,2,1,0:T(8,128)S(1)} %bitcast.101, ...), custom_call_target="tpu_custom_call" | custom-call | flops 20971520 | bytes 1572864 | tf_op jit(solution)/shard_map/back/pallas_call | solution.py:48
  209.2 2.7 collective-permute-start.19
  212.3 3.8 %back.7 = (f32[1,1024,128]{2,1,0:T(8,128)S(1)}, f32[1,16,128]{2,1,0:T(8,128)S(1)}, f32[1,16,128]{2,1,0:T(8,128)S(1)}) custom-call(s32[1]{0:T(128)} %bitcast.6.place_ref.refs_0_, f32[4,1024,128]{2,1,0:T(8,128)S(1)} %copy-done.5, f32[4,128,128]{2,1,0:T(8,128)S(1)} %get-tuple-element.216.refs_2_, f32[4,4,16,128]{3,2,1,0:T(8,128)S(1)} %bitcast.102, ...), custom_call_target="tpu_custom_call" | custom-call | flops 20971520 | bytes 1572864 | tf_op jit(solution)/shard_map/back/pallas_call | solution.py:48
  216.3 2.1 unnorm.1
  222.3 2.3 collective-permute-start.17
  224.6 3.3 %collective-permute-done.17.refs_1_ = f32[72,256]{1,0:T(8,128)S(1)} collective-permute-done((f32[72,256]{1,0:T(8,128)S(1)}, f32[72,256]{1,0:T(8,128)S(1)}, u32[]{:S(2)}, u32[]{:S(2)}) %collective-permute-start.17) | collective-permute-done | bytes 73760 | tf_op jit(solution)/shard_map/ppermute | solution.py:1045
  228.5 2.5 collective-permute-start.20
  231.6 7.5 %collective-permute-done.21.refs_1_ = f32[64,256]{1,0:T(8,128)S(1)} collective-permute-done((f32[64,256]{1,0:T(8,128)S(1)}, f32[64,256]{1,0:T(8,128)S(1)}, u32[]{:S(2)}, u32[]{:S(2)}) %collective-permute-start.21) | collective-permute-done | bytes 65568 | tf_op jit(solution)/shard_map/ppermute | solution.py:1045
  239.2 2.0 collective-permute-start.28
  242.1 5.9 %collective-permute-done.25.refs_1_ = f32[64,256]{1,0:T(8,128)S(1)} collective-permute-done((f32[64,256]{1,0:T(8,128)S(1)}, f32[64,256]{1,0:T(8,128)S(1)}, u32[]{:S(2)}, u32[]{:S(2)}) %collective-permute-start.25) | collective-permute-done | bytes 65568 | tf_op jit(solution)/shard_map/ppermute | solution.py:1045
  248.1 2.1 collective-permute-start.26
  250.2 2.8 collective-permute-done.29.refs_2_
  254.8 1.9 collective-permute-done.27.refs_3_
  257.8 1.7 collective-permute-done.33.refs_3_
  261.2 2.2 collective-permute-start.40
  264.9 10.6 %collective-permute-done.34.refs_7_ = f32[512,256]{1,0:T(8,128)} collective-permute-done((f32[512,256]{1,0:T(8,128)}, f32[512,256]{1,0:T(8,128)}, u32[]{:S(2)}, u32[]{:S(2)}) %collective-permute-start.34) | collective-permute-done | bytes 524320 | tf_op jit(solution)/shard_map/ppermute | solution.py:1045
  275.5 3.6 %all-to-all-start.1 = ((f32[4,1024,128]{2,1,0:T(8,128)}), f32[4,1024,128]{2,1,0:T(8,128)S(1)}, u32[]{:S(2)}, u32[]{:S(2)}) async-start(f32[4,1024,128]{2,1,0:T(8,128)} %copy-done.21), calls=%async_computation.1 | async-start | bytes 4194304 | tf_op jit(solution)/shard_map/all_to_all | solution.py:1523
  279.1 7.1 %collective-permute-done.30.refs_3_.part_b = f32[656,256]{1,0:T(8,128)S(1)} collective-permute-done((f32[656,256]{1,0:T(8,128)S(1)}, f32[656,256]{1,0:T(8,128)S(1)}, u32[]{:S(2)}, u32[]{:S(2)}) %collective-permute-start.30) | collective-permute-done | bytes 671776 | tf_op jit(solution)/shard_map/ppermute | solution.py:1045
  287.4 1.8 collective-permute-done.32.refs_5_.part_d
  290.2 1.8 small_grads.1
  293.1 6.5 %finish_one.1 = (f32[512,1024]{1,0:T(8,128)}, f32[1024,512]{1,0:T(8,128)}, f32[1024,512]{1,0:T(8,128)}, f32[512,2176]{1,0:T(8,128)}, f32[8,128]{1,0:T(8,128)S(1)}) custom-call(s32[4]{0:T(128)S(1)} %add_add_fusion.1.refs_0_.refs_1_, s32[4]{0:T(128)S(1)} %add_add_fusion.refs_1_.refs_0_, f32[1024,256]{1,0:T(8,128)} %get-tuple-element.310.refs_2_, ...), custom_call_target="tpu_custom_call" | custom-call | bytes 1024 | tf_op jit(solution)/shard_map/finish_one/pallas_call | solution.py:48
  299.6 3.9 %finish_rest.1 = (f32[512,1024]{1,0:T(8,128)}, f32[512,2176]{1,0:T(8,128)}, f32[8,128]{1,0:T(8,128)S(1)}) custom-call(s32[4]{0:T(128)S(1)} %add_add_fusion.refs_1_.refs_0_, s32[4]{0:T(128)S(1)} %add_add_fusion.1.refs_0_.refs_1_, f32[656,256]{1,0:T(8,128)S(1)} %get-tuple-element.306.refs_2_.part_a, ...), custom_call_target="tpu_custom_call", output_to_operand_aliasing={{1}: (10, {})} | custom-call | bytes 1024 | tf_op jit(solution)/shard_map/finish_rest/pallas_call | solution.py:48
  303.5 3.3 %all-to-all-done.1.refs_0_ = f32[4,1024,128]{2,1,0:T(8,128)S(1)} async-done(((f32[4,1024,128]{2,1,0:T(8,128)}), f32[4,1024,128]{2,1,0:T(8,128)S(1)}, u32[]{:S(2)}, u32[]{:S(2)}) %all-to-all-start.1) | async-done | bytes 2097184 | tf_op jit(solution)/shard_map/all_to_all | solution.py:1523
  (229 shorter events, 62.5 us)
Async XLA Ops:
  0.7 30.1 %all-to-all-start = ((f32[4,1024,128]{2,1,0:T(8,128)}), f32[4,1024,128]{2,1,0:T(8,128)S(1)}, u32[]{:S(2)}, u32[]{:S(2)}) async-start(f32[4,1024,128]{2,1,0:T(8,128)} %bitcast.141), calls=%async_computation | async-start | bytes 4194304 | tf_op jit(solution)/shard_map/all_to_all | solution.py:1384
  12.8 19.3 %copy-start.35 = (f32[512]{0:T(512)S(1)}, f32[512]{0:T(512)}, u32[]{:S(2)}) copy-start(f32[512]{0:T(512)} %param.20) | copy-start | bytes 6148
  108.7 4.4 %collective-permute-start.1 = (f32[2,1024,256]{2,1,0:T(8,128)}, f32[2,1024,256]{2,1,0:T(8,128)S(1)}, u32[]{:S(2)}, u32[]{:S(2)}) collective-permute-start(f32[2,1024,256]{2,1,0:T(8,128)} %get-tuple-element.202), channel_id=1, source_target_pairs={{0,1},{1,0},{2,3},{3,2},{4,5},{5,4},{6,7},{7,6},{8,9},{9,8},{10,11... | collective-permute-start | bytes 6291464 | tf_op jit(solution)/shard_map/ppermute | solution.py:1045
  109.0 8.3 %collective-permute-start = (f32[2,1024,256]{2,1,0:T(8,128)}, f32[2,1024,256]{2,1,0:T(8,128)S(1)}, u32[]{:S(2)}, u32[]{:S(2)}) collective-permute-start(f32[2,1024,256]{2,1,0:T(8,128)} %get-tuple-element.200), channel_id=1, source_target_pairs={{0,1},{1,0},{2,3},{3,2},{4,5},{5,4},{6,7},{7,6},{8,9},{9,8},{10,11... | collective-permute-start | bytes 6291464 | tf_op jit(solution)/shard_map/ppermute | solution.py:1045
  115.0 37.2 %collective-permute-start.3 = (f32[1024,256]{1,0:T(8,128)S(1)}, f32[1024,256]{1,0:T(8,128)S(1)}, u32[]{:S(2)}, u32[]{:S(2)}) collective-permute-start(f32[1024,256]{1,0:T(8,128)S(1)} %get-tuple-element.211), channel_id=1, source_target_pairs={{0,4},{4,0},{8,12},{12,8},{16,20},{20,16},{24,28},{28,24},{1,5},{5... | collective-permute-start | bytes 3145736 | tf_op jit(solution)/shard_map/ppermute | solution.py:1045
  117.5 34.8 %collective-permute-start.2 = (f32[1024,256]{1,0:T(8,128)S(1)}, f32[1024,256]{1,0:T(8,128)S(1)}, u32[]{:S(2)}, u32[]{:S(2)}) collective-permute-start(f32[1024,256]{1,0:T(8,128)S(1)} %get-tuple-element.209), channel_id=1, source_target_pairs={{0,8},{4,12},{8,0},{12,4},{16,24},{20,28},{24,16},{28,20},{1,9},{5... | collective-permute-start | bytes 3145736 | tf_op jit(solution)/shard_map/ppermute | solution.py:1045
  153.2 10.1 %collective-permute-start.5 = (f32[2,1088,256]{2,1,0:T(8,128)}, f32[2,1088,256]{2,1,0:T(8,128)S(1)}, u32[]{:S(2)}, u32[]{:S(2)}) collective-permute-start(f32[2,1088,256]{2,1,0:T(8,128)} %get-tuple-element.223), channel_id=1, source_target_pairs={{0,1},{1,0},{2,3},{3,2},{4,5},{5,4},{6,7},{7,6},{8,9},{9,8},{10,11... | collective-permute-start | bytes 6684680 | tf_op jit(solution)/shard_map/ppermute | solution.py:1045
  153.2 14.3 %collective-permute-start.6 = (f32[512,256]{1,0:T(8,128)S(1)}, f32[512,256]{1,0:T(8,128)S(1)}, u32[]{:S(2)}, u32[]{:S(2)}) collective-permute-start(f32[512,256]{1,0:T(8,128)S(1)} %get-tuple-element.225), channel_id=1, source_target_pairs={{0,8},{4,12},{8,0},{12,4},{16,24},{20,28},{24,16},{28,20},{1,9},{5... | collective-permute-start | bytes 1572872 | tf_op jit(solution)/shard_map/ppermute | solution.py:1045
  153.7 20.6 %collective-permute-start.4 = (f32[512,256]{1,0:T(8,128)}, f32[512,256]{1,0:T(8,128)}, u32[]{:S(2)}, u32[]{:S(2)}) collective-permute-start(f32[512,256]{1,0:T(8,128)} %get-tuple-element.221), channel_id=1, source_target_pairs={{0,4},{4,0},{8,12},{12,8},{16,20},{20,16},{24,28},{28,24},{1,5},{5... | collective-permute-start | bytes 1572872 | tf_op jit(solution)/shard_map/ppermute | solution.py:1045
  164.9 22.4 %collective-permute-start.10 = (f32[576,256]{1,0:T(8,128)}, f32[576,256]{1,0:T(8,128)}, u32[]{:S(2)}, u32[]{:S(2)}) collective-permute-start(f32[576,256]{1,0:T(8,128)} %get-tuple-element.240), channel_id=1, source_target_pairs={{0,8},{4,12},{8,0},{12,4},{16,24},{20,28},{24,16},{28,20},{1,9},{5... | collective-permute-start | bytes 1769480 | tf_op jit(solution)/shard_map/ppermute | solution.py:1045
  172.4 18.4 %collective-permute-start.9 = (f32[512,256]{1,0:T(8,128)S(1)}, f32[512,256]{1,0:T(8,128)S(1)}, u32[]{:S(2)}, u32[]{:S(2)}) collective-permute-start(f32[512,256]{1,0:T(8,128)S(1)} %get-tuple-element.238), channel_id=1, source_target_pairs={{0,4},{4,0},{8,12},{12,8},{16,20},{20,16},{24,28},{28,24},{1,5},{5... | collective-permute-start | bytes 1572872 | tf_op jit(solution)/shard_map/ppermute | solution.py:1045
  173.7 18.3 %collective-permute-start.8 = (f32[256,256]{1,0:T(8,128)}, f32[256,256]{1,0:T(8,128)}, u32[]{:S(2)}, u32[]{:S(2)}) collective-permute-start(f32[256,256]{1,0:T(8,128)} %get-tuple-element.236), channel_id=1, source_target_pairs={{0,2},{1,3},{2,0},{3,1},{4,6},{5,7},{6,4},{7,5},{8,10},{9,11},{10,... | collective-permute-start | bytes 786440 | tf_op jit(solution)/shard_map/ppermute | solution.py:1045
  177.1 19.6 %collective-permute-start.7 = (f32[256,256]{1,0:T(8,128)}, f32[256,256]{1,0:T(8,128)}, u32[]{:S(2)}, u32[]{:S(2)}) collective-permute-start(f32[256,256]{1,0:T(8,128)} %get-tuple-element.234), channel_id=1, source_target_pairs={{0,2},{1,3},{2,0},{3,1},{4,6},{5,7},{6,4},{7,5},{8,10},{9,11},{10,... | collective-permute-start | bytes 786440 | tf_op jit(solution)/shard_map/ppermute | solution.py:1045
  190.0 16.0 %collective-permute-start.14 = (f32[288,256]{1,0:T(8,128)}, f32[288,256]{1,0:T(8,128)S(1)}, u32[]{:S(2)}, u32[]{:S(2)}) collective-permute-start(f32[288,256]{1,0:T(8,128)} %get-tuple-element.254), channel_id=1, source_target_pairs={{0,4},{4,0},{8,12},{12,8},{16,20},{20,16},{24,28},{28,24},{1,5},{5... | collective-permute-start | bytes 884744 | tf_op jit(solution)/shard_map/ppermute | solution.py:1045
  191.6 15.1 %collective-permute-start.13 = (f32[256,256]{1,0:T(8,128)}, f32[256,256]{1,0:T(8,128)}, u32[]{:S(2)}, u32[]{:S(2)}) collective-permute-start(f32[256,256]{1,0:T(8,128)} %get-tuple-element.252), channel_id=1, source_target_pairs={{0,8},{4,12},{8,0},{12,4},{16,24},{20,28},{24,16},{28,20},{1,9},{5... | collective-permute-start | bytes 786440 | tf_op jit(solution)/shard_map/ppermute | solution.py:1045
  194.0 15.2 %collective-permute-start.12 = (f32[128,256]{1,0:T(8,128)S(1)}, f32[128,256]{1,0:T(8,128)S(1)}, u32[]{:S(2)}, u32[]{:S(2)}) collective-permute-start(f32[128,256]{1,0:T(8,128)S(1)} %get-tuple-element.250), channel_id=1, source_target_pairs={{0,16},{4,20},{8,24},{12,28},{16,0},{20,4},{24,8},{28,12},{1,17},{... | collective-permute-start | bytes 393224 | tf_op jit(solution)/shard_map/ppermute | solution.py:1045
  198.6 13.3 %collective-permute-start.11 = (f32[128,256]{1,0:T(8,128)S(1)}, f32[128,256]{1,0:T(8,128)S(1)}, u32[]{:S(2)}, u32[]{:S(2)}) collective-permute-start(f32[128,256]{1,0:T(8,128)S(1)} %get-tuple-element.248), channel_id=1, source_target_pairs={{0,16},{4,20},{8,24},{12,28},{16,0},{20,4},{24,8},{28,12},{1,17},{... | collective-permute-start | bytes 393224 | tf_op jit(solution)/shard_map/ppermute | solution.py:1045
  206.1 10.1 %collective-permute-start.16 = (f32[144,256]{1,0:T(8,128)S(1)}, f32[144,256]{1,0:T(8,128)S(1)}, u32[]{:S(2)}, u32[]{:S(2)}) collective-permute-start(f32[144,256]{1,0:T(8,128)S(1)} %get-tuple-element.271), channel_id=1, source_target_pairs={{0,2},{1,3},{2,0},{3,1},{4,6},{5,7},{6,4},{7,5},{8,10},{9,11},{10,... | collective-permute-start | bytes 442376 | tf_op jit(solution)/shard_map/ppermute | solution.py:1045
  207.6 8.6 %collective-permute-start.15 = (f32[128,256]{1,0:T(8,128)S(1)}, f32[128,256]{1,0:T(8,128)S(1)}, u32[]{:S(2)}, u32[]{:S(2)}) collective-permute-start(f32[128,256]{1,0:T(8,128)S(1)} %get-tuple-element.269), channel_id=1, source_target_pairs={{0,2},{1,3},{2,0},{3,1},{4,6},{5,7},{6,4},{7,5},{8,10},{9,11},{10,... | collective-permute-start | bytes 393224 | tf_op jit(solution)/shard_map/ppermute | solution.py:1045
  209.2 10.8 %collective-permute-start.19 = (f32[128,256]{1,0:T(8,128)S(1)}, f32[128,256]{1,0:T(8,128)S(1)}, u32[]{:S(2)}, u32[]{:S(2)}) collective-permute-start(f32[128,256]{1,0:T(8,128)S(1)} %get-tuple-element.280.refs_0_), channel_id=1, source_target_pairs={{0,16},{4,20},{8,24},{12,28},{16,0},{20,4},{24,8},{28,12},{1,17},{... | collective-permute-start | bytes 393224 | tf_op jit(solution)/shard_map/ppermute | solution.py:1045
  211.9 9.5 %collective-permute-start.18 = (f32[128,256]{1,0:T(8,128)S(1)}, f32[128,256]{1,0:T(8,128)S(1)}, u32[]{:S(2)}, u32[]{:S(2)}) collective-permute-start(f32[128,256]{1,0:T(8,128)S(1)} %get-tuple-element.279.refs_0_), channel_id=1, source_target_pairs={{0,16},{4,20},{8,24},{12,28},{16,0},{20,4},{24,8},{28,12},{1,17},{... | collective-permute-start | bytes 393224 | tf_op jit(solution)/shard_map/ppermute | solution.py:1045
  220.0 11.5 %collective-permute-start.23 = (f32[256,256]{1,0:T(8,128)S(1)}, f32[256,256]{1,0:T(8,128)S(1)}, u32[]{:S(2)}, u32[]{:S(2)}) collective-permute-start(f32[256,256]{1,0:T(8,128)S(1)} %get-tuple-element.289), channel_id=1, source_target_pairs={{0,8},{4,12},{8,0},{12,4},{16,24},{20,28},{24,16},{28,20},{1,9},{5... | collective-permute-start | bytes 786440 | tf_op jit(solution)/shard_map/ppermute | solution.py:1045
  221.5 10.1 %collective-permute-start.22 = (f32[256,256]{1,0:T(8,128)S(1)}, f32[256,256]{1,0:T(8,128)S(1)}, u32[]{:S(2)}, u32[]{:S(2)}) collective-permute-start(f32[256,256]{1,0:T(8,128)S(1)} %get-tuple-element.288), channel_id=1, source_target_pairs={{0,2},{1,3},{2,0},{3,1},{4,6},{5,7},{6,4},{7,5},{8,10},{9,11},{10,... | collective-permute-start | bytes 786440 | tf_op jit(solution)/shard_map/ppermute | solution.py:1045
  222.3 5.6 %collective-permute-start.17 = (f32[72,256]{1,0:T(8,128)S(1)}, f32[72,256]{1,0:T(8,128)S(1)}, u32[]{:S(2)}, u32[]{:S(2)}) collective-permute-start(f32[72,256]{1,0:T(8,128)S(1)} %get-tuple-element.278), channel_id=1, source_target_pairs={{0,16},{4,20},{8,24},{12,28},{16,0},{20,4},{24,8},{28,12},{1,17},{... | collective-permute-start | bytes 221192 | tf_op jit(solution)/shard_map/ppermute | solution.py:1045
  228.5 10.6 %collective-permute-start.20 = (f32[152,256]{1,0:T(8,128)S(1)}, f32[152,256]{1,0:T(8,128)S(1)}, u32[]{:S(2)}, u32[]{:S(2)}) collective-permute-start(f32[152,256]{1,0:T(8,128)S(1)} %get-tuple-element.285.refs_2_), channel_id=1, source_target_pairs={{0,16},{4,20},{8,24},{12,28},{16,0},{20,4},{24,8},{28,12},{1,17},{... | collective-permute-start | bytes 466952 | tf_op jit(solution)/shard_map/ppermute | solution.py:1045
  231.0 8.1 %collective-permute-start.21 = (f32[64,256]{1,0:T(8,128)S(1)}, f32[64,256]{1,0:T(8,128)S(1)}, u32[]{:S(2)}, u32[]{:S(2)}) collective-permute-start(f32[64,256]{1,0:T(8,128)S(1)} %get-tuple-element.287), channel_id=1, source_target_pairs={{0,16},{4,20},{8,24},{12,28},{16,0},{20,4},{24,8},{28,12},{1,17},{... | collective-permute-start | bytes 196616 | tf_op jit(solution)/shard_map/ppermute | solution.py:1045
  239.1 8.9 %collective-permute-start.24 = (f32[224,256]{1,0:T(8,128)S(1)}, f32[224,256]{1,0:T(8,128)S(1)}, u32[]{:S(2)}, u32[]{:S(2)}) collective-permute-start(f32[224,256]{1,0:T(8,128)S(1)} %get-tuple-element.294.refs_3_), channel_id=1, source_target_pairs={{0,4},{4,0},{8,12},{12,8},{16,20},{20,16},{24,28},{28,24},{1,5},{5... | collective-permute-start | bytes 688136 | tf_op jit(solution)/shard_map/ppermute | solution.py:1045
  239.2 14.6 %collective-permute-start.28 = (f32[512,256]{1,0:T(8,128)S(1)}, f32[512,256]{1,0:T(8,128)S(1)}, u32[]{:S(2)}, u32[]{:S(2)}) collective-permute-start(f32[512,256]{1,0:T(8,128)S(1)} %get-tuple-element.300), channel_id=1, source_target_pairs={{0,2},{1,3},{2,0},{3,1},{4,6},{5,7},{6,4},{7,5},{8,10},{9,11},{10,... | collective-permute-start | bytes 1572872 | tf_op jit(solution)/shard_map/ppermute | solution.py:1045
  241.2 15.5 %collective-permute-start.27 = (f32[512,256]{1,0:T(8,128)S(1)}, f32[512,256]{1,0:T(8,128)S(1)}, u32[]{:S(2)}, u32[]{:S(2)}) collective-permute-start(f32[512,256]{1,0:T(8,128)S(1)} %get-tuple-element.299), channel_id=1, source_target_pairs={{0,4},{4,0},{8,12},{12,8},{16,20},{20,16},{24,28},{28,24},{1,5},{5... | collective-permute-start | bytes 1572872 | tf_op jit(solution)/shard_map/ppermute | solution.py:1045
  242.1 5.9 %collective-permute-start.25 = (f32[64,256]{1,0:T(8,128)S(1)}, f32[64,256]{1,0:T(8,128)S(1)}, u32[]{:S(2)}, u32[]{:S(2)}) collective-permute-start(f32[64,256]{1,0:T(8,128)S(1)} %get-tuple-element.295.refs_0_), channel_id=1, source_target_pairs={{0,16},{4,20},{8,24},{12,28},{16,0},{20,4},{24,8},{28,12},{1,17},{... | collective-permute-start | bytes 196616 | tf_op jit(solution)/shard_map/ppermute | solution.py:1045
  248.0 5.0 %collective-permute-start.29 = (f32[128,256]{1,0:T(8,128)S(1)}, f32[128,256]{1,0:T(8,128)S(1)}, u32[]{:S(2)}, u32[]{:S(2)}) collective-permute-start(f32[128,256]{1,0:T(8,128)S(1)} %get-tuple-element.301), channel_id=1, source_target_pairs={{0,8},{4,12},{8,0},{12,4},{16,24},{20,28},{24,16},{28,20},{1,9},{5... | collective-permute-start | bytes 393224 | tf_op jit(solution)/shard_map/ppermute | solution.py:1045
  248.1 9.7 %collective-permute-start.26 = (f32[368,256]{1,0:T(8,128)S(1)}, f32[368,256]{1,0:T(8,128)S(1)}, u32[]{:S(2)}, u32[]{:S(2)}) collective-permute-start(f32[368,256]{1,0:T(8,128)S(1)} %get-tuple-element.298.refs_4_), channel_id=1, source_target_pairs={{0,8},{4,12},{8,0},{12,4},{16,24},{20,28},{24,16},{28,20},{1,9},{5... | collective-permute-start | bytes 1130504 | tf_op jit(solution)/shard_map/ppermute | solution.py:1045
  253.0 6.5 %collective-permute-start.33 = (f32[256,256]{1,0:T(8,128)S(1)}, f32[256,256]{1,0:T(8,128)S(1)}, u32[]{:S(2)}, u32[]{:S(2)}) collective-permute-start(f32[256,256]{1,0:T(8,128)S(1)} %get-tuple-element.307), channel_id=1, source_target_pairs={{0,4},{4,0},{8,12},{12,8},{16,20},{20,16},{24,28},{28,24},{1,5},{5... | collective-permute-start | bytes 786440 | tf_op jit(solution)/shard_map/ppermute | solution.py:1045
  260.3 15.2 %collective-permute-start.34 = (f32[512,256]{1,0:T(8,128)}, f32[512,256]{1,0:T(8,128)}, u32[]{:S(2)}, u32[]{:S(2)}) collective-permute-start(f32[512,256]{1,0:T(8,128)} %get-tuple-element.309.refs_6_), channel_id=1, source_target_pairs={{0,2},{1,3},{2,0},{3,1},{4,6},{5,7},{6,4},{7,5},{8,10},{9,11},{10,... | collective-permute-start | bytes 1572872 | tf_op jit(solution)/shard_map/ppermute | solution.py:1045
  261.2 25.6 %collective-permute-start.40 = (f32[1024,256]{1,0:T(8,128)}, f32[1024,256]{1,0:T(8,128)}, u32[]{:S(2)}, u32[]{:S(2)}) collective-permute-start(f32[1024,256]{1,0:T(8,128)} %get-tuple-element.311.refs_6_), channel_id=1, source_target_pairs={{0,8},{4,12},{8,0},{12,4},{16,24},{20,28},{24,16},{28,20},{1,9},{5... | collective-permute-start | bytes 3145736 | tf_op jit(solution)/shard_map/ppermute | solution.py:1045
  263.4 23.5 %collective-permute-start.37 = (f32[1024,256]{1,0:T(8,128)}, f32[1024,256]{1,0:T(8,128)}, u32[]{:S(2)}, u32[]{:S(2)}) collective-permute-start(f32[1024,256]{1,0:T(8,128)} %get-tuple-element.310.refs_2_), channel_id=1, source_target_pairs={{0,4},{4,0},{8,12},{12,8},{16,20},{20,16},{24,28},{28,24},{1,5},{5... | collective-permute-start | bytes 3145736 | tf_op jit(solution)/shard_map/ppermute | solution.py:1045
  264.3 25.1 %copy-start.59 = (f32[512,16]{0,1:T(8,128)S(1)}, f32[512,16]{0,1:T(8,128)}, u32[]{:S(2)}) copy-start(f32[512,16]{0,1:T(8,128)} %param.23) | copy-start | bytes 98308
  264.3 25.2 %copy-start.60 = (f32[2,4,8,128]{3,2,1,0:T(8,128)S(1)}, f32[2,4,8,128]{3,2,1,0:T(8,128)}, u32[]{:S(2)}) copy-start(f32[2,4,8,128]{3,2,1,0:T(8,128)} %get-tuple-element.330) | copy-start | bytes 98308
  264.3 21.9 %collective-permute-start.30 = (f32[656,256]{1,0:T(8,128)S(1)}, f32[656,256]{1,0:T(8,128)S(1)}, u32[]{:S(2)}, u32[]{:S(2)}) collective-permute-start(f32[656,256]{1,0:T(8,128)S(1)} %get-tuple-element.306.refs_2_.part_a), channel_id=1, source_target_pairs={{0,2},{1,3},{2,0},{3,1},{4,6},{5,7},{6,4},{7,5},{8,10},{9,11},{10,... | collective-permute-start | bytes 2015240 | tf_op jit(solution)/shard_map/ppermute | solution.py:1045
  264.9 21.3 %collective-permute-start.31 = (f32[656,256]{1,0:T(8,128)S(1)}, f32[656,256]{1,0:T(8,128)}, u32[]{:S(2)}, u32[]{:S(2)}) collective-permute-start(f32[656,256]{1,0:T(8,128)S(1)} %get-tuple-element.306.refs_2_.part_a), channel_id=1, source_target_pairs={{0,1},{1,0},{2,3},{3,2},{4,5},{5,4},{6,7},{7,6},{8,9},{9,8},{10,11... | collective-permute-start | bytes 2015240 | tf_op jit(solution)/shard_map/ppermute | solution.py:1045
  275.5 11.8 %collective-permute-start.41 = (f32[1024,256]{1,0:T(8,128)}, f32[1024,256]{1,0:T(8,128)}, u32[]{:S(2)}, u32[]{:S(2)}) collective-permute-start(f32[1024,256]{1,0:T(8,128)} %get-tuple-element.311.refs_6_), channel_id=1, source_target_pairs={{0,1},{1,0},{2,3},{3,2},{4,5},{5,4},{6,7},{7,6},{8,9},{9,8},{10,11... | collective-permute-start | bytes 3145736 | tf_op jit(solution)/shard_map/ppermute | solution.py:1045
  275.5 31.3 %all-to-all-start.1 = ((f32[4,1024,128]{2,1,0:T(8,128)}), f32[4,1024,128]{2,1,0:T(8,128)S(1)}, u32[]{:S(2)}, u32[]{:S(2)}) async-start(f32[4,1024,128]{2,1,0:T(8,128)} %copy-done.21), calls=%async_computation.1 | async-start | bytes 4194304 | tf_op jit(solution)/shard_map/all_to_all | solution.py:1523
  286.2 3.0 collective-permute-start.32
  286.2 5.8 %collective-permute-start.38 = (f32[1024,256]{1,0:T(8,128)}, f32[1024,256]{1,0:T(8,128)S(1)}, u32[]{:S(2)}, u32[]{:S(2)}) collective-permute-start(f32[1024,256]{1,0:T(8,128)} %get-tuple-element.310.refs_2_), channel_id=1, source_target_pairs={{0,1},{1,0},{2,3},{3,2},{4,5},{5,4},{6,7},{7,6},{8,9},{9,8},{10,11... | collective-permute-start | bytes 3145736 | tf_op jit(solution)/shard_map/ppermute | solution.py:1045
  286.8 5.3 %collective-permute-start.42 = (f32[1024,256]{1,0:T(8,128)}, f32[1024,256]{1,0:T(8,128)S(1)}, u32[]{:S(2)}, u32[]{:S(2)}) collective-permute-start(f32[1024,256]{1,0:T(8,128)} %collective-permute-done.40.refs_7_), channel_id=1, source_target_pairs={{0,1},{1,0},{2,3},{3,2},{4,5},{5,4},{6,7},{7,6},{8,9},{9,8},{10,11... | collective-permute-start | bytes 3145736 | tf_op jit(solution)/shard_map/ppermute | solution.py:1045
  286.8 6.2 %collective-permute-start.39 = (f32[1024,256]{1,0:T(8,128)}, f32[1024,256]{1,0:T(8,128)S(1)}, u32[]{:S(2)}, u32[]{:S(2)}) collective-permute-start(f32[1024,256]{1,0:T(8,128)} %collective-permute-done.37.refs_3_), channel_id=1, source_target_pairs={{0,1},{1,0},{2,3},{3,2},{4,5},{5,4},{6,7},{7,6},{8,9},{9,8},{10,11... | collective-permute-start | bytes 3145736 | tf_op jit(solution)/shard_map/ppermute | solution.py:1045
  287.4 12.2 %collective-permute-start.35 = (f32[512,256]{1,0:T(8,128)}, f32[512,256]{1,0:T(8,128)S(1)}, u32[]{:S(2)}, u32[]{:S(2)}) collective-permute-start(f32[512,256]{1,0:T(8,128)} %get-tuple-element.309.refs_6_), channel_id=1, source_target_pairs={{0,1},{1,0},{2,3},{3,2},{4,5},{5,4},{6,7},{7,6},{8,9},{9,8},{10,11... | collective-permute-start | bytes 1572872 | tf_op jit(solution)/shard_map/ppermute | solution.py:1045
  289.2 10.3 %collective-permute-start.36 = (f32[512,256]{1,0:T(8,128)}, f32[512,256]{1,0:T(8,128)S(1)}, u32[]{:S(2)}, u32[]{:S(2)}) collective-permute-start(f32[512,256]{1,0:T(8,128)} %collective-permute-done.34.refs_7_), channel_id=1, source_target_pairs={{0,1},{1,0},{2,3},{3,2},{4,5},{5,4},{6,7},{7,6},{8,9},{9,8},{10,11... | collective-permute-start | bytes 1572872 | tf_op jit(solution)/shard_map/ppermute | solution.py:1045
  (60 other events, 303.9 us)

commit v3 on v2

--- a/solution.py
+++ b/solution.py
@@ -20,8 +20,8 @@
 TILE = 256
 SMALL = 32
 NORM_MIB = 24
-FORWARD_MIB = 46
-BACKWARD_MIB = 46
+FORWARD_MIB = 42
+BACKWARD_MIB = 38
 VMEM = pl.BlockSpec(memory_space=pltpu.VMEM)
 SMEM = pl.BlockSpec(memory_space=pltpu.SMEM)
 HBM = pl.BlockSpec(memory_space=pltpu.HBM)
@@ -569,36 +569,34 @@
 
 
 class HandOut:
-    def __init__(self, own, total, send, keep, row, sems, last):
+    def __init__(self, own, total, send, keep, row, sems, last, cut=None):
         self.own, self.total, self.send, self.keep = own, total, send, keep
-        self.rows = pl.ds(row, total.shape[1])
-        self.sems, self.last = sems, last
-
-    def each(self, quarter, act):
+        self.row, self.sems, self.last = row, sems, last
+        rows = total.shape[1]
+        self.parts = [(0, rows)] if cut is None else [(0, cut), (cut, rows - cut)]
+
+    def each(self, quarter, part, act):
         apart = quarter ^ self.own
+        first, count = self.parts[part]
+        source = self.total.at[quarter, pl.ds(first, count)]
+        rows = pl.ds(self.row + first, count)
+        sem = self.sems.at[quarter, part]
 
         @pl.when(self.last & (apart >= 2))
         def _():
-            act(
-                pltpu.make_async_copy(
-                    self.total.at[quarter], self.send.at[3 - apart, self.rows], self.sems.at[quarter]
-                )
-            )
+            act(pltpu.make_async_copy(source, self.send.at[3 - apart, rows], sem))
 
         @pl.when(self.last & (apart < 2))
         def _():
-            act(
-                pltpu.make_async_copy(
-                    self.total.at[quarter], self.keep.at[1 - apart, self.rows], self.sems.at[quarter]
-                )
-            )
-
-    def start(self, quarter):
-        self.each(quarter, lambda copy: copy.start())
+            act(pltpu.make_async_copy(source, self.keep.at[1 - apart, rows], sem))
+
+    def start(self, quarter, part=0):
+        self.each(quarter, part, lambda copy: copy.start())
 
     def wait(self):
         for quarter in range(4):
-            self.each(quarter, lambda copy: copy.wait())
+            for part in range(len(self.parts)):
+                self.each(quarter, part, lambda copy: copy.wait())
 
 
 def forward_kernel(
@@ -663,8 +661,8 @@
     units = wu_h.shape[1]
     base_row, length = info_ref[0] + tile * rows, info_ref[1]
     last = tile == pl.num_programs(0) - 1
-    out_a = HandOut(place_ref[0], acc_a, send_a, keep_a, 0, sems_a, last)
-    out_b = HandOut(place_ref[1], acc_b, send_b, keep_b, 0, sems_b, last)
+    out_a = HandOut(place_ref[0], acc_a, send_a, keep_a, 0, sems_a, last, width)
+    out_b = HandOut(place_ref[1], acc_b, send_b, keep_b, 0, sems_b, last, width)
 
     @pl.when(first)
     def _():
@@ -733,9 +731,22 @@
 
     grad_out = cot_ref[...] * live
     do_pair = split(grad_out)
+    for q in range(0, 4, 2):
+        c = slice(q * QUARTER, (q + 2) * QUARTER)
+        down = mm3((a_h[:, c], a_l[:, c]), do_pair, TN)
+        for i in range(2):
+            c = slice(i * QUARTER, (i + 1) * QUARTER)
+            add_to(acc_b, q + i, 0, packed_rows(down[c]), first)
+            out_b.start(q + i)
     for c in columns(units):
         put(du_h, du_l, (EVERY, c), mm3(do_pair, (wd_h[c, :], wd_l[c, :]), NT) * usil[:, c])
     grad_f = mm3((du_h[...], du_l[...]), (wu_h[...], wu_l[...]), NT)
+    for q in range(0, 4, 2):
+        c = slice(q * QUARTER, (q + 2) * QUARTER)
+        up = mm3(f_pair, (du_h[:, c], du_l[:, c]), TN)
+        for i in range(2):
+            add_to(acc_a, q + i, 0, [up[:, i * QUARTER : (i + 1) * QUARTER]], first)
+            out_a.start(q + i)
     gain_grad_ref[...] += jnp.sum(grad_f * centered, 0, keepdims=True)
     scaled = grad_f * gain_ref[...]
     grad_gated = grad_out + scale * (
@@ -752,18 +763,14 @@
         direct_ref[g] = direct[:, g * LANES : (g + 1) * LANES]
     for q in range(0, 4, 2):
         c = slice(q * QUARTER, (q + 2) * QUARTER)
-        up = mm3(f_pair, (du_h[:, c], du_l[:, c]), TN)
         rest = mm3(m_pair, u_pair if q == 0 else h_pair, TN)
-        down = mm3((a_h[:, c], a_l[:, c]), do_pair, TN)
         hid = mm3((gr_h[:, c], gr_l[:, c]), h_pair, TN)
         for i in range(2):
             c = slice(i * QUARTER, (i + 1) * QUARTER)
-            at = add_to(acc_a, q + i, 0, [up[:, c]], first)
-            add_to(acc_a, q + i, at, [rest[:, c]], first)
-            at = add_to(acc_b, q + i, 0, packed_rows(down[c]), first)
-            add_to(acc_b, q + i, at, packed_rows(hid[c]), first)
-            out_a.start(q + i)
-            out_b.start(q + i)
+            add_to(acc_a, q + i, width, [rest[:, c]], first)
+            add_to(acc_b, q + i, width, packed_rows(hid[c]), first)
+            out_a.start(q + i, 1)
+            out_b.start(q + i, 1)
     out_a.wait()
     out_b.wait()
 
@@ -981,7 +988,7 @@
             pltpu.VMEM((TILE, units), BF16),
         ]
         + [pltpu.VMEM((4, height, QUARTER), F32) for height in heights]
-        + [pltpu.SemaphoreType.DMA((4,))] * 2,
+        + [pltpu.SemaphoreType.DMA((4, 2))] * 2,
         compiler_params=params(FORWARD_MIB),
         cost_estimate=pl.CostEstimate(flops=6 * macs, bytes_accessed=48 << 20, transcendentals=0),
         name="forward",
@@ -1027,7 +1034,7 @@
         + [pltpu.VMEM((TILE, values), BF16)] * 2
         + [pltpu.VMEM((4, height, QUARTER), F32) for height in heights]
         + [pltpu.VMEM(w.shape, BF16) for w in fetched]
-        + [pltpu.SemaphoreType.DMA((4,))] * 2
+        + [pltpu.SemaphoreType.DMA((4, 1))] * 2
         + [pltpu.SemaphoreType.DMA((len(fetched),))],
         compiler_params=params(BACKWARD_MIB),
         cost_estimate=pl.CostEstimate(

time: 311 us -> 323 us (1.039)
  waiting for transfers between devices: 53.8 us -> 62 us
  local copies, waits for them, and re-layouts: 38.3 us -> 43.8 us
    ppermute x43, waiting for transfers between devices: 48.9 us -> 58 us  [swap(): return lax.ppermute(value, axis, [(i, i ^ distance) for i in range(size)])]
    unnamed x126 -> x142, local copies, waits for them, and re-layouts: 37.5 us -> 43 us
  transfers between devices with their start and end apart: 45 -> 45, of which waited for: 16 -> 15; matrix products, arithmetic and copies ran while one was open for 1% -> 1% of each run, Pallas kernels for 27% -> 27%
where the time goes in v3:
time: 323 us; the launch traced here: 322 us
  Pallas kernels  155 us (48%)
  waiting for transfers between devices  62 us (19%)
  starting transfers between devices  46.7 us (14%)
  local copies, waits for them, and re-layouts  43.8 us (14%)
  blocking collectives  10.9 us (3%)
    pallas_call x43, Pallas kernels, ordered_call(): return lambda *args: run(*args, *tokens)  81.5 us
    ppermute x43, waiting for transfers between devices, swap(): return lax.ppermute(value, axis, [(i, i ^ distance) for i in range(size)])  58 us
    pallas_call x1, Pallas kernels, forward_call(): pl.pallas_call(forward_kernel, grid=(rows // TILE,), in_specs=[SMEM, SMEM...  56.5 us
    unnamed x142, local copies, waits for them, and re-layouts  43 us
    ppermute x43, starting transfers between devices, swap(): return lax.ppermute(value, axis, [(i, i ^ distance) for i in range(size)])  38.8 us
  transfers between devices with their start and end apart: 45, of which 15 were waited for; matrix products, arithmetic and copies ran while one was open for 1% of the time, Pallas kernels for 27%

profile of v3, /device:TPU:0, one launch (start us, length us, event | category | flops | bytes accessed | tf_op | source)
XLA Modules:
  0.0 321.5 jit_solution(6455623882053717210)
XLA Ops:
  0.7 4.4 %all-to-all-start = ((f32[4,1024,128]{2,1,0:T(8,128)}), f32[4,1024,128]{2,1,0:T(8,128)S(1)}, u32[]{:S(2)}, u32[]{:S(2)}) async-start(f32[4,1024,128]{2,1,0:T(8,128)} %bitcast.140), calls=%async_computation | async-start | bytes 4194304 | tf_op jit(solution)/shard_map/all_to_all | solution.py:1391
  11.2 1.6 copy-done.19
  12.8 5.8 %split_weights.1 = (bf16[512,1024]{1,0:T(8,128)(2,1)S(1)}, bf16[512,1024]{1,0:T(8,128)(2,1)S(1)}, bf16[512,2176]{1,0:T(8,128)(2,1)S(1)}, bf16[512,2176]{1,0:T(8,...) custom-call(f32[512,1024]{1,0:T(8,128)S(1)} %copy-done.16, ...), custom_call_target="tpu_custom_call" | custom-call | flops 12845056 | bytes 25690112 | tf_op jit(solution)/shard_map/split_weights/pallas_call | solution.py:101
  32.1 1.6 copy-done.10
  33.7 3.9 %norm.1 = (f32[4,1024,128]{2,1,0:T(8,128)S(1)}, f32[4,128,128]{2,1,0:T(8,128)S(1)}, f32[4,16,128]{2,1,0:T(8,128)S(1)}) custom-call(f32[4,1024,128]{2,1,0:T(8,128)S(1)} %copy-done.10, f32[4,1,128]{2,1,0:T(1,128)S(1)} %bitcast.134, f32[4,16,128]{2,1,0:T(8,128)S(1)} %bitcast.103, f32[4,16,128]{2,1,0:T(8,128)S(1)} %get-tuple-element.335.chunk_keep_ref.refs_2_.refs_9_), custom_call_target="tpu_custom_call" | custom-call | tf_op jit(solution)/shard_map/norm/pallas_call | solution.py:1413
  37.6 5.4 %all-gather = f32[16,16,128]{2,1,0:T(8,128)S(1)} all-gather(f32[4,16,128]{2,1,0:T(8,128)S(1)} %get-tuple-element.175), channel_id=2, replica_groups=mesh['seq'=8,'ch'=4] {'ch'}, dimensions={0}, use_global_device_ids=true | all-gather | bytes 163840 | tf_op jit(solution)/shard_map/all_gather | solution.py:1421
  43.0 5.6 %mix.1 = (f32[4,1024,128]{2,1,0:T(8,128)S(1)}, f32[4,128,128]{2,1,0:T(8,128)S(1)}) custom-call(s32[1]{0:T(128)} %bitcast.6.place_ref.refs_0_, f32[4,1024,128]{2,1,0:T(8,128)S(1)} %get-tuple-element.173.normed_ref.refs_1_.refs_5_, f32[4,128,128]{2,1,0:T(8,128)S(1)} %get-tuple-element.174.ends_ref, f32[4,4,16,128]{3,2,1,0:T(8,128)S(1)} %bitcast.120, ...), custom_call_target="tpu_custom_call" | custom-call | tf_op jit(solution)/shard_map/mix/pallas_call | solution.py:1422
  54.9 56.5 %forward.1 = (f32[1024,512]{1,0:T(8,128)}, f32[4,1024,128]{2,1,0:T(8,128)}, bf16[1024,1024]{1,0:T(8,128)(2,1)}, bf16[1024,1024]{1,0:T(8,128)(2,1)}, f32[1024,102...) custom-call(s32[2]{0:T(128)S(1)} %get-tuple-element.338.info_ref, ...), custom_call_target="tpu_custom_call" | custom-call | flops 32614907904 | bytes 50331648 | tf_op jit(solution)/shard_map/forward/pallas_call | solution.py:937
  112.0 3.8 %collective-permute-done.1.refs_2_ = f32[2,1024,256]{2,1,0:T(8,128)S(1)} collective-permute-done((f32[2,1024,256]{2,1,0:T(8,128)}, f32[2,1024,256]{2,1,0:T(8,128)S(1)}, u32[]{:S(2)}, u32[]{:S(2)}) %collective-permute-start.1) | collective-permute-done | bytes 2097184 | tf_op jit(solution)/shard_map/ppermute | solution.py:1052
  115.8 1.6 copy-done.23
  117.7 2.5 collective-permute-start.3
  120.4 1.6 collective-permute-start.2
  122.4 32.5 %backward.1 = (f32[4,1024,128]{2,1,0:T(8,128)S(1)}, f32[4,1024,128]{2,1,0:T(8,128)S(1)}, f32[8,128]{1,0:T(8,128)S(1)}, f32[4,1,128]{2,1,0:T(1,128)S(1)}, f32[2,1...) custom-call(s32[2]{0:T(128)S(1)} %pad_add_fusion.2.refs_0_, f32[4,1024,128]{2,1,0:T(8,128)S(1)} %copy-done.1, ...), custom_call_target="tpu_custom_call" | custom-call | flops 26575110144 | bytes 41943040 | tf_op jit(solution)/shard_map/backward/pallas_call | solution.py:48
  161.3 2.8 back_ends.1
  164.1 5.4 %all-gather.1 = f32[16,16,128]{2,1,0:T(8,128)S(1)} all-gather(f32[4,16,128]{2,1,0:T(8,128)S(1)} %get-tuple-element.217), channel_id=3, replica_groups=mesh['seq'=8,'ch'=4] {'ch'}, dimensions={0}, use_global_device_ids=true | all-gather | bytes 163840 | tf_op jit(solution)/shard_map/all_gather | solution.py:1504
  173.9 1.9 halve.21
  176.5 1.6 copy-done.13
  178.1 1.6 copy-done.15
  181.8 1.8 halve.23
  185.0 4.0 %back.4 = (f32[1,1024,128]{2,1,0:T(8,128)S(1)}, f32[1,16,128]{2,1,0:T(8,128)S(1)}, f32[1,16,128]{2,1,0:T(8,128)S(1)}) custom-call(s32[1]{0:T(128)} %bitcast.6.place_ref.refs_0_, f32[4,1024,128]{2,1,0:T(8,128)S(1)} %copy-done.3, f32[4,128,128]{2,1,0:T(8,128)S(1)} %get-tuple-element.216.refs_2_, f32[4,4,16,128]{3,2,1,0:T(8,128)S(1)} %bitcast.99, ...), custom_call_target="tpu_custom_call" | custom-call | flops 20971520 | bytes 1572864 | tf_op jit(solution)/shard_map/back/pallas_call | solution.py:48
  189.9 3.8 %back.5 = (f32[1,1024,128]{2,1,0:T(8,128)S(1)}, f32[1,16,128]{2,1,0:T(8,128)S(1)}, f32[1,16,128]{2,1,0:T(8,128)S(1)}) custom-call(s32[1]{0:T(128)} %bitcast.6.place_ref.refs_0_, f32[4,1024,128]{2,1,0:T(8,128)S(1)} %copy-done.3, f32[4,128,128]{2,1,0:T(8,128)S(1)} %get-tuple-element.216.refs_2_, f32[4,4,16,128]{3,2,1,0:T(8,128)S(1)} %bitcast.100, ...), custom_call_target="tpu_custom_call" | custom-call | flops 20971520 | bytes 1572864 | tf_op jit(solution)/shard_map/back/pallas_call | solution.py:48
  193.7 2.0 halve.24
  201.5 2.7 collective-permute-start.12
  206.5 1.6 copy-done.4
  208.1 1.6 copy-done.8
  209.7 3.8 %back.6 = (f32[1,1024,128]{2,1,0:T(8,128)S(1)}, f32[1,16,128]{2,1,0:T(8,128)S(1)}, f32[1,16,128]{2,1,0:T(8,128)S(1)}) custom-call(s32[1]{0:T(128)} %bitcast.6.place_ref.refs_0_, f32[4,1024,128]{2,1,0:T(8,128)S(1)} %copy-done.4, f32[4,128,128]{2,1,0:T(8,128)S(1)} %get-tuple-element.216.refs_2_, f32[4,4,16,128]{3,2,1,0:T(8,128)S(1)} %bitcast.101, ...), custom_call_target="tpu_custom_call" | custom-call | flops 20971520 | bytes 1572864 | tf_op jit(solution)/shard_map/back/pallas_call | solution.py:48
  216.8 2.7 collective-permute-start.19
  219.9 3.8 %back.7 = (f32[1,1024,128]{2,1,0:T(8,128)S(1)}, f32[1,16,128]{2,1,0:T(8,128)S(1)}, f32[1,16,128]{2,1,0:T(8,128)S(1)}) custom-call(s32[1]{0:T(128)} %bitcast.6.place_ref.refs_0_, f32[4,1024,128]{2,1,0:T(8,128)S(1)} %copy-done.5, f32[4,128,128]{2,1,0:T(8,128)S(1)} %get-tuple-element.216.refs_2_, f32[4,4,16,128]{3,2,1,0:T(8,128)S(1)} %bitcast.102, ...), custom_call_target="tpu_custom_call" | custom-call | flops 20971520 | bytes 1572864 | tf_op jit(solution)/shard_map/back/pallas_call | solution.py:48
  223.8 2.1 unnorm.1
  229.4 1.7 collective-permute-start.17
  231.1 3.7 %collective-permute-done.17.refs_1_ = f32[72,256]{1,0:T(8,128)S(1)} collective-permute-done((f32[72,256]{1,0:T(8,128)S(1)}, f32[72,256]{1,0:T(8,128)S(1)}, u32[]{:S(2)}, u32[]{:S(2)}) %collective-permute-start.17) | collective-permute-done | bytes 73760 | tf_op jit(solution)/shard_map/ppermute | solution.py:1052
  235.4 1.7 collective-permute-start.20
  238.5 7.6 %collective-permute-done.21.refs_1_ = f32[64,256]{1,0:T(8,128)S(1)} collective-permute-done((f32[64,256]{1,0:T(8,128)S(1)}, f32[64,256]{1,0:T(8,128)S(1)}, u32[]{:S(2)}, u32[]{:S(2)}) %collective-permute-start.21) | collective-permute-done | bytes 65568 | tf_op jit(solution)/shard_map/ppermute | solution.py:1052
  247.7 1.7 collective-permute-start.27
  249.4 5.2 %collective-permute-done.25.refs_1_ = f32[64,256]{1,0:T(8,128)S(1)} collective-permute-done((f32[64,256]{1,0:T(8,128)S(1)}, f32[64,256]{1,0:T(8,128)S(1)}, u32[]{:S(2)}, u32[]{:S(2)}) %collective-permute-start.25) | collective-permute-done | bytes 65568 | tf_op jit(solution)/shard_map/ppermute | solution.py:1052
  254.8 2.1 collective-permute-start.26
  256.9 4.3 %collective-permute-done.29.refs_2_ = f32[128,256]{1,0:T(8,128)S(1)} collective-permute-done((f32[128,256]{1,0:T(8,128)S(1)}, f32[128,256]{1,0:T(8,128)S(1)}, u32[]{:S(2)}, u32[]{:S(2)}) %collective-permute-start.29) | collective-permute-done | bytes 131104 | tf_op jit(solution)/shard_map/ppermute | solution.py:1052
  262.6 3.4 %collective-permute-done.27.refs_3_ = f32[512,256]{1,0:T(8,128)S(1)} collective-permute-done((f32[512,256]{1,0:T(8,128)S(1)}, f32[512,256]{1,0:T(8,128)S(1)}, u32[]{:S(2)}, u32[]{:S(2)}) %collective-permute-start.27) | collective-permute-done | bytes 524320 | tf_op jit(solution)/shard_map/ppermute | solution.py:1052
  267.1 2.8 collective-permute-done.33.refs_3_
  272.5 2.0 collective-permute-start.30
  274.5 11.4 %collective-permute-done.34.refs_7_ = f32[512,256]{1,0:T(8,128)} collective-permute-done((f32[512,256]{1,0:T(8,128)}, f32[512,256]{1,0:T(8,128)}, u32[]{:S(2)}, u32[]{:S(2)}) %collective-permute-start.34) | collective-permute-done | bytes 524320 | tf_op jit(solution)/shard_map/ppermute | solution.py:1052
  285.9 3.6 %all-to-all-start.1 = ((f32[4,1024,128]{2,1,0:T(8,128)}), f32[4,1024,128]{2,1,0:T(8,128)S(1)}, u32[]{:S(2)}, u32[]{:S(2)}) async-start(f32[4,1024,128]{2,1,0:T(8,128)} %copy-done.22), calls=%async_computation.1 | async-start | bytes 4194304 | tf_op jit(solution)/shard_map/all_to_all | solution.py:1530
  289.5 10.7 %collective-permute-done.30.refs_3_.part_b = f32[656,256]{1,0:T(8,128)S(1)} collective-permute-done((f32[656,256]{1,0:T(8,128)S(1)}, f32[656,256]{1,0:T(8,128)S(1)}, u32[]{:S(2)}, u32[]{:S(2)}) %collective-permute-start.30) | collective-permute-done | bytes 671776 | tf_op jit(solution)/shard_map/ppermute | solution.py:1052
  301.4 1.8 collective-permute-done.32.refs_5_.part_d
  304.2 1.8 small_grads.1
  307.0 6.5 %finish_one.1 = (f32[512,1024]{1,0:T(8,128)}, f32[1024,512]{1,0:T(8,128)}, f32[1024,512]{1,0:T(8,128)}, f32[512,2176]{1,0:T(8,128)}, f32[8,128]{1,0:T(8,128)S(1)}) custom-call(s32[4]{0:T(128)S(1)} %add_add_fusion.1.refs_0_.refs_1_, s32[4]{0:T(128)S(1)} %add_add_fusion.refs_1_.refs_0_, f32[1024,256]{1,0:T(8,128)} %get-tuple-element.310.refs_2_, ...), custom_call_target="tpu_custom_call" | custom-call | bytes 1024 | tf_op jit(solution)/shard_map/finish_one/pallas_call | solution.py:48
  313.5 3.9 %finish_rest.1 = (f32[512,1024]{1,0:T(8,128)}, f32[512,2176]{1,0:T(8,128)}, f32[8,128]{1,0:T(8,128)S(1)}) custom-call(s32[4]{0:T(128)S(1)} %add_add_fusion.refs_1_.refs_0_, s32[4]{0:T(128)S(1)} %add_add_fusion.1.refs_0_.refs_1_, f32[656,256]{1,0:T(8,128)S(1)} %get-tuple-element.306.refs_2_.part_a, ...), custom_call_target="tpu_custom_call", output_to_operand_aliasing={{1}: (10, {})} | custom-call | bytes 1024 | tf_op jit(solution)/shard_map/finish_rest/pallas_call | solution.py:48
  317.4 2.6 all-to-all-done.1.refs_0_
  (245 shorter events, 70.9 us)
Async XLA Ops:
  0.7 30.1 %all-to-all-start = ((f32[4,1024,128]{2,1,0:T(8,128)}), f32[4,1024,128]{2,1,0:T(8,128)S(1)}, u32[]{:S(2)}, u32[]{:S(2)}) async-start(f32[4,1024,128]{2,1,0:T(8,128)} %bitcast.140), calls=%async_computation | async-start | bytes 4194304 | tf_op jit(solution)/shard_map/all_to_all | solution.py:1391
  12.8 19.3 %copy-start.38 = (f32[512]{0:T(512)S(1)}, f32[512]{0:T(512)}, u32[]{:S(2)}) copy-start(f32[512]{0:T(512)} %param.20) | copy-start | bytes 6148
  111.4 4.4 %collective-permute-start.1 = (f32[2,1024,256]{2,1,0:T(8,128)}, f32[2,1024,256]{2,1,0:T(8,128)S(1)}, u32[]{:S(2)}, u32[]{:S(2)}) collective-permute-start(f32[2,1024,256]{2,1,0:T(8,128)} %get-tuple-element.202), channel_id=1, source_target_pairs={{0,1},{1,0},{2,3},{3,2},{4,5},{5,4},{6,7},{7,6},{8,9},{9,8},{10,11... | collective-permute-start | bytes 6291464 | tf_op jit(solution)/shard_map/ppermute | solution.py:1052
  111.7 8.4 %collective-permute-start = (f32[2,1024,256]{2,1,0:T(8,128)}, f32[2,1024,256]{2,1,0:T(8,128)S(1)}, u32[]{:S(2)}, u32[]{:S(2)}) collective-permute-start(f32[2,1024,256]{2,1,0:T(8,128)} %get-tuple-element.200), channel_id=1, source_target_pairs={{0,1},{1,0},{2,3},{3,2},{4,5},{5,4},{6,7},{7,6},{8,9},{9,8},{10,11... | collective-permute-start | bytes 6291464 | tf_op jit(solution)/shard_map/ppermute | solution.py:1052
  117.7 37.3 %collective-permute-start.3 = (f32[1024,256]{1,0:T(8,128)S(1)}, f32[1024,256]{1,0:T(8,128)S(1)}, u32[]{:S(2)}, u32[]{:S(2)}) collective-permute-start(f32[1024,256]{1,0:T(8,128)S(1)} %get-tuple-element.211), channel_id=1, source_target_pairs={{0,4},{4,0},{8,12},{12,8},{16,20},{20,16},{24,28},{28,24},{1,5},{5... | collective-permute-start | bytes 3145736 | tf_op jit(solution)/shard_map/ppermute | solution.py:1052
  120.4 36.4 %collective-permute-start.2 = (f32[1024,256]{1,0:T(8,128)S(1)}, f32[1024,256]{1,0:T(8,128)S(1)}, u32[]{:S(2)}, u32[]{:S(2)}) collective-permute-start(f32[1024,256]{1,0:T(8,128)S(1)} %get-tuple-element.209), channel_id=1, source_target_pairs={{0,8},{4,12},{8,0},{12,4},{16,24},{20,28},{24,16},{28,20},{1,9},{5... | collective-permute-start | bytes 3145736 | tf_op jit(solution)/shard_map/ppermute | solution.py:1052
  158.2 11.3 %collective-permute-start.5 = (f32[2,1088,256]{2,1,0:T(8,128)S(1)}, f32[2,1088,256]{2,1,0:T(8,128)S(1)}, u32[]{:S(2)}, u32[]{:S(2)}) collective-permute-start(f32[2,1088,256]{2,1,0:T(8,128)S(1)} %copy-done.70), channel_id=1, source_target_pairs={{0,1},{1,0},{2,3},{3,2},{4,5},{5,4},{6,7},{7,6},{8,9},{9,8},{10,11... | collective-permute-start | bytes 6684680 | tf_op jit(solution)/shard_map/ppermute | solution.py:1052
  158.2 14.7 %collective-permute-start.6 = (f32[512,256]{1,0:T(8,128)}, f32[512,256]{1,0:T(8,128)}, u32[]{:S(2)}, u32[]{:S(2)}) collective-permute-start(f32[512,256]{1,0:T(8,128)} %get-tuple-element.225), channel_id=1, source_target_pairs={{0,8},{4,12},{8,0},{12,4},{16,24},{20,28},{24,16},{28,20},{1,9},{5... | collective-permute-start | bytes 1572872 | tf_op jit(solution)/shard_map/ppermute | solution.py:1052
  159.8 22.0 %collective-permute-start.4 = (f32[512,256]{1,0:T(8,128)}, f32[512,256]{1,0:T(8,128)}, u32[]{:S(2)}, u32[]{:S(2)}) collective-permute-start(f32[512,256]{1,0:T(8,128)} %get-tuple-element.221), channel_id=1, source_target_pairs={{0,4},{4,0},{8,12},{12,8},{16,20},{20,16},{24,28},{28,24},{1,5},{5... | collective-permute-start | bytes 1572872 | tf_op jit(solution)/shard_map/ppermute | solution.py:1052
  171.1 22.6 %collective-permute-start.10 = (f32[576,256]{1,0:T(8,128)}, f32[576,256]{1,0:T(8,128)}, u32[]{:S(2)}, u32[]{:S(2)}) collective-permute-start(f32[576,256]{1,0:T(8,128)} %get-tuple-element.240), channel_id=1, source_target_pairs={{0,8},{4,12},{8,0},{12,4},{16,24},{20,28},{24,16},{28,20},{1,9},{5... | collective-permute-start | bytes 1769480 | tf_op jit(solution)/shard_map/ppermute | solution.py:1052
  179.8 17.4 %collective-permute-start.9 = (f32[512,256]{1,0:T(8,128)S(1)}, f32[512,256]{1,0:T(8,128)S(1)}, u32[]{:S(2)}, u32[]{:S(2)}) collective-permute-start(f32[512,256]{1,0:T(8,128)S(1)} %get-tuple-element.238), channel_id=1, source_target_pairs={{0,4},{4,0},{8,12},{12,8},{16,20},{20,16},{24,28},{28,24},{1,5},{5... | collective-permute-start | bytes 1572872 | tf_op jit(solution)/shard_map/ppermute | solution.py:1052
  181.1 18.4 %collective-permute-start.8 = (f32[256,256]{1,0:T(8,128)}, f32[256,256]{1,0:T(8,128)}, u32[]{:S(2)}, u32[]{:S(2)}) collective-permute-start(f32[256,256]{1,0:T(8,128)} %get-tuple-element.236), channel_id=1, source_target_pairs={{0,2},{1,3},{2,0},{3,1},{4,6},{5,7},{6,4},{7,5},{8,10},{9,11},{10,... | collective-permute-start | bytes 786440 | tf_op jit(solution)/shard_map/ppermute | solution.py:1052
  183.6 20.6 %collective-permute-start.7 = (f32[256,256]{1,0:T(8,128)}, f32[256,256]{1,0:T(8,128)}, u32[]{:S(2)}, u32[]{:S(2)}) collective-permute-start(f32[256,256]{1,0:T(8,128)} %get-tuple-element.234), channel_id=1, source_target_pairs={{0,2},{1,3},{2,0},{3,1},{4,6},{5,7},{6,4},{7,5},{8,10},{9,11},{10,... | collective-permute-start | bytes 786440 | tf_op jit(solution)/shard_map/ppermute | solution.py:1052
  196.5 17.1 %collective-permute-start.14 = (f32[288,256]{1,0:T(8,128)}, f32[288,256]{1,0:T(8,128)S(1)}, u32[]{:S(2)}, u32[]{:S(2)}) collective-permute-start(f32[288,256]{1,0:T(8,128)} %get-tuple-element.254), channel_id=1, source_target_pairs={{0,4},{4,0},{8,12},{12,8},{16,20},{20,16},{24,28},{28,24},{1,5},{5... | collective-permute-start | bytes 884744 | tf_op jit(solution)/shard_map/ppermute | solution.py:1052
  198.0 16.3 %collective-permute-start.13 = (f32[256,256]{1,0:T(8,128)}, f32[256,256]{1,0:T(8,128)}, u32[]{:S(2)}, u32[]{:S(2)}) collective-permute-start(f32[256,256]{1,0:T(8,128)} %get-tuple-element.252), channel_id=1, source_target_pairs={{0,8},{4,12},{8,0},{12,4},{16,24},{20,28},{24,16},{28,20},{1,9},{5... | collective-permute-start | bytes 786440 | tf_op jit(solution)/shard_map/ppermute | solution.py:1052
  201.5 15.2 %collective-permute-start.12 = (f32[128,256]{1,0:T(8,128)S(1)}, f32[128,256]{1,0:T(8,128)S(1)}, u32[]{:S(2)}, u32[]{:S(2)}) collective-permute-start(f32[128,256]{1,0:T(8,128)S(1)} %get-tuple-element.250), channel_id=1, source_target_pairs={{0,16},{4,20},{8,24},{12,28},{16,0},{20,4},{24,8},{28,12},{1,17},{... | collective-permute-start | bytes 393224 | tf_op jit(solution)/shard_map/ppermute | solution.py:1052
  206.1 13.3 %collective-permute-start.11 = (f32[128,256]{1,0:T(8,128)S(1)}, f32[128,256]{1,0:T(8,128)S(1)}, u32[]{:S(2)}, u32[]{:S(2)}) collective-permute-start(f32[128,256]{1,0:T(8,128)S(1)} %get-tuple-element.248), channel_id=1, source_target_pairs={{0,16},{4,20},{8,24},{12,28},{16,0},{20,4},{24,8},{28,12},{1,17},{... | collective-permute-start | bytes 393224 | tf_op jit(solution)/shard_map/ppermute | solution.py:1052
  213.6 10.1 %collective-permute-start.16 = (f32[144,256]{1,0:T(8,128)S(1)}, f32[144,256]{1,0:T(8,128)S(1)}, u32[]{:S(2)}, u32[]{:S(2)}) collective-permute-start(f32[144,256]{1,0:T(8,128)S(1)} %get-tuple-element.271), channel_id=1, source_target_pairs={{0,2},{1,3},{2,0},{3,1},{4,6},{5,7},{6,4},{7,5},{8,10},{9,11},{10,... | collective-permute-start | bytes 442376 | tf_op jit(solution)/shard_map/ppermute | solution.py:1052
  215.3 8.5 %collective-permute-start.15 = (f32[128,256]{1,0:T(8,128)S(1)}, f32[128,256]{1,0:T(8,128)S(1)}, u32[]{:S(2)}, u32[]{:S(2)}) collective-permute-start(f32[128,256]{1,0:T(8,128)S(1)} %get-tuple-element.269), channel_id=1, source_target_pairs={{0,2},{1,3},{2,0},{3,1},{4,6},{5,7},{6,4},{7,5},{8,10},{9,11},{10,... | collective-permute-start | bytes 393224 | tf_op jit(solution)/shard_map/ppermute | solution.py:1052
  216.8 10.5 %collective-permute-start.19 = (f32[128,256]{1,0:T(8,128)S(1)}, f32[128,256]{1,0:T(8,128)S(1)}, u32[]{:S(2)}, u32[]{:S(2)}) collective-permute-start(f32[128,256]{1,0:T(8,128)S(1)} %get-tuple-element.280.refs_0_), channel_id=1, source_target_pairs={{0,16},{4,20},{8,24},{12,28},{16,0},{20,4},{24,8},{28,12},{1,17},{... | collective-permute-start | bytes 393224 | tf_op jit(solution)/shard_map/ppermute | solution.py:1052
  219.5 9.3 %collective-permute-start.18 = (f32[128,256]{1,0:T(8,128)S(1)}, f32[128,256]{1,0:T(8,128)S(1)}, u32[]{:S(2)}, u32[]{:S(2)}) collective-permute-start(f32[128,256]{1,0:T(8,128)S(1)} %get-tuple-element.279.refs_0_), channel_id=1, source_target_pairs={{0,16},{4,20},{8,24},{12,28},{16,0},{20,4},{24,8},{28,12},{1,17},{... | collective-permute-start | bytes 393224 | tf_op jit(solution)/shard_map/ppermute | solution.py:1052
  227.3 11.1 %collective-permute-start.23 = (f32[256,256]{1,0:T(8,128)S(1)}, f32[256,256]{1,0:T(8,128)S(1)}, u32[]{:S(2)}, u32[]{:S(2)}) collective-permute-start(f32[256,256]{1,0:T(8,128)S(1)} %get-tuple-element.289), channel_id=1, source_target_pairs={{0,8},{4,12},{8,0},{12,4},{16,24},{20,28},{24,16},{28,20},{1,9},{5... | collective-permute-start | bytes 786440 | tf_op jit(solution)/shard_map/ppermute | solution.py:1052
  228.8 9.7 %collective-permute-start.22 = (f32[256,256]{1,0:T(8,128)S(1)}, f32[256,256]{1,0:T(8,128)S(1)}, u32[]{:S(2)}, u32[]{:S(2)}) collective-permute-start(f32[256,256]{1,0:T(8,128)S(1)} %get-tuple-element.288), channel_id=1, source_target_pairs={{0,2},{1,3},{2,0},{3,1},{4,6},{5,7},{6,4},{7,5},{8,10},{9,11},{10,... | collective-permute-start | bytes 786440 | tf_op jit(solution)/shard_map/ppermute | solution.py:1052
  229.4 5.4 %collective-permute-start.17 = (f32[72,256]{1,0:T(8,128)S(1)}, f32[72,256]{1,0:T(8,128)S(1)}, u32[]{:S(2)}, u32[]{:S(2)}) collective-permute-start(f32[72,256]{1,0:T(8,128)S(1)} %get-tuple-element.278), channel_id=1, source_target_pairs={{0,16},{4,20},{8,24},{12,28},{16,0},{20,4},{24,8},{28,12},{1,17},{... | collective-permute-start | bytes 221192 | tf_op jit(solution)/shard_map/ppermute | solution.py:1052
  235.4 10.7 %collective-permute-start.20 = (f32[152,256]{1,0:T(8,128)S(1)}, f32[152,256]{1,0:T(8,128)S(1)}, u32[]{:S(2)}, u32[]{:S(2)}) collective-permute-start(f32[152,256]{1,0:T(8,128)S(1)} %get-tuple-element.285.refs_2_), channel_id=1, source_target_pairs={{0,16},{4,20},{8,24},{12,28},{16,0},{20,4},{24,8},{28,12},{1,17},{... | collective-permute-start | bytes 466952 | tf_op jit(solution)/shard_map/ppermute | solution.py:1052
  237.1 8.9 %collective-permute-start.21 = (f32[64,256]{1,0:T(8,128)S(1)}, f32[64,256]{1,0:T(8,128)S(1)}, u32[]{:S(2)}, u32[]{:S(2)}) collective-permute-start(f32[64,256]{1,0:T(8,128)S(1)} %get-tuple-element.287), channel_id=1, source_target_pairs={{0,16},{4,20},{8,24},{12,28},{16,0},{20,4},{24,8},{28,12},{1,17},{... | collective-permute-start | bytes 196616 | tf_op jit(solution)/shard_map/ppermute | solution.py:1052
  246.1 8.6 %collective-permute-start.24 = (f32[224,256]{1,0:T(8,128)S(1)}, f32[224,256]{1,0:T(8,128)S(1)}, u32[]{:S(2)}, u32[]{:S(2)}) collective-permute-start(f32[224,256]{1,0:T(8,128)S(1)} %get-tuple-element.294.refs_3_), channel_id=1, source_target_pairs={{0,4},{4,0},{8,12},{12,8},{16,20},{20,16},{24,28},{28,24},{1,5},{5... | collective-permute-start | bytes 688136 | tf_op jit(solution)/shard_map/ppermute | solution.py:1052
  247.7 13.8 %collective-permute-start.28 = (f32[512,256]{1,0:T(8,128)S(1)}, f32[512,256]{1,0:T(8,128)S(1)}, u32[]{:S(2)}, u32[]{:S(2)}) collective-permute-start(f32[512,256]{1,0:T(8,128)S(1)} %get-tuple-element.300), channel_id=1, source_target_pairs={{0,2},{1,3},{2,0},{3,1},{4,6},{5,7},{6,4},{7,5},{8,10},{9,11},{10,... | collective-permute-start | bytes 1572872 | tf_op jit(solution)/shard_map/ppermute | solution.py:1052
  247.7 18.3 %collective-permute-start.27 = (f32[512,256]{1,0:T(8,128)S(1)}, f32[512,256]{1,0:T(8,128)S(1)}, u32[]{:S(2)}, u32[]{:S(2)}) collective-permute-start(f32[512,256]{1,0:T(8,128)S(1)} %get-tuple-element.299), channel_id=1, source_target_pairs={{0,4},{4,0},{8,12},{12,8},{16,20},{20,16},{24,28},{28,24},{1,5},{5... | collective-permute-start | bytes 1572872 | tf_op jit(solution)/shard_map/ppermute | solution.py:1052
  249.4 5.2 %collective-permute-start.25 = (f32[64,256]{1,0:T(8,128)S(1)}, f32[64,256]{1,0:T(8,128)S(1)}, u32[]{:S(2)}, u32[]{:S(2)}) collective-permute-start(f32[64,256]{1,0:T(8,128)S(1)} %get-tuple-element.295.refs_0_), channel_id=1, source_target_pairs={{0,16},{4,20},{8,24},{12,28},{16,0},{20,4},{24,8},{28,12},{1,17},{... | collective-permute-start | bytes 196616 | tf_op jit(solution)/shard_map/ppermute | solution.py:1052
  254.7 6.5 %collective-permute-start.29 = (f32[128,256]{1,0:T(8,128)S(1)}, f32[128,256]{1,0:T(8,128)S(1)}, u32[]{:S(2)}, u32[]{:S(2)}) collective-permute-start(f32[128,256]{1,0:T(8,128)S(1)} %get-tuple-element.301), channel_id=1, source_target_pairs={{0,8},{4,12},{8,0},{12,4},{16,24},{20,28},{24,16},{28,20},{1,9},{5... | collective-permute-start | bytes 393224 | tf_op jit(solution)/shard_map/ppermute | solution.py:1052
  254.8 12.2 %collective-permute-start.26 = (f32[368,256]{1,0:T(8,128)S(1)}, f32[368,256]{1,0:T(8,128)S(1)}, u32[]{:S(2)}, u32[]{:S(2)}) collective-permute-start(f32[368,256]{1,0:T(8,128)S(1)} %get-tuple-element.298.refs_4_), channel_id=1, source_target_pairs={{0,8},{4,12},{8,0},{12,4},{16,24},{20,28},{24,16},{28,20},{1,9},{5... | collective-permute-start | bytes 1130504 | tf_op jit(solution)/shard_map/ppermute | solution.py:1052
  261.2 8.7 %collective-permute-start.33 = (f32[256,256]{1,0:T(8,128)S(1)}, f32[256,256]{1,0:T(8,128)S(1)}, u32[]{:S(2)}, u32[]{:S(2)}) collective-permute-start(f32[256,256]{1,0:T(8,128)S(1)} %get-tuple-element.307), channel_id=1, source_target_pairs={{0,4},{4,0},{8,12},{12,8},{16,20},{20,16},{24,28},{28,24},{1,5},{5... | collective-permute-start | bytes 786440 | tf_op jit(solution)/shard_map/ppermute | solution.py:1052
  270.7 15.2 %collective-permute-start.34 = (f32[512,256]{1,0:T(8,128)}, f32[512,256]{1,0:T(8,128)}, u32[]{:S(2)}, u32[]{:S(2)}) collective-permute-start(f32[512,256]{1,0:T(8,128)} %get-tuple-element.309.refs_6_), channel_id=1, source_target_pairs={{0,2},{1,3},{2,0},{3,1},{4,6},{5,7},{6,4},{7,5},{8,10},{9,11},{10,... | collective-permute-start | bytes 1572872 | tf_op jit(solution)/shard_map/ppermute | solution.py:1052
  271.5 29.2 %collective-permute-start.40 = (f32[1024,256]{1,0:T(8,128)}, f32[1024,256]{1,0:T(8,128)}, u32[]{:S(2)}, u32[]{:S(2)}) collective-permute-start(f32[1024,256]{1,0:T(8,128)} %get-tuple-element.311.refs_6_), channel_id=1, source_target_pairs={{0,8},{4,12},{8,0},{12,4},{16,24},{20,28},{24,16},{28,20},{1,9},{5... | collective-permute-start | bytes 3145736 | tf_op jit(solution)/shard_map/ppermute | solution.py:1052
  271.5 29.3 %collective-permute-start.37 = (f32[1024,256]{1,0:T(8,128)}, f32[1024,256]{1,0:T(8,128)}, u32[]{:S(2)}, u32[]{:S(2)}) collective-permute-start(f32[1024,256]{1,0:T(8,128)} %get-tuple-element.310.refs_2_), channel_id=1, source_target_pairs={{0,4},{4,0},{8,12},{12,8},{16,20},{20,16},{24,28},{28,24},{1,5},{5... | collective-permute-start | bytes 3145736 | tf_op jit(solution)/shard_map/ppermute | solution.py:1052
  272.5 30.9 %copy-start.66 = (f32[512,16]{0,1:T(8,128)S(1)}, f32[512,16]{0,1:T(8,128)}, u32[]{:S(2)}) copy-start(f32[512,16]{0,1:T(8,128)} %param.23) | copy-start | bytes 98308
  272.5 30.9 %copy-start.67 = (f32[2,4,8,128]{3,2,1,0:T(8,128)S(1)}, f32[2,4,8,128]{3,2,1,0:T(8,128)}, u32[]{:S(2)}) copy-start(f32[2,4,8,128]{3,2,1,0:T(8,128)} %get-tuple-element.330) | copy-start | bytes 98308
  272.5 27.7 %collective-permute-start.30 = (f32[656,256]{1,0:T(8,128)S(1)}, f32[656,256]{1,0:T(8,128)S(1)}, u32[]{:S(2)}, u32[]{:S(2)}) collective-permute-start(f32[656,256]{1,0:T(8,128)S(1)} %get-tuple-element.306.refs_2_.part_a), channel_id=1, source_target_pairs={{0,2},{1,3},{2,0},{3,1},{4,6},{5,7},{6,4},{7,5},{8,10},{9,11},{10,... | collective-permute-start | bytes 2015240 | tf_op jit(solution)/shard_map/ppermute | solution.py:1052
  274.5 25.7 %collective-permute-start.31 = (f32[656,256]{1,0:T(8,128)S(1)}, f32[656,256]{1,0:T(8,128)}, u32[]{:S(2)}, u32[]{:S(2)}) collective-permute-start(f32[656,256]{1,0:T(8,128)S(1)} %get-tuple-element.306.refs_2_.part_a), channel_id=1, source_target_pairs={{0,1},{1,0},{2,3},{3,2},{4,5},{5,4},{6,7},{7,6},{8,9},{9,8},{10,11... | collective-permute-start | bytes 2015240 | tf_op jit(solution)/shard_map/ppermute | solution.py:1052
  285.9 15.4 %collective-permute-start.41 = (f32[1024,256]{1,0:T(8,128)}, f32[1024,256]{1,0:T(8,128)}, u32[]{:S(2)}, u32[]{:S(2)}) collective-permute-start(f32[1024,256]{1,0:T(8,128)} %get-tuple-element.311.refs_6_), channel_id=1, source_target_pairs={{0,1},{1,0},{2,3},{3,2},{4,5},{5,4},{6,7},{7,6},{8,9},{9,8},{10,11... | collective-permute-start | bytes 3145736 | tf_op jit(solution)/shard_map/ppermute | solution.py:1052
  285.9 34.1 %all-to-all-start.1 = ((f32[4,1024,128]{2,1,0:T(8,128)}), f32[4,1024,128]{2,1,0:T(8,128)S(1)}, u32[]{:S(2)}, u32[]{:S(2)}) async-start(f32[4,1024,128]{2,1,0:T(8,128)} %copy-done.22), calls=%async_computation.1 | async-start | bytes 4194304 | tf_op jit(solution)/shard_map/all_to_all | solution.py:1530
  300.2 3.0 collective-permute-start.32
  300.2 5.8 %collective-permute-start.38 = (f32[1024,256]{1,0:T(8,128)}, f32[1024,256]{1,0:T(8,128)S(1)}, u32[]{:S(2)}, u32[]{:S(2)}) collective-permute-start(f32[1024,256]{1,0:T(8,128)} %get-tuple-element.310.refs_2_), channel_id=1, source_target_pairs={{0,1},{1,0},{2,3},{3,2},{4,5},{5,4},{6,7},{7,6},{8,9},{9,8},{10,11... | collective-permute-start | bytes 3145736 | tf_op jit(solution)/shard_map/ppermute | solution.py:1052
  300.7 5.3 %collective-permute-start.42 = (f32[1024,256]{1,0:T(8,128)}, f32[1024,256]{1,0:T(8,128)S(1)}, u32[]{:S(2)}, u32[]{:S(2)}) collective-permute-start(f32[1024,256]{1,0:T(8,128)} %collective-permute-done.40.refs_7_), channel_id=1, source_target_pairs={{0,1},{1,0},{2,3},{3,2},{4,5},{5,4},{6,7},{7,6},{8,9},{9,8},{10,11... | collective-permute-start | bytes 3145736 | tf_op jit(solution)/shard_map/ppermute | solution.py:1052
  300.8 6.2 %collective-permute-start.39 = (f32[1024,256]{1,0:T(8,128)}, f32[1024,256]{1,0:T(8,128)S(1)}, u32[]{:S(2)}, u32[]{:S(2)}) collective-permute-start(f32[1024,256]{1,0:T(8,128)} %collective-permute-done.37.refs_3_), channel_id=1, source_target_pairs={{0,1},{1,0},{2,3},{3,2},{4,5},{5,4},{6,7},{7,6},{8,9},{9,8},{10,11... | collective-permute-start | bytes 3145736 | tf_op jit(solution)/shard_map/ppermute | solution.py:1052
  301.3 12.2 %collective-permute-start.35 = (f32[512,256]{1,0:T(8,128)}, f32[512,256]{1,0:T(8,128)S(1)}, u32[]{:S(2)}, u32[]{:S(2)}) collective-permute-start(f32[512,256]{1,0:T(8,128)} %get-tuple-element.309.refs_6_), channel_id=1, source_target_pairs={{0,1},{1,0},{2,3},{3,2},{4,5},{5,4},{6,7},{7,6},{8,9},{9,8},{10,11... | collective-permute-start | bytes 1572872 | tf_op jit(solution)/shard_map/ppermute | solution.py:1052
  303.2 10.3 %collective-permute-start.36 = (f32[512,256]{1,0:T(8,128)}, f32[512,256]{1,0:T(8,128)S(1)}, u32[]{:S(2)}, u32[]{:S(2)}) collective-permute-start(f32[512,256]{1,0:T(8,128)} %collective-permute-done.34.refs_7_), channel_id=1, source_target_pairs={{0,1},{1,0},{2,3},{3,2},{4,5},{5,4},{6,7},{7,6},{8,9},{9,8},{10,11... | collective-permute-start | bytes 1572872 | tf_op jit(solution)/shard_map/ppermute | solution.py:1052
  (68 other events, 320.4 us)
